TPU v7x, 32 devices: a whole 2x2x4 slice. The times are simulated.
32 devices in a mesh: view: 4 (over y, core), row: 4 (over z), col: 2 (over x).
Axes of the slice: x: 2, y: 2, z: 4, core: 2. Of those that a mesh axis runs over, the one named last changes fastest.
Arguments:
- volume: bfloat16 [64, 1024, 1024], P('view', 'row', 'col'), may hold values from -5 to 5
- tf_color: float32 [3, 16], replicated, may hold values from 0 to 1
- tf_opacity: float32 [16], replicated, may hold values from 0.2 to 4
Outputs:
- picture: float32 [4, 4, 256, 1024], P(None, 'view', 'row', 'col')
All inputs are finite; a program needn't handle non-finite values.
Results may differ from a plain program's by a relative error of at most 0.00095.
Values may be sent and summed in bfloat16 or wider, within the bound.
No kernel may reach another device: no remote copies, remote signals or barrier semaphores. Data moves between devices by JAX's collectives and lax.ppermute only.
A program may use at most 64 MiB of HBM per device.

v0:
```python
import jax
import jax.numpy as jnp
from jax import lax
from jax.sharding import PartitionSpec as P

LIGHT_Z = 0.48
LIGHT_Y = 0.6
LIGHT_X = 0.64
VALUE_LOW = -3.0
VALUE_HIGH = 3.0


def extended(cells, sides, width):
    for axis, dim in sides:
        count = lax.axis_size(axis)
        ends = count - 1
        head = lax.slice_in_dim(cells, 0, width, axis=dim)
        tail = lax.slice_in_dim(cells, cells.shape[dim] - width, cells.shape[dim], axis=dim)
        cells = jnp.concatenate(
            [
                lax.ppermute(tail, axis, [(i, (i + 1) % count) for i in range(ends)]),
                cells,
                lax.ppermute(head, axis, [((i + 1) % count, i) for i in range(ends)]),
            ],
            axis=dim,
        )
    return cells


def from_partner(value, axis, stride):
    mask = 2**stride
    pairs = [(source, source ^ mask) for source in range(lax.axis_size(axis))]
    return lax.ppermute(value, axis, pairs)


def classify(three_slices, tf_color, tf_opacity, depth_total):
    centre = three_slices[1, 1:-1, 1:-1]
    grad_z = (three_slices[2, 1:-1, 1:-1] - three_slices[0, 1:-1, 1:-1]) * 0.5
    grad_y = (three_slices[1, 2:, 1:-1] - three_slices[1, :-2, 1:-1]) * 0.5
    grad_x = (three_slices[1, 1:-1, 2:] - three_slices[1, 1:-1, :-2]) * 0.5
    grad_sq = grad_z * grad_z + grad_y * grad_y + grad_x * grad_x
    shading = 0.35 + 0.65 * jnp.abs(
        LIGHT_Z * grad_z + LIGHT_Y * grad_y + LIGHT_X * grad_x
    ) / jnp.sqrt(grad_sq + 1.0)
    knot_count = tf_color.shape[1]
    scaled = jnp.clip(
        (centre - VALUE_LOW) * ((knot_count - 1) / (VALUE_HIGH - VALUE_LOW)), 0.0, knot_count - 1.0
    )
    places = jnp.arange(knot_count, dtype=jnp.float32).reshape(knot_count, 1)
    weights = jnp.maximum(0.0, 1.0 - jnp.abs(scaled.reshape(1, -1) - places))
    colour = jnp.dot(tf_color, weights, precision=lax.Precision.HIGHEST).reshape(
        (3,) + centre.shape
    )
    extinction = jnp.dot(
        tf_opacity.reshape(1, knot_count), weights, precision=lax.Precision.HIGHEST
    ).reshape(centre.shape)
    opacity_cell = 1.0 - jnp.exp(
        -2.0 * extinction * (0.2 + grad_sq / (grad_sq + 1.0)) / depth_total
    )
    return (colour * shading * opacity_cell, opacity_cell)


def composite_over(nearer, farther):
    return nearer + (1.0 - nearer[3:4]) * farther


def on_device(volume, tf_color, tf_opacity):
    view_count = lax.axis_size("view")
    slice_count, height, tile_width = volume.shape
    depth_total = slice_count * view_count
    padded = extended(volume, (("view", 0), ("row", 1), ("col", 2)), 1)

    def advance(slice_index, running):
        colour_sum, through = running
        three_slices = lax.dynamic_slice_in_dim(padded, slice_index, 3, 0).astype(jnp.float32)
        emission, opacity_cell = classify(three_slices, tf_color, tf_opacity, depth_total)
        return (colour_sum + through * emission, through * (1.0 - opacity_cell))

    initial = (
        jnp.zeros((3, height, tile_width), jnp.float32),
        jnp.ones((height, tile_width), jnp.float32),
    )
    colour_sum, through = lax.fori_loop(0, slice_count, advance, initial)
    partial_image = jnp.concatenate([colour_sum, (1.0 - through)[None]], axis=0)
    tile_rows = height // view_count
    depth_bits = view_count.bit_length() - 1
    row_blocks = partial_image.reshape((4,) + (2,) * depth_bits + (tile_rows, tile_width))
    position = lax.axis_index("view")
    for bit_level in range(depth_bits):
        side_bit = position // 2**bit_level % 2
        bit_axis = depth_bits - bit_level
        kept_half = lax.dynamic_index_in_dim(row_blocks, side_bit, bit_axis, keepdims=False)
        sent_half = lax.dynamic_index_in_dim(row_blocks, 1 - side_bit, bit_axis, keepdims=False)
        partner_half = from_partner(sent_half, "view", bit_level)
        nearer = jnp.where(side_bit == 0, kept_half, partner_half)
        farther = jnp.where(side_bit == 0, partner_half, kept_half)
        row_blocks = composite_over(nearer, farther)
    return row_blocks.reshape(4, 1, tile_rows, tile_width)


def solution(mesh):
    placed = (P("view", "row", "col"), P(), P())
    return jax.shard_map(
        on_device,
        mesh=mesh,
        in_specs=placed,
        out_specs=P(None, "view", "row", "col"),
        check_vma=False,
    )
```

profile of v0, /device:TPU:12, one launch (start us, length us, event | category | flops | bytes accessed | tf_op | source)
XLA Modules:
  0.0 399.5 jit_solution(2429002785775430665)
XLA Ops:
  46.6 16.9 %pad_maximum_fusion = bf16[18,258,514]{2,0,1:T(8,128)(2,1)S(1)} fusion(bf16[18,258,1]{2,0,1:T(8,128)(2,1)S(1)} %copy.28, bf16[18,1,512]{2,0,1:T(8,128)(2,1)S(1)} %collective-permute-done.3, bf16[1,256,512]{2,0,1:T(2,128)(2,1)} %copy-done.4, bf16[16,256,512]{2,0,1:T(8,128)(2,1)} %copy-done, bf16[1,256,512]{2,0,1:T(2,128)(2,1)} %copy-done.3, ...), kind=kLoop, calls=%fused_computation.47 | loop fusion | flops 33418224 | bytes 9548064 | tf_op jit(solution)/shard_map/concatenate | solution.py:19
  66.9 311.5 %while.18 = (s32[]{:T(128)}, f32[3,256,512]{2,1,0:T(8,128)}, f32[256,512]{1,0:T(8,128)}, bf16[18,258,514]{2,1,0:T(8,128)(2,1)}, f32[3,16]{1,0:T(4,128)S(1)}, /*index=5*/f32[16]{0:T(128)S(1)}, s32[]{:T(128)}, s32[]{:T(128)}) while((s32[]{:T(128)}, f32[3,256,512]{2,1,0:T(8,128)}, f32[256,512]{1,0:T(8,128)}, ...), condition=%wide.region_1.2_spmd.clone, body=%wide.region_0.1_spmd.clone.sunk | while | flops 125702672 | bytes 36466144 | solution.py:83
  69.1 6.3 %fusion.59 = f32[1,256,512]{2,0,1:T(1,128)} fusion(f32[256,512]{1,0:T(8,128)S(1)} %get-tuple-element.274, f32[16]{0:T(128)S(1)} %get-tuple-element.300), kind=kOutput, calls=%fused_computation.clone.1 | convolution fusion | flops 33554432 | bytes 1048640 | tf_op jit(solution)/shard_map/while/body/eval_jaxpr/dot_general | solution.py:54
  88.5 6.3 %fusion.59 = f32[1,256,512]{2,0,1:T(1,128)} fusion(f32[256,512]{1,0:T(8,128)S(1)} %get-tuple-element.274, f32[16]{0:T(128)S(1)} %get-tuple-element.300), kind=kOutput, calls=%fused_computation.clone.1 | convolution fusion | flops 33554432 | bytes 1048640 | tf_op jit(solution)/shard_map/while/body/eval_jaxpr/dot_general | solution.py:54
  107.9 6.3 %fusion.59 = f32[1,256,512]{2,0,1:T(1,128)} fusion(f32[256,512]{1,0:T(8,128)S(1)} %get-tuple-element.274, f32[16]{0:T(128)S(1)} %get-tuple-element.300), kind=kOutput, calls=%fused_computation.clone.1 | convolution fusion | flops 33554432 | bytes 1048640 | tf_op jit(solution)/shard_map/while/body/eval_jaxpr/dot_general | solution.py:54
  127.4 6.3 %fusion.59 = f32[1,256,512]{2,0,1:T(1,128)} fusion(f32[256,512]{1,0:T(8,128)S(1)} %get-tuple-element.274, f32[16]{0:T(128)S(1)} %get-tuple-element.300), kind=kOutput, calls=%fused_computation.clone.1 | convolution fusion | flops 33554432 | bytes 1048640 | tf_op jit(solution)/shard_map/while/body/eval_jaxpr/dot_general | solution.py:54
  136.7 5.6 %fusion.58 = f32[131072,3]{0,1:T(4,128)S(1)} fusion(f32[3,16]{1,0:T(4,128)S(1)} %get-tuple-element.299, f32[131072]{0:T(1024)S(1)} %bitcast.76), kind=kOutput, calls=%fused_computation.6.clone.1 | convolution fusion | flops 83886080 | bytes 2097344 | tf_op jit(solution)/shard_map/while/body/eval_jaxpr/dot_general | solution.py:51
  146.9 6.3 %fusion.59 = f32[1,256,512]{2,0,1:T(1,128)} fusion(f32[256,512]{1,0:T(8,128)S(1)} %get-tuple-element.274, f32[16]{0:T(128)S(1)} %get-tuple-element.300), kind=kOutput, calls=%fused_computation.clone.1 | convolution fusion | flops 33554432 | bytes 1048640 | tf_op jit(solution)/shard_map/while/body/eval_jaxpr/dot_general | solution.py:54
  156.2 5.6 %fusion.58 = f32[131072,3]{0,1:T(4,128)S(1)} fusion(f32[3,16]{1,0:T(4,128)S(1)} %get-tuple-element.299, f32[131072]{0:T(1024)S(1)} %bitcast.76), kind=kOutput, calls=%fused_computation.6.clone.1 | convolution fusion | flops 83886080 | bytes 2097344 | tf_op jit(solution)/shard_map/while/body/eval_jaxpr/dot_general | solution.py:51
  166.4 6.3 %fusion.59 = f32[1,256,512]{2,0,1:T(1,128)} fusion(f32[256,512]{1,0:T(8,128)S(1)} %get-tuple-element.274, f32[16]{0:T(128)S(1)} %get-tuple-element.300), kind=kOutput, calls=%fused_computation.clone.1 | convolution fusion | flops 33554432 | bytes 1048640 | tf_op jit(solution)/shard_map/while/body/eval_jaxpr/dot_general | solution.py:54
  185.8 6.3 %fusion.59 = f32[1,256,512]{2,0,1:T(1,128)} fusion(f32[256,512]{1,0:T(8,128)S(1)} %get-tuple-element.274, f32[16]{0:T(128)S(1)} %get-tuple-element.300), kind=kOutput, calls=%fused_computation.clone.1 | convolution fusion | flops 33554432 | bytes 1048640 | tf_op jit(solution)/shard_map/while/body/eval_jaxpr/dot_general | solution.py:54
  205.3 6.3 %fusion.59 = f32[1,256,512]{2,0,1:T(1,128)} fusion(f32[256,512]{1,0:T(8,128)S(1)} %get-tuple-element.274, f32[16]{0:T(128)S(1)} %get-tuple-element.300), kind=kOutput, calls=%fused_computation.clone.1 | convolution fusion | flops 33554432 | bytes 1048640 | tf_op jit(solution)/shard_map/while/body/eval_jaxpr/dot_general | solution.py:54
  214.7 5.6 %fusion.58 = f32[131072,3]{0,1:T(4,128)S(1)} fusion(f32[3,16]{1,0:T(4,128)S(1)} %get-tuple-element.299, f32[131072]{0:T(1024)S(1)} %bitcast.76), kind=kOutput, calls=%fused_computation.6.clone.1 | convolution fusion | flops 83886080 | bytes 2097344 | tf_op jit(solution)/shard_map/while/body/eval_jaxpr/dot_general | solution.py:51
  224.8 6.3 %fusion.59 = f32[1,256,512]{2,0,1:T(1,128)} fusion(f32[256,512]{1,0:T(8,128)S(1)} %get-tuple-element.274, f32[16]{0:T(128)S(1)} %get-tuple-element.300), kind=kOutput, calls=%fused_computation.clone.1 | convolution fusion | flops 33554432 | bytes 1048640 | tf_op jit(solution)/shard_map/while/body/eval_jaxpr/dot_general | solution.py:54
  234.1 5.6 %fusion.58 = f32[131072,3]{0,1:T(4,128)S(1)} fusion(f32[3,16]{1,0:T(4,128)S(1)} %get-tuple-element.299, f32[131072]{0:T(1024)S(1)} %bitcast.76), kind=kOutput, calls=%fused_computation.6.clone.1 | convolution fusion | flops 83886080 | bytes 2097344 | tf_op jit(solution)/shard_map/while/body/eval_jaxpr/dot_general | solution.py:51
  244.3 6.3 %fusion.59 = f32[1,256,512]{2,0,1:T(1,128)} fusion(f32[256,512]{1,0:T(8,128)S(1)} %get-tuple-element.274, f32[16]{0:T(128)S(1)} %get-tuple-element.300), kind=kOutput, calls=%fused_computation.clone.1 | convolution fusion | flops 33554432 | bytes 1048640 | tf_op jit(solution)/shard_map/while/body/eval_jaxpr/dot_general | solution.py:54
  263.8 6.3 %fusion.59 = f32[1,256,512]{2,0,1:T(1,128)} fusion(f32[256,512]{1,0:T(8,128)S(1)} %get-tuple-element.274, f32[16]{0:T(128)S(1)} %get-tuple-element.300), kind=kOutput, calls=%fused_computation.clone.1 | convolution fusion | flops 33554432 | bytes 1048640 | tf_op jit(solution)/shard_map/while/body/eval_jaxpr/dot_general | solution.py:54
  283.2 6.3 %fusion.59 = f32[1,256,512]{2,0,1:T(1,128)} fusion(f32[256,512]{1,0:T(8,128)S(1)} %get-tuple-element.274, f32[16]{0:T(128)S(1)} %get-tuple-element.300), kind=kOutput, calls=%fused_computation.clone.1 | convolution fusion | flops 33554432 | bytes 1048640 | tf_op jit(solution)/shard_map/while/body/eval_jaxpr/dot_general | solution.py:54
  302.7 6.3 %fusion.59 = f32[1,256,512]{2,0,1:T(1,128)} fusion(f32[256,512]{1,0:T(8,128)S(1)} %get-tuple-element.274, f32[16]{0:T(128)S(1)} %get-tuple-element.300), kind=kOutput, calls=%fused_computation.clone.1 | convolution fusion | flops 33554432 | bytes 1048640 | tf_op jit(solution)/shard_map/while/body/eval_jaxpr/dot_general | solution.py:54
  312.0 5.6 %fusion.58 = f32[131072,3]{0,1:T(4,128)S(1)} fusion(f32[3,16]{1,0:T(4,128)S(1)} %get-tuple-element.299, f32[131072]{0:T(1024)S(1)} %bitcast.76), kind=kOutput, calls=%fused_computation.6.clone.1 | convolution fusion | flops 83886080 | bytes 2097344 | tf_op jit(solution)/shard_map/while/body/eval_jaxpr/dot_general | solution.py:51
  322.2 6.3 %fusion.59 = f32[1,256,512]{2,0,1:T(1,128)} fusion(f32[256,512]{1,0:T(8,128)S(1)} %get-tuple-element.274, f32[16]{0:T(128)S(1)} %get-tuple-element.300), kind=kOutput, calls=%fused_computation.clone.1 | convolution fusion | flops 33554432 | bytes 1048640 | tf_op jit(solution)/shard_map/while/body/eval_jaxpr/dot_general | solution.py:54
  341.7 6.3 %fusion.59 = f32[1,256,512]{2,0,1:T(1,128)} fusion(f32[256,512]{1,0:T(8,128)S(1)} %get-tuple-element.274, f32[16]{0:T(128)S(1)} %get-tuple-element.300), kind=kOutput, calls=%fused_computation.clone.1 | convolution fusion | flops 33554432 | bytes 1048640 | tf_op jit(solution)/shard_map/while/body/eval_jaxpr/dot_general | solution.py:54
  361.1 6.3 %fusion.59 = f32[1,256,512]{2,0,1:T(1,128)} fusion(f32[256,512]{1,0:T(8,128)S(1)} %get-tuple-element.274, f32[16]{0:T(128)S(1)} %get-tuple-element.300), kind=kOutput, calls=%fused_computation.clone.1 | convolution fusion | flops 33554432 | bytes 1048640 | tf_op jit(solution)/shard_map/while/body/eval_jaxpr/dot_general | solution.py:54
  384.5 13.9 %collective-permute-done.7 = f32[4,64,512]{2,1,0:T(8,128)S(1)} collective-permute-done((f32[4,64,512]{2,1,0:T(8,128)S(1)}, f32[4,64,512]{2,1,0:T(8,128)S(1)}, u32[]{:S(2)}, u32[]{:S(2)}) %collective-permute-start.7) | collective-permute-done | bytes 524320 | tf_op jit(solution)/shard_map/ppermute | solution.py:33
  (201 shorter events, 238.5 us)
Async XLA Ops:
  4.5 22.3 %copy-start = (bf16[16,256,512]{2,0,1:T(8,128)(2,1)}, bf16[16,256,512]{2,0,1:T(8,128)(2,1)S(1)}, u32[]{:S(2)}) copy-start(bf16[16,256,512]{2,0,1:T(8,128)(2,1)S(1)} %copy.22) | copy-start | bytes 12582916
  5.4 10.5 %collective-permute-start = (bf16[1,256,512]{2,0,1:T(2,128)(2,1)S(1)}, bf16[1,256,512]{2,0,1:T(2,128)(2,1)S(1)}, u32[]{:S(2)}, u32[]{:S(2)}) collective-permute-start(bf16[1,256,512]{2,0,1:T(2,128)(2,1)S(1)} %get-tuple-element.226), channel_id=1, source_target_pairs={{0,8},{8,16},{16,24},{1,9},{9,17},{17,25},{2,10},{10,18},{18,26},{... | collective-permute-start | bytes 786440 | tf_op jit(solution)/shard_map/ppermute | solution.py:21
  7.3 10.3 %collective-permute-start.1 = (bf16[1,256,512]{2,0,1:T(2,128)(2,1)S(1)}, bf16[1,256,512]{2,0,1:T(2,128)(2,1)S(1)}, u32[]{:S(2)}, u32[]{:S(2)}) collective-permute-start(bf16[1,256,512]{2,0,1:T(2,128)(2,1)S(1)} %get-tuple-element.227), channel_id=1, source_target_pairs={{8,0},{16,8},{24,16},{9,1},{17,9},{25,17},{10,2},{18,10},{26,18},{... | collective-permute-start | bytes 786440 | tf_op jit(solution)/shard_map/ppermute | solution.py:23
  15.9 14.7 %copy-start.3 = (bf16[1,256,512]{2,0,1:T(2,128)(2,1)}, bf16[1,256,512]{2,0,1:T(2,128)(2,1)S(1)}, u32[]{:S(2)}) copy-start(bf16[1,256,512]{2,0,1:T(2,128)(2,1)S(1)} %collective-permute-done) | copy-start | bytes 786436
  17.6 12.9 %copy-start.4 = (bf16[1,256,512]{2,0,1:T(2,128)(2,1)}, bf16[1,256,512]{2,0,1:T(2,128)(2,1)S(1)}, u32[]{:S(2)}) copy-start(bf16[1,256,512]{2,0,1:T(2,128)(2,1)S(1)} %collective-permute-done.1) | copy-start | bytes 786436
  17.6 5.9 %collective-permute-start.2 = (bf16[18,1,512]{2,0,1:T(8,128)(2,1)S(1)}, bf16[18,1,512]{2,0,1:T(8,128)(2,1)S(1)}, u32[]{:S(2)}, u32[]{:S(2)}) collective-permute-start(bf16[18,1,512]{2,0,1:T(8,128)(2,1)S(1)} %get-tuple-element.224), channel_id=1, source_target_pairs={{0,2},{2,4},{4,6},{1,3},{3,5},{5,7},{8,10},{10,12},{12,14},{9,11},... | collective-permute-start | bytes 55304 | tf_op jit(solution)/shard_map/ppermute | solution.py:21
  21.1 5.7 %collective-permute-start.3 = (bf16[18,1,512]{2,0,1:T(8,128)(2,1)S(1)}, bf16[18,1,512]{2,0,1:T(8,128)(2,1)S(1)}, u32[]{:S(2)}, u32[]{:S(2)}) collective-permute-start(bf16[18,1,512]{2,0,1:T(8,128)(2,1)S(1)} %get-tuple-element.225), channel_id=1, source_target_pairs={{2,0},{4,2},{6,4},{3,1},{5,3},{7,5},{10,8},{12,10},{14,12},{11,9},... | collective-permute-start | bytes 55304 | tf_op jit(solution)/shard_map/ppermute | solution.py:23
  32.8 7.2 %collective-permute-start.4 = (bf16[18,258,1]{1,0,2:T(8,128)(2,1)S(1)}, bf16[18,258,1]{1,0,2:T(8,128)(2,1)S(1)}, u32[]{:S(2)}, u32[]{:S(2)}) collective-permute-start(bf16[18,258,1]{1,0,2:T(8,128)(2,1)S(1)} %copy.25), channel_id=1, source_target_pairs={{0,1},{2,3},{4,5},{6,7},{8,9},{10,11},{12,13},{14,15},{16,17},{18,... | collective-permute-start | bytes 27872 | tf_op jit(solution)/shard_map/ppermute | solution.py:21
  38.4 5.7 %collective-permute-start.5 = (bf16[18,258,1]{1,0,2:T(8,128)(2,1)S(1)}, bf16[18,258,1]{1,0,2:T(8,128)(2,1)S(1)}, u32[]{:S(2)}, u32[]{:S(2)}) collective-permute-start(bf16[18,258,1]{1,0,2:T(8,128)(2,1)S(1)} %copy.26), channel_id=1, source_target_pairs={{1,0},{3,2},{5,4},{7,6},{9,8},{11,10},{13,12},{15,14},{17,16},{19,... | collective-permute-start | bytes 27872 | tf_op jit(solution)/shard_map/ppermute | solution.py:23
  78.3 5.6 %copy-start.1 = (f32[3,256,512]{2,1,0:T(8,128)S(1)}, f32[3,256,512]{2,1,0:T(8,128)}, u32[]{:S(2)}) copy-start(f32[3,256,512]{2,1,0:T(8,128)} %get-tuple-element.288) | copy-start | bytes 4718596 | tf_op jit(solution)/shard_map/while
  97.8 5.6 %copy-start.1 = (f32[3,256,512]{2,1,0:T(8,128)S(1)}, f32[3,256,512]{2,1,0:T(8,128)}, u32[]{:S(2)}) copy-start(f32[3,256,512]{2,1,0:T(8,128)} %get-tuple-element.288) | copy-start | bytes 4718596 | tf_op jit(solution)/shard_map/while
  117.3 5.6 %copy-start.1 = (f32[3,256,512]{2,1,0:T(8,128)S(1)}, f32[3,256,512]{2,1,0:T(8,128)}, u32[]{:S(2)}) copy-start(f32[3,256,512]{2,1,0:T(8,128)} %get-tuple-element.288) | copy-start | bytes 4718596 | tf_op jit(solution)/shard_map/while
  136.7 5.6 %copy-start.1 = (f32[3,256,512]{2,1,0:T(8,128)S(1)}, f32[3,256,512]{2,1,0:T(8,128)}, u32[]{:S(2)}) copy-start(f32[3,256,512]{2,1,0:T(8,128)} %get-tuple-element.288) | copy-start | bytes 4718596 | tf_op jit(solution)/shard_map/while
  156.2 5.6 %copy-start.1 = (f32[3,256,512]{2,1,0:T(8,128)S(1)}, f32[3,256,512]{2,1,0:T(8,128)}, u32[]{:S(2)}) copy-start(f32[3,256,512]{2,1,0:T(8,128)} %get-tuple-element.288) | copy-start | bytes 4718596 | tf_op jit(solution)/shard_map/while
  195.2 5.6 %copy-start.1 = (f32[3,256,512]{2,1,0:T(8,128)S(1)}, f32[3,256,512]{2,1,0:T(8,128)}, u32[]{:S(2)}) copy-start(f32[3,256,512]{2,1,0:T(8,128)} %get-tuple-element.288) | copy-start | bytes 4718596 | tf_op jit(solution)/shard_map/while
  214.7 5.6 %copy-start.1 = (f32[3,256,512]{2,1,0:T(8,128)S(1)}, f32[3,256,512]{2,1,0:T(8,128)}, u32[]{:S(2)}) copy-start(f32[3,256,512]{2,1,0:T(8,128)} %get-tuple-element.288) | copy-start | bytes 4718596 | tf_op jit(solution)/shard_map/while
  234.1 5.6 %copy-start.1 = (f32[3,256,512]{2,1,0:T(8,128)S(1)}, f32[3,256,512]{2,1,0:T(8,128)}, u32[]{:S(2)}) copy-start(f32[3,256,512]{2,1,0:T(8,128)} %get-tuple-element.288) | copy-start | bytes 4718596 | tf_op jit(solution)/shard_map/while
  273.1 5.6 %copy-start.1 = (f32[3,256,512]{2,1,0:T(8,128)S(1)}, f32[3,256,512]{2,1,0:T(8,128)}, u32[]{:S(2)}) copy-start(f32[3,256,512]{2,1,0:T(8,128)} %get-tuple-element.288) | copy-start | bytes 4718596 | tf_op jit(solution)/shard_map/while
  292.6 5.6 %copy-start.1 = (f32[3,256,512]{2,1,0:T(8,128)S(1)}, f32[3,256,512]{2,1,0:T(8,128)}, u32[]{:S(2)}) copy-start(f32[3,256,512]{2,1,0:T(8,128)} %get-tuple-element.288) | copy-start | bytes 4718596 | tf_op jit(solution)/shard_map/while
  312.0 5.6 %copy-start.1 = (f32[3,256,512]{2,1,0:T(8,128)S(1)}, f32[3,256,512]{2,1,0:T(8,128)}, u32[]{:S(2)}) copy-start(f32[3,256,512]{2,1,0:T(8,128)} %get-tuple-element.288) | copy-start | bytes 4718596 | tf_op jit(solution)/shard_map/while
  351.0 5.6 %copy-start.1 = (f32[3,256,512]{2,1,0:T(8,128)S(1)}, f32[3,256,512]{2,1,0:T(8,128)}, u32[]{:S(2)}) copy-start(f32[3,256,512]{2,1,0:T(8,128)} %get-tuple-element.288) | copy-start | bytes 4718596 | tf_op jit(solution)/shard_map/while
  370.5 5.6 %copy-start.1 = (f32[3,256,512]{2,1,0:T(8,128)S(1)}, f32[3,256,512]{2,1,0:T(8,128)}, u32[]{:S(2)}) copy-start(f32[3,256,512]{2,1,0:T(8,128)} %get-tuple-element.288) | copy-start | bytes 4718596 | tf_op jit(solution)/shard_map/while
  381.1 2.7 collective-permute-start.6
  384.4 14.0 %collective-permute-start.7 = (f32[4,64,512]{2,1,0:T(8,128)S(1)}, f32[4,64,512]{2,1,0:T(8,128)S(1)}, u32[]{:S(2)}, u32[]{:S(2)}) collective-permute-start(f32[4,64,512]{2,1,0:T(8,128)S(1)} %dynamic-slice_bitcast_fusion), channel_id=1, source_target_pairs={{0,16},{8,24},{16,0},{24,8},{1,17},{9,25},{17,1},{25,9},{2,18},{10... | collective-permute-start | bytes 1572872 | tf_op jit(solution)/shard_map/ppermute | solution.py:33
  (21 other events, 42.0 us)
where the time goes:
time: 402 us; the launch traced here: 400 us
  matrix products  190 us (47%)
  other arithmetic  125 us (31%)
  local copies, waits for them, and re-layouts  38.9 us (10%)
  waiting for transfers between devices  28.1 us (7%)
  starting transfers between devices  16.4 us (4%)
    dot_general x16, matrix products, classify(): jnp.dot(tf_opacity.reshape(1, knot_count), weights, precision=lax.Precisi...  101 us
    dot_general x16, matrix products, classify(): jnp.dot(tf_color, weights, precision=lax.Precision.HIGHEST)  89.3 us
    mul x16, other arithmetic, advance(): return (colour_sum + through * emission, through * (1.0 - opacity_cell))  45.8 us
    convert_element_type x16, other arithmetic, advance(): lax.dynamic_slice_in_dim(padded, slice_index, 3, 0).astype(jnp.float32)  21.5 us
    while x80, local copies, waits for them, and re-layouts  20.5 us
    add x16, other arithmetic, advance(): return (colour_sum + through * emission, through * (1.0 - opacity_cell))  18 us
    concatenate x1, other arithmetic, extended(): jnp.concatenate([lax.ppermute(tail, axis, [(i, (i + 1) % count) for i in...  16.9 us
    ppermute x2, waiting for transfers between devices, from_partner(): return lax.ppermute(value, axis, pairs)  16.5 us
  transfers between devices with their start and end apart: 8, of which 6 were waited for; matrix products, arithmetic and copies ran while one was open for 1% of the time, Pallas kernels for 0%

commit v1 on v0

v1 whole, which is shorter than its diff:
```python
import functools

import jax
import jax.numpy as jnp
import numpy as np
from jax import lax
from jax.experimental import pallas as pl
from jax.experimental.pallas import tpu as pltpu
from jax.sharding import PartitionSpec as P

BASIS = ((12.0, 15.0, 16.0), (-20.0, 0.0, 15.0), (9.0, -20.0, 12.0))
NORM = 25.0
VALUE_LOW = -3.0
VALUE_HIGH = 3.0
AMBIENT = 0.35
DIFFUSE = 0.65
LANES = 128
PACK = 16
HALF = 8


def stencil(tile, knot_count):
    scale = (knot_count - 1) / (VALUE_HIGH - VALUE_LOW)
    width = 5 * tile + 3 * PACK
    after, before, above, centre, below, right, left, one = np.cumsum(
        [0, tile, tile, PACK, tile, PACK, tile, tile]
    )
    matrix = np.zeros((4 * tile, width), np.float32)
    for row in range(tile):
        for part, (along_z, along_y, along_x) in enumerate(BASIS):
            line = matrix[part * tile + row]
            line[after + row] += along_z / 2
            line[before + row] -= along_z / 2
            line[centre + row + 1 if row + 1 < tile else below] += along_y / 2
            line[centre + row - 1 if row > 0 else above + PACK - 1] -= along_y / 2
            line[right + row] += along_x / 2
            line[left + row] -= along_x / 2
        line = matrix[3 * tile + row]
        line[centre + row] = scale
        line[one] = -VALUE_LOW * scale
    rounded = matrix.astype(jnp.bfloat16)
    assert np.array_equal(rounded.astype(np.float32), matrix)
    return rounded


def edges_kernel(first_ref, last_ref, top_ref, bottom_ref, lo_ref, hi_ref, up_ref, down_ref):
    slices, height, lanes = first_ref.shape
    lane = lax.broadcasted_iota(jnp.int16, (height, lanes), 1)
    row = lax.broadcasted_iota(jnp.int16, up_ref.shape, 0)
    lo = hi = jnp.zeros((height, lanes), first_ref.dtype)
    up = down = jnp.zeros(up_ref.shape, up_ref.dtype)
    for z in range(slices):
        first, last = first_ref[z], last_ref[z]
        lo = jnp.where(lane == z, pltpu.roll(first, z, 1) if z else first, lo)
        hi = jnp.where(lane == z, pltpu.roll(last, z + 1, 1), hi)
        up = jnp.where(row == z, jnp.broadcast_to(top_ref[z, :1], up.shape), up)
        down = jnp.where(row == z, jnp.broadcast_to(bottom_ref[z, PACK - 1 :], up.shape), down)
    lo_ref[...] = lo
    hi_ref[...] = hi
    up_ref[...] = up
    down_ref[...] = down


def edges(volume):
    slices, height, width = volume.shape
    column = jax.ShapeDtypeStruct((height, LANES), volume.dtype)
    line = jax.ShapeDtypeStruct((slices, width), volume.dtype)
    last_lane, last_row = width // LANES - 1, height // PACK - 1
    return pl.pallas_call(
        edges_kernel,
        grid=(1,),
        out_shape=(column, column, line, line),
        in_specs=[
            pl.BlockSpec((slices, height, LANES), lambda i: (0, 0, 0)),
            pl.BlockSpec((slices, height, LANES), lambda i: (0, 0, last_lane)),
            pl.BlockSpec((slices, PACK, width), lambda i: (0, 0, 0)),
            pl.BlockSpec((slices, PACK, width), lambda i: (0, last_row, 0)),
        ],
        out_specs=(
            pl.BlockSpec((height, LANES), lambda i: (0, 0)),
            pl.BlockSpec((height, LANES), lambda i: (0, 0)),
            pl.BlockSpec((slices, width), lambda i: (0, 0)),
            pl.BlockSpec((slices, width), lambda i: (0, 0)),
        ),
        compiler_params=pltpu.CompilerParams(vmem_limit_bytes=32 * 2**20),
    )(volume, volume, volume, volume)


def from_neighbours(first, last, axis):
    count = lax.axis_size(axis)
    if count == 2:
        here = lax.axis_index(axis)
        other = lax.ppermute(jnp.where(here == 0, last, first), axis, [(0, 1), (1, 0)])
        nothing = jnp.zeros_like(other)
        return jnp.where(here == 0, nothing, other), jnp.where(here == 0, other, nothing)
    ends = range(count - 1)
    return (
        lax.ppermute(last, axis, [(i, i + 1) for i in ends]),
        lax.ppermute(first, axis, [(i + 1, i) for i in ends]),
    )


def march_kernel(
    ids_ref,
    stencil_ref,
    table_ref,
    cells_ref,
    above_ref,
    below_ref,
    before_ref,
    after_ref,
    lo_ref,
    hi_ref,
    up_ref,
    down_ref,
    out_ref,
    parts_ref,
    *,
    last_id,
    knot_count,
):
    slices, tile, width = cells_ref.shape
    place = ids_ref[pl.program_id(0)]
    lane = lax.broadcasted_iota(jnp.int16, (tile, LANES), 1)
    ones = jnp.ones((PACK, width), cells_ref.dtype)
    halves = -(-knot_count // HALF)
    rest = width - LANES

    def gradients(z):
        cells = cells_ref[z]
        above = jnp.where(
            place == 0, jnp.broadcast_to(up_ref[z : z + 1], (PACK, width)), above_ref[z]
        )
        below = jnp.where(
            place == last_id, jnp.broadcast_to(down_ref[z : z + 1], (PACK, width)), below_ref[z]
        )
        before = cells_ref[z - 1] if z > 0 else before_ref[...]
        after = cells_ref[z + 1] if z + 1 < slices else after_ref[...]
        right = pltpu.roll(cells, width - 1, 1)
        left = pltpu.roll(cells, 1, 1)
        hi = pltpu.roll(hi_ref[...], LANES - 1 - z, 1)
        lo = pltpu.roll(lo_ref[...], LANES - z, 1) if z else lo_ref[...]
        right_end = jnp.where(lane == LANES - 1, hi, right[:, rest:])
        left_end = jnp.where(lane == 0, lo, left[:, :LANES])
        if rest:
            right_end = jnp.concatenate([right[:, :rest], right_end], axis=1)
            left_end = jnp.concatenate([left_end, left[:, LANES:]], axis=1)
        stacked = jnp.concatenate(
            [after, before, above, cells, below, right_end, left_end, ones], axis=0
        )
        parts_ref[z % 2] = jnp.dot(
            stencil_ref[...], stacked, preferred_element_type=jnp.float32
        )

    def look_up(which, index, in_half):
        for half in range(halves):
            start = (which * halves + half) * HALF
            found = jnp.take_along_axis(
                table_ref[start : start + HALF], index, axis=0, mode="promise_in_bounds"
            )
            value = found if half == 0 else jnp.where(in_half[half - 1], found, value)
        return value

    def shade(z):
        slot = z % 2
        for row in range(0, tile, HALF):
            for column in range(0, width, LANES):
                here = (pl.ds(row, HALF), pl.ds(column, LANES))
                lit, second, third, knot = (
                    parts_ref[slot, pl.ds(part * tile + row, HALF), pl.ds(column, LANES)]
                    for part in range(4)
                )
                knot = jnp.minimum(jnp.maximum(knot, 0.0), knot_count - 1.0)
                segment = knot.astype(jnp.int32)
                index = segment & (HALF - 1)
                in_half = [knot >= float(HALF * half) for half in range(1, halves)]
                inverse = lax.rsqrt(
                    (lit * lit + second * second) + (third * third + NORM * NORM)
                )
                shading = jnp.abs(lit) * inverse + AMBIENT / DIFFUSE
                density = 1.2 / NORM**2 - inverse * inverse
                values = [
                    look_up(2 * c, index, in_half) + look_up(2 * c + 1, index, in_half) * knot
                    for c in range(4)
                ]
                kept = jnp.exp2(values[3] * density)
                if z == 0:
                    through = kept
                    weight = (1.0 - kept) * shading
                    for c in range(3):
                        out_ref[(c,) + here] = values[c] * weight
                else:
                    earlier = out_ref[(3,) + here]
                    through = earlier * kept
                    weight = (earlier - through) * shading
                    for c in range(3):
                        out_ref[(c,) + here] += values[c] * weight
                out_ref[(3,) + here] = through

    gradients(0)
    for z in range(slices):
        if z + 1 < slices:
            gradients(z + 1)
        shade(z)


def march(volume, halos, ids, tables, knot_count, tile):
    slices, height, width = volume.shape
    before, after, lo, hi, up, down = halos
    matrix = jnp.asarray(stencil(tile, knot_count))
    count = ids.shape[0]
    step, last = tile // PACK, height // PACK - 1
    whole = lambda shape: pl.BlockSpec(shape, lambda i, ids: (0,) * len(shape))
    grid_spec = pltpu.PrefetchScalarGridSpec(
        num_scalar_prefetch=1,
        grid=(count,),
        in_specs=[
            whole(matrix.shape),
            whole(tables.shape),
            pl.BlockSpec((slices, tile, width), lambda i, ids: (0, ids[i], 0)),
            pl.BlockSpec(
                (slices, PACK, width), lambda i, ids: (0, jnp.maximum(ids[i] * step - 1, 0), 0)
            ),
            pl.BlockSpec(
                (slices, PACK, width),
                lambda i, ids: (0, jnp.minimum((ids[i] + 1) * step, last), 0),
            ),
            pl.BlockSpec((tile, width), lambda i, ids: (ids[i], 0)),
            pl.BlockSpec((tile, width), lambda i, ids: (ids[i], 0)),
            pl.BlockSpec((tile, LANES), lambda i, ids: (ids[i], 0)),
            pl.BlockSpec((tile, LANES), lambda i, ids: (ids[i], 0)),
            whole(up.shape),
            whole(down.shape),
        ],
        out_specs=pl.BlockSpec((4, tile, width), lambda i, ids: (0, i, 0)),
        scratch_shapes=[pltpu.VMEM((2, 4 * tile, width), jnp.float32)],
    )
    return pl.pallas_call(
        functools.partial(march_kernel, last_id=height // tile - 1, knot_count=knot_count),
        grid_spec=grid_spec,
        out_shape=jax.ShapeDtypeStruct((4, count * tile, width), jnp.float32),
        compiler_params=pltpu.CompilerParams(vmem_limit_bytes=48 * 2**20),
    )(ids, matrix, tables, volume, volume, volume, before, after, lo, hi, up, down)


def make_tables(tf_color, tf_opacity, depth_total):
    knot_count = tf_color.shape[1]
    optical = -2.0 / depth_total * NORM**2 * np.log2(np.e)
    knots = jnp.concatenate([tf_color * DIFFUSE, tf_opacity[None] * np.float32(optical)], axis=0)
    slope = jnp.concatenate([knots[:, 1:] - knots[:, :-1], jnp.zeros((4, 1), knots.dtype)], axis=1)
    base = knots - slope * jnp.arange(knot_count, dtype=knots.dtype)
    lines = jnp.stack([base, slope], axis=1)
    lines = jnp.pad(lines, ((0, 0), (0, 0), (0, -knot_count % HALF)))
    return jnp.broadcast_to(lines.reshape(-1, 1), (lines.size, LANES))


def over(nearer, farther):
    through = nearer[3:]
    return jnp.concatenate([nearer[:3] + through * farther[:3], through * farther[3:]], axis=0)


def merged(own, other, side):
    nearer = jnp.where(side == 0, own, other)
    farther = jnp.where(side == 0, other, own)
    return over(nearer, farther)


def from_partner(value, axis, bit):
    pairs = [(source, source ^ (1 << bit)) for source in range(lax.axis_size(axis))]
    return lax.ppermute(value, axis, pairs)


def on_device(volume, tf_color, tf_opacity):
    view_count = lax.axis_size("view")
    position = lax.axis_index("view")
    slices, height, width = volume.shape
    knot_count = tf_color.shape[1]
    tile_rows = height // view_count
    tile = min(32, tile_rows)
    bits = view_count.bit_length() - 1
    group_bits = min(2, bits)
    groups = 1 << group_bits
    per_group = view_count // groups

    before, after = from_neighbours(volume[0], volume[-1], "view")
    lo_face, hi_face, up_face, down_face = edges(volume)
    lo, hi = from_neighbours(lo_face, hi_face, "col")
    up, down = from_neighbours(up_face, down_face, "row")
    halos = (before, after, lo, hi, up, down)
    tables = make_tables(tf_color, tf_opacity, slices * view_count)

    steps = tile_rows // tile
    pieces = {}
    earlier = None
    for distance in reversed(range(groups)):
        blocks = np.arange(per_group) * groups + (position % groups ^ distance)
        ids = (blocks[:, None] * steps + np.arange(steps)).reshape(-1).astype(jnp.int32)
        if earlier is not None:
            ids, earlier = lax.optimization_barrier((ids, earlier))
            pieces[distance + 1] = earlier
        earlier = march(volume, halos, ids, tables, knot_count, tile)
    pieces[0] = earlier

    for bit in range(group_bits):
        side = position >> bit & 1
        for distance in reversed(range(0, groups, 2 << bit)):
            sent = pieces.pop(distance + (1 << bit))
            pieces[distance] = merged(pieces[distance], from_partner(sent, "view", bit), side)
    image = pieces[0].reshape((4,) + (2,) * (bits - group_bits) + (tile_rows, width))
    for bit in range(group_bits, bits):
        side = position >> bit & 1
        axis = bits - bit
        kept = lax.dynamic_index_in_dim(image, side, axis, keepdims=False)
        sent = lax.dynamic_index_in_dim(image, 1 - side, axis, keepdims=False)
        image = merged(kept, from_partner(sent, "view", bit), side)
    image = jnp.concatenate([image[:3], 1.0 - image[3:]], axis=0)
    return image.reshape(4, 1, tile_rows, width)


def solution(mesh):
    placed = (P("view", "row", "col"), P(), P())
    return jax.shard_map(
        on_device,
        mesh=mesh,
        in_specs=placed,
        out_specs=P(None, "view", "row", "col"),
        check_vma=False,
    )
```

time: 402 us -> 67.5 us (0.17)
  matrix products: 190 us -> 0 us
  other arithmetic: 125 us -> 1.7 us
  local copies, waits for them, and re-layouts: 38.9 us -> 7.79 us
  Pallas kernels: 0 us -> 26.2 us
  waiting for transfers between devices: 28.1 us -> 18.7 us
    dot_general x32 -> x0, matrix products: 190 us -> none  [the longest x16 101 us: classify(): jnp.dot(tf_opacity.reshape(1, knot_count), weights, precision=lax.Precisi...]
    mul x34 -> x5, other arithmetic: 60.3 us -> 0.07 us  [the longest x3 0.06 us: over(): through * farther[:3]]
    pallas_call x0 -> x5, Pallas kernels: none -> 26.2 us  [the longest x4 25.5 us: march(): pl.pallas_call(functools.partial(march_kernel, last_id=height // tile - 1...]
    convert_element_type x16 -> x0, other arithmetic: 21.5 us -> none  [advance(): lax.dynamic_slice_in_dim(padded, slice_index, 3, 0).astype(jnp.float32)]
    while x80 -> x0, local copies, waits for them, and re-layouts: 20.5 us -> none
    concatenate x2, other arithmetic: 18.5 us -> 0.05 us  [the longest x1 0.04 us: over(): jnp.concatenate([nearer[:3] + through * farther[:3], through * farther[3:...]
    add x17 -> x7, other arithmetic: 18.3 us -> 0.25 us  [the longest x3 0.23 us: over(): nearer[:3] + through * farther[:3]]
    ppermute x6 -> x5, waiting for transfers between devices: 11.5 us -> 4.91 us  [the longest x2 3.82 us: from_neighbours(): lax.ppermute(last, axis, [(i, i + 1) for i in ends])]
  transfers between devices with their start and end apart: 8 -> 8, of which waited for: 6 -> 3; matrix products, arithmetic and copies ran while one was open for 1% -> 2% of each run, Pallas kernels for 0% -> 9%
where the time goes in v1:
time: 67.5 us; the launch traced here: 67.1 us
  Pallas kernels  26.2 us (39%)
  waiting for transfers between devices  18.7 us (28%)
  starting transfers between devices  12.4 us (18%)
  local copies, waits for them, and re-layouts  7.79 us (12%)
  other arithmetic  1.7 us (3%)
    pallas_call x4, Pallas kernels, march(): pl.pallas_call(functools.partial(march_kernel, last_id=height // tile - 1...  25.5 us
    ppermute x3, waiting for transfers between devices, from_partner(): return lax.ppermute(value, axis, pairs)  13.8 us
    unnamed x12, local copies, waits for them, and re-layouts  6.57 us
    ppermute x2, starting transfers between devices, from_neighbours(): lax.ppermute(last, axis, [(i, i + 1) for i in ends])  5.9 us
    ppermute x2, starting transfers between devices, from_neighbours(): lax.ppermute(first, axis, [(i + 1, i) for i in ends])  4.27 us
    ppermute x2, waiting for transfers between devices, from_neighbours(): lax.ppermute(last, axis, [(i, i + 1) for i in ends])  3.82 us
    ppermute x1, starting transfers between devices, from_neighbours(): lax.ppermute(jnp.where(here == 0, last, first), axis, [(0, 1), (1, 0)])  1.56 us
  transfers between devices with their start and end apart: 8, of which 3 were waited for; matrix products, arithmetic and copies ran while one was open for 2% of the time, Pallas kernels for 9%

profile of v1, /device:TPU:12, one launch (start us, length us, event | category | flops | bytes accessed | tf_op | source)
XLA Modules:
  0.0 67.1 jit_solution(10887122065557873663)
XLA Ops:
  0.0 2.2 %copy-done = bf16[16,256,512]{2,1,0:T(8,128)(2,1)S(1)} copy-done((bf16[16,256,512]{2,1,0:T(8,128)(2,1)S(1)}, bf16[16,256,512]{2,1,0:T(8,128)(2,1)}, u32[]{:S(2)}) %copy-start) | copy-done | bytes 4194328
  2.2 0.7 %shard_map.145 = (bf16[256,128]{1,0:T(8,128)(2,1)S(1)}, bf16[256,128]{1,0:T(8,128)(2,1)S(1)}, bf16[16,512]{1,0:T(8,128)(2,1)S(1)}, bf16[16,512]{1,0:T(8,128)(2,1)S(1)}) custom-call(bf16[16,256,512]{2,1,0:T(8,128)(2,1)S(1)} %copy-done, bf16[16,256,512]{2,1,0:T(8,128)(2,1)S(1)} %copy-done, bf16[16,256,512]{2,1,0:T(8,128)(2,1)S(1)} %copy-done, ...), custom_call_target="tpu_custom_call" | custom-call | tf_op jit(solution)/shard_map/pallas_call | solution.py:69
  2.9 3.5 %collective-permute-start.3 = (bf16[16,512]{1,0:T(8,128)(2,1)S(1)}, bf16[16,512]{1,0:T(8,128)(2,1)S(1)}, u32[]{:S(2)}, u32[]{:S(2)}) collective-permute-start(bf16[16,512]{1,0:T(8,128)(2,1)S(1)} %get-tuple-element.17), channel_id=1, source_target_pairs={{0,2},{2,4},{4,6},{1,3},{3,5},{5,7},{8,10},{10,12},{12,14},{9,11},... | collective-permute-start | bytes 49160 | tf_op jit(solution)/shard_map/ppermute | solution.py:98
  6.4 2.4 %collective-permute-start.4 = (bf16[16,512]{1,0:T(8,128)(2,1)S(1)}, bf16[16,512]{1,0:T(8,128)(2,1)S(1)}, u32[]{:S(2)}, u32[]{:S(2)}) collective-permute-start(bf16[16,512]{1,0:T(8,128)(2,1)S(1)} %get-tuple-element.18), channel_id=1, source_target_pairs={{2,0},{4,2},{6,4},{3,1},{5,3},{7,5},{10,8},{12,10},{14,12},{11,9},... | collective-permute-start | bytes 49160 | tf_op jit(solution)/shard_map/ppermute | solution.py:99
  8.8 1.6 %collective-permute-start.2 = (bf16[256,128]{1,0:T(8,128)(2,1)S(1)}, bf16[256,128]{1,0:T(8,128)(2,1)S(1)}, u32[]{:S(2)}, u32[]{:S(2)}) collective-permute-start(bf16[256,128]{1,0:T(8,128)(2,1)S(1)} %broadcast_select_fusion.6), channel_id=1, source_target_pairs={{0,1},{1,0},{2,3},{3,2},{4,5},{5,4},{6,7},{7,6},{8,9},{9,8},{10,11... | collective-permute-start | bytes 196616 | tf_op jit(solution)/shard_map/ppermute | solution.py:93
  10.3 1.1 %slice_bitcast_fusion = (bf16[256,512]{1,0:T(8,128)(2,1)S(1)}, bf16[256,512]{1,0:T(8,128)(2,1)S(1)}) fusion(bf16[16,256,512]{2,1,0:T(8,128)(2,1)} %below_ref.7), kind=kLoop, calls=%fused_computation.11 | loop fusion | bytes 1048576 | tf_op jit(solution)/shard_map/squeeze | solution.py:285
  11.4 1.9 %collective-permute-start.1 = (bf16[256,512]{1,0:T(8,128)(2,1)S(1)}, bf16[256,512]{1,0:T(8,128)(2,1)S(1)}, u32[]{:S(2)}, u32[]{:S(2)}) collective-permute-start(bf16[256,512]{1,0:T(8,128)(2,1)S(1)} %get-tuple-element.25), channel_id=1, source_target_pairs={{8,0},{16,8},{24,16},{9,1},{17,9},{25,17},{10,2},{18,10},{26,18},{... | collective-permute-start | bytes 786440 | tf_op jit(solution)/shard_map/ppermute | solution.py:99
  13.3 2.4 %collective-permute-start = (bf16[256,512]{1,0:T(8,128)(2,1)S(1)}, bf16[256,512]{1,0:T(8,128)(2,1)S(1)}, u32[]{:S(2)}, u32[]{:S(2)}) collective-permute-start(bf16[256,512]{1,0:T(8,128)(2,1)S(1)} %get-tuple-element.26), channel_id=1, source_target_pairs={{0,8},{8,16},{16,24},{1,9},{9,17},{17,25},{2,10},{10,18},{18,26},{... | collective-permute-start | bytes 786440 | tf_op jit(solution)/shard_map/ppermute | solution.py:98
  16.0 0.1 broadcast_in_dim.6
  16.1 1.1 %collective-permute-done.1.after_ref = bf16[256,512]{1,0:T(8,128)(2,1)S(1)} collective-permute-done((bf16[256,512]{1,0:T(8,128)(2,1)S(1)}, bf16[256,512]{1,0:T(8,128)(2,1)S(1)}, u32[]{:S(2)}, u32[]{:S(2)}) %collective-permute-start.1) | collective-permute-done | bytes 262176 | tf_op jit(solution)/shard_map/ppermute | solution.py:99
  17.2 3.8 %collective-permute-done.before_ref = bf16[256,512]{1,0:T(8,128)(2,1)S(1)} collective-permute-done((bf16[256,512]{1,0:T(8,128)(2,1)S(1)}, bf16[256,512]{1,0:T(8,128)(2,1)S(1)}, u32[]{:S(2)}, u32[]{:S(2)}) %collective-permute-start) | collective-permute-done | bytes 262176 | tf_op jit(solution)/shard_map/ppermute | solution.py:98
  21.1 2.2 %copy-done.1 = bf16[16,256,512]{2,1,0:T(8,128)(2,1)S(1)} copy-done((bf16[16,256,512]{2,1,0:T(8,128)(2,1)S(1)}, bf16[16,256,512]{2,1,0:T(8,128)(2,1)}, u32[]{:S(2)}) %copy-start.1) | copy-done | bytes 4194328
  23.3 6.4 %shard_map.146 = f32[4,64,512]{2,1,0:T(8,128)S(1)} custom-call(s32[2]{0:T(128)S(1)} %iota_add_fusion.2.ids_ref, bf16[128,208]{1,0:T(8,128)(2,1)S(1)} %copy-done.3, f32[128,128]{1,0:T(8,128)S(1)} %broadcast_in_dim.7.table_ref, bf16[16,256,512]{2,1,0:T(8,128)(2,1)S(1)} %copy-done.1, bf16[16,256,512]{2,1,0:T(8,128)(2,1)S(1)} %copy-done.1, ...), custom_call_target="tpu_custom_call" | custom-call | tf_op jit(solution)/shard_map/pallas_call | solution.py:238
  29.7 6.4 %shard_map.147 = f32[4,64,512]{2,1,0:T(8,128)S(1)} custom-call(s32[2]{0:T(128)S(1)} %iota_add_fusion.3.ids_ref, bf16[128,208]{1,0:T(8,128)(2,1)S(1)} %copy-done.3, f32[128,128]{1,0:T(8,128)S(1)} %broadcast_in_dim.7.table_ref, bf16[16,256,512]{2,1,0:T(8,128)(2,1)S(1)} %copy-done.1, bf16[16,256,512]{2,1,0:T(8,128)(2,1)S(1)} %copy-done.1, ...), custom_call_target="tpu_custom_call" | custom-call | tf_op jit(solution)/shard_map/pallas_call | solution.py:238
  36.0 6.4 %shard_map.148 = f32[4,64,512]{2,1,0:T(8,128)S(1)} custom-call(s32[2]{0:T(128)S(1)} %iota_add_fusion.ids_ref, bf16[128,208]{1,0:T(8,128)(2,1)S(1)} %copy-done.3, f32[128,128]{1,0:T(8,128)S(1)} %broadcast_in_dim.7.table_ref, bf16[16,256,512]{2,1,0:T(8,128)(2,1)S(1)} %copy-done.1, bf16[16,256,512]{2,1,0:T(8,128)(2,1)S(1)} %copy-done.1, ...), custom_call_target="tpu_custom_call" | custom-call | tf_op jit(solution)/shard_map/pallas_call | solution.py:238
  42.5 0.5 collective-permute-start.6
  43.0 2.2 %copy-done.2 = bf16[16,256,512]{2,1,0:T(8,128)(2,1)S(1)} copy-done((bf16[16,256,512]{2,1,0:T(8,128)(2,1)S(1)}, bf16[16,256,512]{2,1,0:T(8,128)(2,1)}, u32[]{:S(2)}) %copy-start.2) | copy-done | bytes 4194328
  45.2 6.4 %shard_map.149 = f32[4,64,512]{2,1,0:T(8,128)S(1)} custom-call(s32[2]{0:T(128)S(1)} %iota_add_fusion.1.ids_ref, bf16[128,208]{1,0:T(8,128)(2,1)S(1)} %copy-done.3, f32[128,128]{1,0:T(8,128)S(1)} %broadcast_in_dim.7.table_ref, bf16[16,256,512]{2,1,0:T(8,128)(2,1)S(1)} %copy-done.2, bf16[16,256,512]{2,1,0:T(8,128)(2,1)S(1)} %copy-done.2, ...), custom_call_target="tpu_custom_call" | custom-call | tf_op jit(solution)/shard_map/pallas_call | solution.py:238
  51.6 0.3 broadcast_select_fusion.1
  52.1 0.1 fusion.4
  52.2 13.8 %collective-permute-done.7 = f32[4,64,512]{2,1,0:T(8,128)S(1)} collective-permute-done((f32[4,64,512]{2,1,0:T(8,128)S(1)}, f32[4,64,512]{2,1,0:T(8,128)S(1)}, u32[]{:S(2)}, u32[]{:S(2)}) %collective-permute-start.7) | collective-permute-done | bytes 524320 | tf_op jit(solution)/shard_map/ppermute | solution.py:270
  66.0 0.1 fusion.1
  66.2 0.1 fusion.2
  66.2 0.8 %maximum_bitcast_fusion = f32[4,1,64,512]{3,2,1,0:T(8,128)} fusion(f32[1,64,512]{2,1,0:T(8,128)S(1)} %get-tuple-element.34, f32[3,64,512]{2,1,0:T(8,128)S(1)} %fusion.2), kind=kLoop, calls=%fused_computation.2 | loop fusion | flops 131072 | bytes 1048576 | tf_op jit(solution)/shard_map/reshape | solution.py:317
  (35 shorter events, 0.6 us)
Async XLA Ops:
  0.0 2.2 %copy-start = (bf16[16,256,512]{2,1,0:T(8,128)(2,1)S(1)}, bf16[16,256,512]{2,1,0:T(8,128)(2,1)}, u32[]{:S(2)}) copy-start(bf16[16,256,512]{2,1,0:T(8,128)(2,1)} %below_ref.7) | copy-start | bytes 12582916
  2.2 13.6 %copy-start.5 = (f32[16]{0:T(128)S(1)}, f32[16]{0:T(128)}, u32[]{:S(2)}) copy-start(f32[16]{0:T(128)} %param.17) | copy-start | bytes 196
  2.2 13.6 %copy-start.4 = (f32[3,16]{1,0:T(4,128)S(1)}, f32[3,16]{1,0:T(4,128)}, u32[]{:S(2)}) copy-start(f32[3,16]{1,0:T(4,128)} %param.16) | copy-start | bytes 580
  2.2 18.9 %copy-start.3 = (bf16[128,208]{1,0:T(8,128)(2,1)S(1)}, bf16[128,208]{1,0:T(8,128)(2,1)}, u32[]{:S(2)}) copy-start(bf16[128,208]{1,0:T(8,128)(2,1)} %constant.57.clone.stencil_ref) | copy-start | bytes 159748
  2.9 13.2 %collective-permute-start.3 = (bf16[16,512]{1,0:T(8,128)(2,1)S(1)}, bf16[16,512]{1,0:T(8,128)(2,1)S(1)}, u32[]{:S(2)}, u32[]{:S(2)}) collective-permute-start(bf16[16,512]{1,0:T(8,128)(2,1)S(1)} %get-tuple-element.17), channel_id=1, source_target_pairs={{0,2},{2,4},{4,6},{1,3},{3,5},{5,7},{8,10},{10,12},{12,14},{9,11},... | collective-permute-start | bytes 49160 | tf_op jit(solution)/shard_map/ppermute | solution.py:98
  6.4 9.7 %collective-permute-start.4 = (bf16[16,512]{1,0:T(8,128)(2,1)S(1)}, bf16[16,512]{1,0:T(8,128)(2,1)S(1)}, u32[]{:S(2)}, u32[]{:S(2)}) collective-permute-start(bf16[16,512]{1,0:T(8,128)(2,1)S(1)} %get-tuple-element.18), channel_id=1, source_target_pairs={{2,0},{4,2},{6,4},{3,1},{5,3},{7,5},{10,8},{12,10},{14,12},{11,9},... | collective-permute-start | bytes 49160 | tf_op jit(solution)/shard_map/ppermute | solution.py:99
  8.8 7.3 %collective-permute-start.2 = (bf16[256,128]{1,0:T(8,128)(2,1)S(1)}, bf16[256,128]{1,0:T(8,128)(2,1)S(1)}, u32[]{:S(2)}, u32[]{:S(2)}) collective-permute-start(bf16[256,128]{1,0:T(8,128)(2,1)S(1)} %broadcast_select_fusion.6), channel_id=1, source_target_pairs={{0,1},{1,0},{2,3},{3,2},{4,5},{5,4},{6,7},{7,6},{8,9},{9,8},{10,11... | collective-permute-start | bytes 196616 | tf_op jit(solution)/shard_map/ppermute | solution.py:93
  11.4 5.8 %collective-permute-start.1 = (bf16[256,512]{1,0:T(8,128)(2,1)S(1)}, bf16[256,512]{1,0:T(8,128)(2,1)S(1)}, u32[]{:S(2)}, u32[]{:S(2)}) collective-permute-start(bf16[256,512]{1,0:T(8,128)(2,1)S(1)} %get-tuple-element.25), channel_id=1, source_target_pairs={{8,0},{16,8},{24,16},{9,1},{17,9},{25,17},{10,2},{18,10},{26,18},{... | collective-permute-start | bytes 786440 | tf_op jit(solution)/shard_map/ppermute | solution.py:99
  13.3 7.7 %collective-permute-start = (bf16[256,512]{1,0:T(8,128)(2,1)S(1)}, bf16[256,512]{1,0:T(8,128)(2,1)S(1)}, u32[]{:S(2)}, u32[]{:S(2)}) collective-permute-start(bf16[256,512]{1,0:T(8,128)(2,1)S(1)} %get-tuple-element.26), channel_id=1, source_target_pairs={{0,8},{8,16},{16,24},{1,9},{9,17},{17,25},{2,10},{10,18},{18,26},{... | collective-permute-start | bytes 786440 | tf_op jit(solution)/shard_map/ppermute | solution.py:98
  21.1 2.2 %copy-start.1 = (bf16[16,256,512]{2,1,0:T(8,128)(2,1)S(1)}, bf16[16,256,512]{2,1,0:T(8,128)(2,1)}, u32[]{:S(2)}) copy-start(bf16[16,256,512]{2,1,0:T(8,128)(2,1)} %below_ref.7) | copy-start | bytes 12582916
  42.4 9.1 %collective-permute-start.5 = (f32[4,64,512]{2,1,0:T(8,128)S(1)}, f32[4,64,512]{2,1,0:T(8,128)S(1)}, u32[]{:S(2)}, u32[]{:S(2)}) collective-permute-start(f32[4,64,512]{2,1,0:T(8,128)S(1)} %shard_map.148), channel_id=1, source_target_pairs={{0,8},{8,0},{16,24},{24,16},{1,9},{9,1},{17,25},{25,17},{2,10},{10... | collective-permute-start | bytes 1572872 | tf_op jit(solution)/shard_map/ppermute | solution.py:270
  42.5 9.1 %collective-permute-start.6 = (f32[4,64,512]{2,1,0:T(8,128)S(1)}, f32[4,64,512]{2,1,0:T(8,128)S(1)}, u32[]{:S(2)}, u32[]{:S(2)}) collective-permute-start(f32[4,64,512]{2,1,0:T(8,128)S(1)} %shard_map.146), channel_id=1, source_target_pairs={{0,8},{8,0},{16,24},{24,16},{1,9},{9,1},{17,25},{25,17},{2,10},{10... | collective-permute-start | bytes 1572872 | tf_op jit(solution)/shard_map/ppermute | solution.py:270
  43.0 2.2 %copy-start.2 = (bf16[16,256,512]{2,1,0:T(8,128)(2,1)S(1)}, bf16[16,256,512]{2,1,0:T(8,128)(2,1)}, u32[]{:S(2)}) copy-start(bf16[16,256,512]{2,1,0:T(8,128)(2,1)} %below_ref.7) | copy-start | bytes 12582916
  52.0 14.0 %collective-permute-start.7 = (f32[4,64,512]{2,1,0:T(8,128)S(1)}, f32[4,64,512]{2,1,0:T(8,128)S(1)}, u32[]{:S(2)}, u32[]{:S(2)}) collective-permute-start(f32[4,64,512]{2,1,0:T(8,128)S(1)} %pad_maximum_fusion.1), channel_id=1, source_target_pairs={{0,16},{8,24},{16,0},{24,8},{1,17},{9,25},{17,1},{25,9},{2,18},{10... | collective-permute-start | bytes 1572872 | tf_op jit(solution)/shard_map/ppermute | solution.py:270

commit v2 on v1

v2 whole, which is shorter than its diff:
```python
import functools

import jax
import jax.numpy as jnp
import numpy as np
from jax import lax
from jax.experimental import pallas as pl
from jax.experimental.pallas import tpu as pltpu
from jax.sharding import PartitionSpec as P

BASIS = ((12.0, 15.0, 16.0), (-20.0, 0.0, 15.0), (9.0, -20.0, 12.0))
NORM = 25.0
VALUE_LOW = -3.0
VALUE_HIGH = 3.0
AMBIENT = 0.35
DIFFUSE = 0.65
LANES = 128
PACK = 16
HALF = 8
DEPTH = 2
SLOTS = 4


def stencil(tile, knot_count):
    scale = (knot_count - 1) / (VALUE_HIGH - VALUE_LOW)
    width = 5 * tile + 3 * PACK
    after, before, above, centre, below, right, left, one = np.cumsum(
        [0, tile, tile, PACK, tile, PACK, tile, tile]
    )
    matrix = np.zeros((4 * tile, width), np.float32)
    for row in range(tile):
        for part, (along_z, along_y, along_x) in enumerate(BASIS):
            line = matrix[part * tile + row]
            line[after + row] += along_z / 2
            line[before + row] -= along_z / 2
            line[centre + row + 1 if row + 1 < tile else below] += along_y / 2
            line[centre + row - 1 if row > 0 else above + PACK - 1] -= along_y / 2
            line[right + row] += along_x / 2
            line[left + row] -= along_x / 2
        line = matrix[3 * tile + row]
        line[centre + row] = scale / 2
        line[one] = -VALUE_LOW * scale / 2 - 0.5
    rounded = matrix.astype(jnp.bfloat16)
    assert np.array_equal(rounded.astype(np.float32), matrix)
    return rounded


def exchange(first, last, axis):
    count = lax.axis_size(axis)
    received = []
    for face, start in ((first, 0), (last, 1)):
        pairs = [(i, i + 1) for i in range(start, count - 1, 2)]
        if pairs:
            received.append(lax.ppermute(face, axis, pairs + [(j, i) for i, j in pairs]))
        else:
            received.append(jnp.zeros_like(face))
    return received


def edges_kernel(odd_ref, *refs):
    depth_refs, row_refs, column_refs = refs[0:2], refs[2:4], refs[4:6]
    depth_outs, row_outs, column_outs = refs[6:8], refs[8:10], refs[10:12]
    slices, height, lanes = column_refs[0].shape
    lane = lax.broadcasted_iota(jnp.int16, (height, lanes), 1)
    row = lax.broadcasted_iota(jnp.int16, row_outs[0].shape, 0)
    for turn in range(2):
        depth_outs[turn][...] = depth_refs[turn][0]
        is_first = odd_ref[1] == 1 - turn
        lines = jnp.zeros(row_outs[turn].shape, row_outs[turn].dtype)
        for z in range(slices):
            line = jnp.where(
                is_first, row_refs[turn][z, :1], row_refs[turn][z, PACK - 1 :]
            )
            lines = jnp.where(row == z, jnp.broadcast_to(line, lines.shape), lines)
        row_outs[turn][...] = lines

        def columns(turn, source, shift):
            found = jnp.zeros((height, lanes), column_outs[turn].dtype)
            for z in range(slices):
                target = (2 * z + shift) % lanes
                moved = pltpu.roll(column_refs[turn][z], (target - source) % lanes, 1)
                found = jnp.where(lane == target, moved, found)
            column_outs[turn][...] = found

        pl.when(odd_ref[2] == 1 - turn)(functools.partial(columns, turn, 0, -1))
        pl.when(odd_ref[2] == turn)(functools.partial(columns, turn, lanes - 1, 0))


def edges(volume, odd):
    slices, height, width = volume.shape
    assert 2 * slices <= LANES
    column = jax.ShapeDtypeStruct((height, LANES), volume.dtype)
    line = jax.ShapeDtypeStruct((slices, width), volume.dtype)
    face = jax.ShapeDtypeStruct((height, width), volume.dtype)

    def at(block, dim, turn):
        last = volume.shape[dim] // block[dim] - 1

        def index(i, odd):
            place = jnp.where(odd[dim] == 1 - turn, 0, last)
            return tuple(place if d == dim else 0 for d in range(3))

        return pl.BlockSpec(block, index)

    blocks = ((1, height, width), (slices, PACK, width), (slices, height, LANES))
    shapes = (face, face, line, line, column, column)
    return pl.pallas_call(
        edges_kernel,
        grid_spec=pltpu.PrefetchScalarGridSpec(
            num_scalar_prefetch=1,
            grid=(1,),
            in_specs=[at(block, dim, turn) for dim, block in enumerate(blocks) for turn in range(2)],
            out_specs=[pl.BlockSpec(shape.shape, lambda i, odd: (0, 0)) for shape in shapes],
        ),
        out_shape=shapes,
        compiler_params=pltpu.CompilerParams(vmem_limit_bytes=32 * 2**20),
    )(odd, *[volume] * 6)


def march_kernel(
    ids_ref,
    odd_ref,
    stencil_ref,
    table_ref,
    cells_ref,
    above_ref,
    below_ref,
    depth_refs,
    line_refs,
    ends_ref,
    out_ref,
    parts_ref,
    *,
    last_id,
    knot_count,
):
    slices, tile, width = cells_ref.shape
    place = ids_ref[pl.program_id(0)]
    lane = lax.broadcasted_iota(jnp.int16, (tile, LANES), 1)
    ones = jnp.ones((PACK, width), cells_ref.dtype)
    halves = -(-knot_count // (2 * HALF))
    rest = width - LANES

    def ordered(axis, pair):
        early, late = pair[0][...], pair[1][...]
        odd = odd_ref[axis] == 1
        return jnp.where(odd, early, late), jnp.where(odd, late, early)

    behind, ahead = ordered(0, depth_refs)
    up, down = ordered(1, line_refs)

    def gradients(z):
        cells = cells_ref[z]
        above = jnp.where(
            place == 0, jnp.broadcast_to(up[z : z + 1], (PACK, width)), above_ref[z]
        )
        below = jnp.where(
            place == last_id, jnp.broadcast_to(down[z : z + 1], (PACK, width)), below_ref[z]
        )
        before = cells_ref[z - 1] if z > 0 else behind
        after = cells_ref[z + 1] if z + 1 < slices else ahead
        right = pltpu.roll(cells, width - 1, 1)
        left = pltpu.roll(cells, 1, 1)
        ends = pltpu.roll(ends_ref[...], LANES - 2 * z, 1) if z else ends_ref[...]
        right_end = jnp.where(lane == LANES - 1, ends, right[:, rest:])
        left_end = jnp.where(lane == 0, ends, left[:, :LANES])
        if rest:
            right_end = jnp.concatenate([right[:, :rest], right_end], axis=1)
            left_end = jnp.concatenate([left_end, left[:, LANES:]], axis=1)
        stacked = jnp.concatenate(
            [after, before, above, cells, below, right_end, left_end, ones], axis=0
        )
        parts_ref[z % SLOTS] = jnp.dot(
            stencil_ref[...], stacked, preferred_element_type=jnp.float32
        )

    tables = [table_ref[start * HALF : start * HALF + HALF] for start in range(12 * halves)]

    def look_up(which, index, in_half):
        for half in range(halves):
            found = jnp.take_along_axis(
                tables[which * halves + half], index, axis=0, mode="promise_in_bounds"
            )
            value = found if half == 0 else jnp.where(in_half[half - 1], found, value)
        return value

    def shade(first):
        for row in range(0, tile, HALF):
            for column in range(0, width, LANES):
                here = (pl.ds(row, HALF), pl.ds(column, LANES))
                state = None if first == 0 else [out_ref[(c,) + here] for c in range(4)]
                for z in range(first, first + DEPTH):
                    state = one(z, row, column, state)
                for c in range(4):
                    out_ref[(c,) + here] = state[c]

    def one(z, row, column, state):
        slot = z % SLOTS
        lit, second, third, knot = (
            parts_ref[slot, pl.ds(part * tile + row, HALF), pl.ds(column, LANES)]
            for part in range(4)
        )
        knot = jnp.minimum(jnp.maximum(knot, -0.5), knot_count / 2 - 1.0)
        middle = jnp.round(knot)
        segment = middle.astype(jnp.int32)
        offset = knot - middle
        before_middle = offset < 0.0
        index = segment & (HALF - 1) if halves > 1 else segment
        in_half = [middle >= float(HALF * half) for half in range(1, halves)]
        inverse = lax.rsqrt((lit * lit + second * second) + (third * third + NORM * NORM))
        shading = jnp.abs(lit) * inverse + AMBIENT / DIFFUSE
        density = 1.2 / NORM**2 - inverse * inverse
        values = [
            look_up(3 * c, index, in_half)
            + offset
            * jnp.where(
                before_middle,
                look_up(3 * c + 1, index, in_half),
                look_up(3 * c + 2, index, in_half),
            )
            for c in range(4)
        ]
        kept = jnp.exp2(values[3] * density)
        if state is None:
            weight = (1.0 - kept) * shading
            return [value * weight for value in values[:3]] + [kept]
        through = state[3] * kept
        weight = (state[3] - through) * shading
        return [total + value * weight for total, value in zip(state, values[:3])] + [through]

    for z in range(DEPTH):
        gradients(z)
    for z in range(0, slices, DEPTH):
        if z + DEPTH < slices:
            for later in range(z + DEPTH, z + 2 * DEPTH):
                gradients(later)
        shade(z)


def march(volume, halos, ids, odd, tables, knot_count, tile):
    slices, height, width = volume.shape
    depth, lines, ends = halos
    matrix = jnp.asarray(stencil(tile, knot_count))
    count = ids.shape[0]
    step, last = tile // PACK, height // PACK - 1
    whole = lambda shape: pl.BlockSpec(shape, lambda i, ids, odd: (0,) * len(shape))
    grid_spec = pltpu.PrefetchScalarGridSpec(
        num_scalar_prefetch=2,
        grid=(count,),
        in_specs=[
            whole(matrix.shape),
            whole(tables.shape),
            pl.BlockSpec((slices, tile, width), lambda i, ids, odd: (0, ids[i], 0)),
            pl.BlockSpec(
                (slices, PACK, width), lambda i, ids, odd: (0, jnp.maximum(ids[i] * step - 1, 0), 0)
            ),
            pl.BlockSpec(
                (slices, PACK, width),
                lambda i, ids, odd: (0, jnp.minimum((ids[i] + 1) * step, last), 0),
            ),
            [pl.BlockSpec((tile, width), lambda i, ids, odd: (ids[i], 0))] * 2,
            [whole(lines[0].shape)] * 2,
            pl.BlockSpec((tile, LANES), lambda i, ids, odd: (ids[i], 0)),
        ],
        out_specs=pl.BlockSpec((4, tile, width), lambda i, ids, odd: (0, i, 0)),
        scratch_shapes=[pltpu.VMEM((SLOTS, 4 * tile, width), jnp.float32)],
    )
    return pl.pallas_call(
        functools.partial(march_kernel, last_id=height // tile - 1, knot_count=knot_count),
        grid_spec=grid_spec,
        out_shape=jax.ShapeDtypeStruct((4, count * tile, width), jnp.float32),
        compiler_params=pltpu.CompilerParams(vmem_limit_bytes=48 * 2**20),
    )(ids, odd, matrix, tables, volume, volume, volume, depth, lines, ends)


def make_tables(tf_color, tf_opacity, depth_total):
    knot_count = tf_color.shape[1]
    optical = -2.0 / depth_total * NORM**2 * np.log2(np.e)
    knots = jnp.concatenate([tf_color * DIFFUSE, tf_opacity[None] * np.float32(optical)], axis=0)
    segments = (knot_count + 1) // 2
    knots = jnp.pad(knots, ((0, 0), (0, 2 * segments + 1 - knot_count)), mode="edge")
    middle = knots[:, 1::2]
    slopes = [2.0 * (middle - knots[:, :-1:2]), 2.0 * (knots[:, 2::2] - middle)]
    lines = jnp.stack([middle] + slopes, axis=1)
    lines = jnp.pad(lines, ((0, 0), (0, 0), (0, -segments % HALF)))
    return jnp.broadcast_to(lines.reshape(-1, 1), (lines.size, LANES))


def over(nearer, farther):
    through = nearer[3:]
    return jnp.concatenate([nearer[:3] + through * farther[:3], through * farther[3:]], axis=0)


def merged(own, other, side):
    nearer = jnp.where(side == 0, own, other)
    farther = jnp.where(side == 0, other, own)
    return over(nearer, farther)


def from_partner(value, axis, bit):
    pairs = [(source, source ^ (1 << bit)) for source in range(lax.axis_size(axis))]
    return lax.ppermute(value, axis, pairs)


def on_device(volume, tf_color, tf_opacity):
    view_count = lax.axis_size("view")
    position = lax.axis_index("view")
    slices, height, width = volume.shape
    knot_count = tf_color.shape[1]
    tile_rows = height // view_count
    tile = min(32, tile_rows)
    bits = view_count.bit_length() - 1
    group_bits = min(2, bits)
    groups = 1 << group_bits
    per_group = view_count // groups

    volume = pltpu.with_memory_space_constraint(volume, pltpu.HBM)
    odd = jnp.stack([lax.axis_index(axis) % 2 for axis in ("view", "row", "col")])
    faces = edges(volume, odd)
    depth = exchange(*faces[0:2], "view")
    lines = exchange(*faces[2:4], "row")
    ends = exchange(*faces[4:6], "col")
    halos = (depth, lines, ends[0] + ends[1] if lax.axis_size("col") > 2 else ends[0])
    tables = make_tables(tf_color, tf_opacity, slices * view_count)

    steps = tile_rows // tile

    def march_group(distance, after):
        blocks = np.arange(per_group) * groups + (position % groups ^ distance)
        ids = (blocks[:, None] * steps + np.arange(steps)).reshape(-1).astype(jnp.int32)
        if after is not None:
            ids, after = lax.optimization_barrier((ids, after))
        return march(volume, halos, ids, odd, tables, knot_count, tile), after

    def gather_group(distance, bit, after):
        if bit == 0:
            return march_group(distance, after)
        bit -= 1
        sent, after = gather_group(distance + (1 << bit), bit, after)
        received = from_partner(sent, "view", bit)
        kept, _ = gather_group(distance, bit, sent)
        return merged(kept, received, position >> bit & 1), after

    pieces = {0: gather_group(0, group_bits, None)[0]}
    image = pieces[0].reshape((4,) + (2,) * (bits - group_bits) + (tile_rows, width))
    for bit in range(group_bits, bits):
        side = position >> bit & 1
        axis = bits - bit
        kept = lax.dynamic_index_in_dim(image, side, axis, keepdims=False)
        sent = lax.dynamic_index_in_dim(image, 1 - side, axis, keepdims=False)
        image = merged(kept, from_partner(sent, "view", bit), side)
    image = jnp.concatenate([image[:3], 1.0 - image[3:]], axis=0)
    return image.reshape(4, 1, tile_rows, width)


def solution(mesh):
    placed = (P("view", "row", "col"), P(), P())
    return jax.shard_map(
        on_device,
        mesh=mesh,
        in_specs=placed,
        out_specs=P(None, "view", "row", "col"),
        check_vma=False,
    )
```

time: 67.5 us -> 52.6 us (0.78)
  waiting for transfers between devices: 18.7 us -> 9.05 us
  local copies, waits for them, and re-layouts: 7.79 us -> 0.53 us
  Pallas kernels: 26.2 us -> 31 us
  starting transfers between devices: 12.4 us -> 9.77 us
    ppermute x3, waiting for transfers between devices: 13.8 us -> 6.91 us  [from_partner(): return lax.ppermute(value, axis, pairs)]
    unnamed x12 -> x6, local copies, waits for them, and re-layouts: 6.57 us -> 0.01 us
    pallas_call x1, Pallas kernels: 0.68 us -> 3.88 us  [edges(): pl.pallas_call(edges_kernel, grid_spec=pltpu.PrefetchScalarGridSpec(num_s...]
    ppermute x5, waiting for transfers between devices: 4.91 us -> 2.14 us  [exchange(): lax.ppermute(face, axis, pairs + [(j, i) for i, j in pairs])]
    ppermute x5, starting transfers between devices: 11.7 us -> 9.18 us  [exchange(): lax.ppermute(face, axis, pairs + [(j, i) for i, j in pairs])]
    pallas_call x4, Pallas kernels: 25.5 us -> 27.1 us  [march(): pl.pallas_call(functools.partial(march_kernel, last_id=height // tile - 1...]
    squeeze x1 -> x0, local copies, waits for them, and re-layouts: 1.06 us -> none  [on_device(): before, after = from_neighbours(volume[0], volume[-1], 'view')]
  transfers between devices with their start and end apart: 8 -> 8, of which waited for: 3 -> 2; matrix products, arithmetic and copies ran while one was open for 2% -> 1% of each run, Pallas kernels for 9% -> 26%
where the time goes in v2:
time: 52.6 us; the launch traced here: 52.3 us
  Pallas kernels  31 us (59%)
  starting transfers between devices  9.77 us (19%)
  waiting for transfers between devices  9.05 us (17%)
  other arithmetic  1.68 us (3%)
  local copies, waits for them, and re-layouts  0.53 us (1%)
    pallas_call x4, Pallas kernels, march(): pl.pallas_call(functools.partial(march_kernel, last_id=height // tile - 1...  27.1 us
    ppermute x5, starting transfers between devices, exchange(): lax.ppermute(face, axis, pairs + [(j, i) for i, j in pairs])  9.18 us
    ppermute x3, waiting for transfers between devices, from_partner(): return lax.ppermute(value, axis, pairs)  6.91 us
    pallas_call x1, Pallas kernels, edges(): pl.pallas_call(edges_kernel, grid_spec=pltpu.PrefetchScalarGridSpec(num_s...  3.88 us
    ppermute x5, waiting for transfers between devices, exchange(): lax.ppermute(face, axis, pairs + [(j, i) for i, j in pairs])  2.14 us
  transfers between devices with their start and end apart: 8, of which 2 were waited for; matrix products, arithmetic and copies ran while one was open for 1% of the time, Pallas kernels for 26%

profile of v2, /device:TPU:12, one launch (start us, length us, event | category | flops | bytes accessed | tf_op | source)
XLA Modules:
  0.0 52.3 jit_solution(11860337060347239925)
XLA Ops:
  0.0 0.1 pad_add_fusion.odd_ref
  0.1 3.9 %shard_map.145 = (bf16[256,512]{1,0:T(8,128)(2,1)S(1)}, bf16[256,512]{1,0:T(8,128)(2,1)S(1)}, bf16[16,512]{1,0:T(8,128)(2,1)S(1)}, bf16[16,512]{1,0:T(8,128)(2,1...) custom-call(s32[3]{0:T(128)S(1)} %pad_add_fusion.odd_ref, bf16[16,256,512]{2,1,0:T(8,128)(2,1)} %below_ref.7, ...), custom_call_target="tpu_custom_call" | custom-call | tf_op jit(solution)/shard_map/pallas_call | solution.py:107
  4.0 2.5 %collective-permute-start.1 = (bf16[256,512]{1,0:T(8,128)(2,1)S(1)}, bf16[256,512]{1,0:T(8,128)(2,1)S(1)}, u32[]{:S(2)}, u32[]{:S(2)}) collective-permute-start(bf16[256,512]{1,0:T(8,128)(2,1)S(1)} %get-tuple-element.14), channel_id=1, source_target_pairs={{8,16},{16,8},{9,17},{17,9},{10,18},{18,10},{11,19},{19,11},{12,20... | collective-permute-start | bytes 786440 | tf_op jit(solution)/shard_map/ppermute | solution.py:54
  6.6 5.0 %collective-permute-start.3 = (bf16[16,512]{1,0:T(8,128)(2,1)S(1)}, bf16[16,512]{1,0:T(8,128)(2,1)S(1)}, u32[]{:S(2)}, u32[]{:S(2)}) collective-permute-start(bf16[16,512]{1,0:T(8,128)(2,1)S(1)} %get-tuple-element.16), channel_id=1, source_target_pairs={{2,4},{4,2},{3,5},{5,3},{10,12},{12,10},{11,13},{13,11},{18,20},{2... | collective-permute-start | bytes 49160 | tf_op jit(solution)/shard_map/ppermute | solution.py:54
  11.6 1.6 %collective-permute-start.4 = (bf16[256,128]{1,0:T(8,128)(2,1)S(1)}, bf16[256,128]{1,0:T(8,128)(2,1)S(1)}, u32[]{:S(2)}, u32[]{:S(2)}) collective-permute-start(bf16[256,128]{1,0:T(8,128)(2,1)S(1)} %get-tuple-element.17), channel_id=1, source_target_pairs={{0,1},{1,0},{2,3},{3,2},{4,5},{5,4},{6,7},{7,6},{8,9},{9,8},{10,11... | collective-permute-start | bytes 196616 | tf_op jit(solution)/shard_map/ppermute | solution.py:54
  13.3 0.1 pad_maximum_fusion.4
  13.4 0.1 slice.50
  13.5 0.1 slice.51
  13.5 0.1 slice.52
  13.7 0.1 broadcast_in_dim.4
  13.8 2.1 %collective-permute-done.4.ends_ref = bf16[256,128]{1,0:T(8,128)(2,1)S(1)} collective-permute-done((bf16[256,128]{1,0:T(8,128)(2,1)S(1)}, bf16[256,128]{1,0:T(8,128)(2,1)S(1)}, u32[]{:S(2)}, u32[]{:S(2)}) %collective-permute-start.4) | collective-permute-done | bytes 65568 | tf_op jit(solution)/shard_map/ppermute | solution.py:54
  16.0 6.8 %shard_map.146 = f32[4,64,512]{2,1,0:T(8,128)S(1)} custom-call(s32[2]{0:T(128)S(1)} %iota_add_fusion.2.ids_ref, s32[3]{0:T(128)S(1)} %pad_add_fusion.odd_ref, bf16[128,208]{1,0:T(8,128)(2,1)S(1)} %copy-done, f32[96,128]{1,0:T(8,128)S(1)} %broadcast_in_dim.5.table_ref, bf16[16,256,512]{2,1,0:T(8,128)(2,1)} %below_ref.7, bf16[16,256,512]{2,1,0:T(8,128)(2,1)} %below_ref.7, ...), custom_call_target="tpu_custom_call" | custom-call | tf_op jit(solution)/shard_map/pallas_call | solution.py:268
  22.9 6.8 %shard_map.147 = f32[4,64,512]{2,1,0:T(8,128)S(1)} custom-call(s32[2]{0:T(128)S(1)} %iota_add_fusion.3.ids_ref, s32[3]{0:T(128)S(1)} %pad_add_fusion.odd_ref, bf16[128,208]{1,0:T(8,128)(2,1)S(1)} %copy-done, f32[96,128]{1,0:T(8,128)S(1)} %broadcast_in_dim.5.table_ref, bf16[16,256,512]{2,1,0:T(8,128)(2,1)} %below_ref.7, bf16[16,256,512]{2,1,0:T(8,128)(2,1)} %below_ref.7, ...), custom_call_target="tpu_custom_call" | custom-call | tf_op jit(solution)/shard_map/pallas_call | solution.py:268
  29.7 0.1 broadcast_select_fusion.3
  29.9 0.1 fusion.4
  30.0 6.8 %shard_map.148 = f32[4,64,512]{2,1,0:T(8,128)S(1)} custom-call(s32[2]{0:T(128)S(1)} %iota_add_fusion.ids_ref, s32[3]{0:T(128)S(1)} %pad_add_fusion.odd_ref, bf16[128,208]{1,0:T(8,128)(2,1)S(1)} %copy-done, f32[96,128]{1,0:T(8,128)S(1)} %broadcast_in_dim.5.table_ref, bf16[16,256,512]{2,1,0:T(8,128)(2,1)} %below_ref.7, bf16[16,256,512]{2,1,0:T(8,128)(2,1)} %below_ref.7, ...), custom_call_target="tpu_custom_call" | custom-call | tf_op jit(solution)/shard_map/pallas_call | solution.py:268
  36.8 0.5 collective-permute-start.6
  37.3 6.8 %shard_map.149 = f32[4,64,512]{2,1,0:T(8,128)S(1)} custom-call(s32[2]{0:T(128)S(1)} %iota_add_fusion.1.ids_ref, s32[3]{0:T(128)S(1)} %pad_add_fusion.odd_ref, bf16[128,208]{1,0:T(8,128)(2,1)S(1)} %copy-done, f32[96,128]{1,0:T(8,128)S(1)} %broadcast_in_dim.5.table_ref, bf16[16,256,512]{2,1,0:T(8,128)(2,1)} %below_ref.7, bf16[16,256,512]{2,1,0:T(8,128)(2,1)} %below_ref.7, ...), custom_call_target="tpu_custom_call" | custom-call | tf_op jit(solution)/shard_map/pallas_call | solution.py:268
  44.1 0.1 broadcast_select_fusion.1
  44.3 0.1 fusion.3
  44.3 6.9 %collective-permute-done.7 = f32[4,64,512]{2,1,0:T(8,128)S(1)} collective-permute-done((f32[4,64,512]{2,1,0:T(8,128)S(1)}, f32[4,64,512]{2,1,0:T(8,128)S(1)}, u32[]{:S(2)}, u32[]{:S(2)}) %collective-permute-start.7) | collective-permute-done | bytes 524320 | tf_op jit(solution)/shard_map/ppermute | solution.py:302
  51.2 0.1 fusion.1
  51.4 0.1 fusion.2
  51.5 0.8 %maximum_bitcast_fusion = f32[4,1,64,512]{3,2,1,0:T(8,128)} fusion(f32[1,64,512]{2,1,0:T(8,128)S(1)} %get-tuple-element.28, f32[3,64,512]{2,1,0:T(8,128)S(1)} %fusion.2), kind=kLoop, calls=%fused_computation.2 | loop fusion | flops 131072 | bytes 1048576 | tf_op jit(solution)/shard_map/reshape | solution.py:353
  (32 shorter events, 0.5 us)
Async XLA Ops:
  0.1 13.1 %copy-start.2 = (f32[16]{0:T(128)S(1)}, f32[16]{0:T(128)}, u32[]{:S(2)}) copy-start(f32[16]{0:T(128)} %param.17) | copy-start | bytes 196
  0.1 13.1 %copy-start.1 = (f32[3,16]{1,0:T(4,128)S(1)}, f32[3,16]{1,0:T(4,128)}, u32[]{:S(2)}) copy-start(f32[3,16]{1,0:T(4,128)} %param.16) | copy-start | bytes 580
  0.1 15.9 %copy-start = (bf16[128,208]{1,0:T(8,128)(2,1)S(1)}, bf16[128,208]{1,0:T(8,128)(2,1)}, u32[]{:S(2)}) copy-start(bf16[128,208]{1,0:T(8,128)(2,1)} %constant.72.clone.stencil_ref) | copy-start | bytes 159748
  4.0 12.0 %collective-permute-start = (bf16[256,512]{1,0:T(8,128)(2,1)S(1)}, bf16[256,512]{1,0:T(8,128)(2,1)S(1)}, u32[]{:S(2)}, u32[]{:S(2)}) collective-permute-start(bf16[256,512]{1,0:T(8,128)(2,1)S(1)} %get-tuple-element.13), channel_id=1, source_target_pairs={{0,8},{16,24},{8,0},{24,16},{1,9},{17,25},{9,1},{25,17},{2,10},{18... | collective-permute-start | bytes 786440 | tf_op jit(solution)/shard_map/ppermute | solution.py:54
  4.0 12.0 %collective-permute-start.1 = (bf16[256,512]{1,0:T(8,128)(2,1)S(1)}, bf16[256,512]{1,0:T(8,128)(2,1)S(1)}, u32[]{:S(2)}, u32[]{:S(2)}) collective-permute-start(bf16[256,512]{1,0:T(8,128)(2,1)S(1)} %get-tuple-element.14), channel_id=1, source_target_pairs={{8,16},{16,8},{9,17},{17,9},{10,18},{18,10},{11,19},{19,11},{12,20... | collective-permute-start | bytes 786440 | tf_op jit(solution)/shard_map/ppermute | solution.py:54
  6.5 7.3 %collective-permute-start.2 = (bf16[16,512]{1,0:T(8,128)(2,1)S(1)}, bf16[16,512]{1,0:T(8,128)(2,1)S(1)}, u32[]{:S(2)}, u32[]{:S(2)}) collective-permute-start(bf16[16,512]{1,0:T(8,128)(2,1)S(1)} %get-tuple-element.15), channel_id=1, source_target_pairs={{0,2},{4,6},{2,0},{6,4},{1,3},{5,7},{3,1},{7,5},{8,10},{12,14},{10... | collective-permute-start | bytes 49160 | tf_op jit(solution)/shard_map/ppermute | solution.py:54
  6.6 7.2 %collective-permute-start.3 = (bf16[16,512]{1,0:T(8,128)(2,1)S(1)}, bf16[16,512]{1,0:T(8,128)(2,1)S(1)}, u32[]{:S(2)}, u32[]{:S(2)}) collective-permute-start(bf16[16,512]{1,0:T(8,128)(2,1)S(1)} %get-tuple-element.16), channel_id=1, source_target_pairs={{2,4},{4,2},{3,5},{5,3},{10,12},{12,10},{11,13},{13,11},{18,20},{2... | collective-permute-start | bytes 49160 | tf_op jit(solution)/shard_map/ppermute | solution.py:54
  11.6 4.3 %collective-permute-start.4 = (bf16[256,128]{1,0:T(8,128)(2,1)S(1)}, bf16[256,128]{1,0:T(8,128)(2,1)S(1)}, u32[]{:S(2)}, u32[]{:S(2)}) collective-permute-start(bf16[256,128]{1,0:T(8,128)(2,1)S(1)} %get-tuple-element.17), channel_id=1, source_target_pairs={{0,1},{1,0},{2,3},{3,2},{4,5},{5,4},{6,7},{7,6},{8,9},{9,8},{10,11... | collective-permute-start | bytes 196616 | tf_op jit(solution)/shard_map/ppermute | solution.py:54
  22.8 6.9 %collective-permute-start.5 = (f32[4,64,512]{2,1,0:T(8,128)S(1)}, f32[4,64,512]{2,1,0:T(8,128)S(1)}, u32[]{:S(2)}, u32[]{:S(2)}) collective-permute-start(f32[4,64,512]{2,1,0:T(8,128)S(1)} %shard_map.146), channel_id=1, source_target_pairs={{0,8},{8,0},{16,24},{24,16},{1,9},{9,1},{17,25},{25,17},{2,10},{10... | collective-permute-start | bytes 1572872 | tf_op jit(solution)/shard_map/ppermute | solution.py:302
  36.8 7.3 %collective-permute-start.6 = (f32[4,64,512]{2,1,0:T(8,128)S(1)}, f32[4,64,512]{2,1,0:T(8,128)S(1)}, u32[]{:S(2)}, u32[]{:S(2)}) collective-permute-start(f32[4,64,512]{2,1,0:T(8,128)S(1)} %shard_map.148), channel_id=1, source_target_pairs={{0,8},{8,0},{16,24},{24,16},{1,9},{9,1},{17,25},{25,17},{2,10},{10... | collective-permute-start | bytes 1572872 | tf_op jit(solution)/shard_map/ppermute | solution.py:302
  37.3 13.9 %collective-permute-start.7 = (f32[4,64,512]{2,1,0:T(8,128)S(1)}, f32[4,64,512]{2,1,0:T(8,128)S(1)}, u32[]{:S(2)}, u32[]{:S(2)}) collective-permute-start(f32[4,64,512]{2,1,0:T(8,128)S(1)} %pad_maximum_fusion), channel_id=1, source_target_pairs={{0,16},{8,24},{16,0},{24,8},{1,17},{9,25},{17,1},{25,9},{2,18},{10... | collective-permute-start | bytes 1572872 | tf_op jit(solution)/shard_map/ppermute | solution.py:302

commit v3 on v2

v3 whole, which is shorter than its diff:
```python
import functools

import jax
import jax.numpy as jnp
import numpy as np
from jax import lax
from jax.experimental import pallas as pl
from jax.experimental.pallas import tpu as pltpu
from jax.sharding import PartitionSpec as P

BASIS = ((12.0, 15.0, 16.0), (-20.0, 0.0, 15.0), (9.0, -20.0, 12.0))
NORM = 25.0
VALUE_LOW = -3.0
VALUE_HIGH = 3.0
AMBIENT = 0.35
DIFFUSE = 0.65
LANES = 128
PACK = 16
HALF = 8
AXES = ("view", "row", "col")
DEPTH = 2
SLOTS = 4


def stencil(tile, knot_count):
    scale = (knot_count - 1) / (VALUE_HIGH - VALUE_LOW)
    width = 5 * tile + 3 * PACK
    after, before, above, centre, below, right, left, one = np.cumsum(
        [0, tile, tile, PACK, tile, PACK, tile, tile]
    )
    matrix = np.zeros((4 * tile, width), np.float32)
    for row in range(tile):
        for part, (along_z, along_y, along_x) in enumerate(BASIS):
            line = matrix[part * tile + row]
            line[after + row] += along_z / 2
            line[before + row] -= along_z / 2
            line[centre + row + 1 if row + 1 < tile else below] += along_y / 2
            line[centre + row - 1 if row > 0 else above + PACK - 1] -= along_y / 2
            line[right + row] += along_x / 2
            line[left + row] -= along_x / 2
        line = matrix[3 * tile + row]
        line[centre + row] = scale / 2
        line[one] = -VALUE_LOW * scale / 2 - 0.5
    rounded = matrix.astype(jnp.bfloat16)
    assert np.array_equal(rounded.astype(np.float32), matrix)
    return rounded


def exchange(faces, axis):
    count = lax.axis_size(axis)
    received = []
    for start, face in enumerate(faces):
        pairs = [(i, i + 1) for i in range(start, count - 1, 2)]
        both = pairs + [(j, i) for i, j in pairs]
        received.append(lax.ppermute(face, axis, both) if both else jnp.zeros_like(face))
    return received


def segment_lines(knot_count):
    segments = (knot_count + 1) // 2
    rows = -(-segments // HALF) * HALF
    lines = np.zeros((3, rows, knot_count), np.float32)
    for segment in range(segments):
        left, middle, right = (min(2 * segment + i, knot_count - 1) for i in range(3))
        lines[0, segment, middle] += 1.0
        lines[1, segment, middle] += 2.0
        lines[1, segment, left] -= 2.0
        lines[2, segment, right] += 2.0
        lines[2, segment, middle] -= 2.0
    return lines.reshape(3 * rows, knot_count)


def prepare_kernel(
    odd_ref,
    volume_ref,
    lines_ref,
    color_ref,
    opacity_ref,
    cells_ref,
    table_ref,
    depth_outs,
    row_outs,
    column_outs,
    arrived,
    *,
    optical,
):
    slices, height, width = cells_ref.shape
    chunks = arrived.shape[0]
    size = slices // chunks
    copies = [
        pltpu.make_async_copy(
            volume_ref.at[pl.ds(chunk * size, size)],
            cells_ref.at[pl.ds(chunk * size, size)],
            arrived.at[chunk],
        )
        for chunk in range(chunks)
    ]
    for copy in copies:
        copy.start()
    block = lines_ref.shape[0]
    for channel in range(4):
        knots = color_ref[channel : channel + 1] * DIFFUSE if channel < 3 else opacity_ref[...] * optical
        value = jnp.sum(lines_ref[...] * knots, axis=1, keepdims=True)
        table_ref[pl.ds(channel * block, block)] = jnp.broadcast_to(value, (block, LANES))
    lane = lax.broadcasted_iota(jnp.int16, (height, LANES), 1)
    row = lax.broadcasted_iota(jnp.int16, (slices, width), 0)
    lines = [jnp.zeros((slices, width), cells_ref.dtype)] * len(row_outs)
    for chunk, copy in enumerate(copies):
        copy.wait()
        here = range(chunk * size, (chunk + 1) * size)
        for turn in range(len(row_outs)):
            is_first = odd_ref[1] == 1 - turn
            for z in here:
                line = jnp.where(is_first, cells_ref[z, :1], cells_ref[z, height - 1 :])
                lines[turn] = jnp.where(
                    row == z, jnp.broadcast_to(line, (slices, width)), lines[turn]
                )

        def columns(turn, column, source, shift):
            found = (
                column_outs[turn][...] if chunk else jnp.zeros((height, LANES), cells_ref.dtype)
            )
            for z in here:
                target = (2 * z + shift) % LANES
                cells = cells_ref[z, :, pl.ds(column, LANES)]
                moved = pltpu.roll(cells, (target - source) % LANES, 1)
                found = jnp.where(lane == target, moved, found)
            column_outs[turn][...] = found

        for turn in range(len(column_outs)):
            pl.when(odd_ref[2] == 1 - turn)(functools.partial(columns, turn, 0, 0, -1))
            pl.when(odd_ref[2] == turn)(
                functools.partial(columns, turn, width - LANES, LANES - 1, 0)
            )
    for turn in range(len(row_outs)):
        row_outs[turn][...] = lines[turn]
    for turn in range(len(depth_outs)):
        face = jnp.where(odd_ref[0] == 1 - turn, 0, slices - 1)
        depth_outs[turn][...] = cells_ref[face]


def prepare(volume, tf_color, tf_opacity, odd, depth_total):
    slices, height, width = volume.shape
    assert 2 * slices <= LANES
    knot_count = tf_color.shape[1]
    lines = jnp.asarray(segment_lines(knot_count))
    shapes = [(height, width), (slices, width), (height, LANES)]
    turns = [2 if lax.axis_size(axis) > 2 else 1 for axis in AXES]
    faces = [
        [jax.ShapeDtypeStruct(shape, volume.dtype)] * count for shape, count in zip(shapes, turns)
    ]
    vectors = pl.BlockSpec(memory_space=pltpu.VMEM)
    out_shape = [
        jax.ShapeDtypeStruct(volume.shape, volume.dtype),
        jax.ShapeDtypeStruct((4 * lines.shape[0], LANES), jnp.float32),
        *faces,
    ]
    return pl.pallas_call(
        functools.partial(
            prepare_kernel, optical=float(-2.0 / depth_total * NORM**2 * np.log2(np.e))
        ),
        in_specs=[pl.BlockSpec(memory_space=pltpu.SMEM), pl.BlockSpec(memory_space=pltpu.HBM)]
        + [vectors] * 3,
        out_specs=jax.tree.map(lambda _: vectors, out_shape),
        out_shape=out_shape,
        scratch_shapes=[pltpu.SemaphoreType.DMA((4 if slices % 4 == 0 else 1,))],
        compiler_params=pltpu.CompilerParams(vmem_limit_bytes=48 * 2**20),
    )(odd, volume, lines, tf_color, tf_opacity.reshape(1, knot_count))


def march_kernel(
    ids_ref,
    odd_ref,
    stencil_ref,
    table_ref,
    cells_ref,
    depth_refs,
    line_refs,
    ends_ref,
    out_ref,
    parts_ref,
    sides_ref,
    *,
    tile,
    knot_count,
):
    slices, height, width = cells_ref.shape
    lane = lax.broadcasted_iota(jnp.int16, (tile, LANES), 1)
    ones = jnp.ones((PACK, width), cells_ref.dtype)
    halves = -(-knot_count // (2 * HALF))
    rest = width - LANES
    half_width = width // 2 if width % (2 * LANES) == 0 else width
    tables = [table_ref[start * HALF : start * HALF + HALF] for start in range(12 * halves)]

    def look_up(which, index, in_half):
        for half in range(halves):
            found = jnp.take_along_axis(
                tables[which * halves + half], index, axis=0, mode="promise_in_bounds"
            )
            value = found if half == 0 else jnp.where(in_half[half - 1], found, value)
        return value

    def shade(z, slot, row, column, state):
        lit, second, third, knot = (
            parts_ref[slot, pl.ds(part * tile + row, HALF), pl.ds(column, LANES)]
            for part in range(4)
        )
        knot = jnp.minimum(jnp.maximum(knot, -0.5), knot_count / 2 - 1.0)
        middle = jnp.round(knot)
        segment = middle.astype(jnp.int32)
        offset = knot - middle
        before_middle = offset < 0.0
        index = segment & (HALF - 1) if halves > 1 else segment
        in_half = [middle >= float(HALF * half) for half in range(1, halves)]
        inverse = lax.rsqrt((lit * lit + second * second) + (third * third + NORM * NORM))
        shading = jnp.abs(lit) * inverse + AMBIENT / DIFFUSE
        density = 1.2 / NORM**2 - inverse * inverse
        values = [
            look_up(3 * c, index, in_half)
            + offset
            * jnp.where(
                before_middle,
                look_up(3 * c + 1, index, in_half),
                look_up(3 * c + 2, index, in_half),
            )
            for c in range(4)
        ]
        kept = jnp.exp2(values[3] * density)
        if state is None:
            weight = (1.0 - kept) * shading
            return [value * weight for value in values[:3]] + [kept]
        through = state[3] * kept
        weight = (state[3] - through) * shading
        return [total + value * weight for total, value in zip(state, values[:3])] + [through]

    def one_tile(i, carry):
        place = ids_ref[i]
        start = pl.multiple_of(place * tile, tile)
        steps = ids_ref.shape[0] // out_ref.shape[0]
        group = i // steps
        target = pl.multiple_of((i - group * steps) * tile, tile)
        rows = pl.ds(start, tile)
        odd = [odd_ref[axis] == 1 for axis in range(2)]
        behind, ahead = (
            jnp.where(odd[0], depth_refs[a][rows, :], depth_refs[1 - a][rows, :]) for a in range(2)
        )
        for side, at_face, neighbour in (
            (0, place == 0, pl.ds(jnp.maximum(start - PACK, 0), PACK)),
            (1, start == height - tile, pl.ds(jnp.minimum(start + tile, height - PACK), PACK)),
        ):

            @pl.when(at_face)
            def _():
                lines = jnp.where(odd[1], line_refs[side][...], line_refs[1 - side][...])
                for z in range(slices):
                    sides_ref[side, z] = jnp.broadcast_to(lines[z : z + 1], (PACK, width))

            @pl.when(jnp.logical_not(at_face))
            def _():
                near = pl.ds(pl.multiple_of(neighbour.start, PACK), PACK)
                for z in range(slices):
                    sides_ref[side, z] = cells_ref[z, near, :]

        def gradients(z):
            cells = cells_ref[z, rows, :]
            before = cells_ref[z - 1, rows, :] if z > 0 else behind
            after = cells_ref[z + 1, rows, :] if z + 1 < slices else ahead
            right = pltpu.roll(cells, width - 1, 1)
            left = pltpu.roll(cells, 1, 1)
            ends = ends_ref[rows, :]
            ends = pltpu.roll(ends, LANES - 2 * z, 1) if z else ends
            right_end = jnp.where(lane == LANES - 1, ends, right[:, rest:])
            left_end = jnp.where(lane == 0, ends, left[:, :LANES])
            if rest:
                right_end = jnp.concatenate([right[:, :rest], right_end], axis=1)
                left_end = jnp.concatenate([left_end, left[:, LANES:]], axis=1)
            stacked = jnp.concatenate(
                [after, before, sides_ref[0, z], cells, sides_ref[1, z], right_end, left_end, ones],
                axis=0,
            )
            for column in range(0, width, half_width):
                parts_ref[z % SLOTS, :, pl.ds(column, half_width)] = jnp.dot(
                    stencil_ref[...],
                    stacked[:, column : column + half_width],
                    preferred_element_type=jnp.float32,
                )
                yield

        def shades(first):
            for column in range(0, width, LANES):
                for row in range(0, tile, HALF):
                    here = (pl.ds(target + row, HALF), pl.ds(column, LANES))
                    state = None if first == 0 else [out_ref[(group, c) + here] for c in range(4)]
                    for z in range(first, first + DEPTH):
                        state = shade(z, z % SLOTS, row, column, state)
                    for c in range(4):
                        out_ref[(group, c) + here] = state[c]
                    yield

        def later(first):
            for z in range(first, min(first + DEPTH, slices)):
                yield from gradients(z)

        for _ in later(0):
            pass
        for z in range(0, slices, DEPTH):
            work = list_steps(later(z + DEPTH), DEPTH * (width // half_width), shades(z), (tile // HALF) * (width // LANES))
            for _ in work:
                pass
        return carry

    lax.fori_loop(0, ids_ref.shape[0], one_tile, 0)


def list_steps(first, first_count, second, second_count):
    done = 0
    for step in range(second_count):
        while done * second_count <= step * first_count and done < first_count:
            next(first, None)
            done += 1
        next(second)
        yield
    for _ in first:
        pass


def march(volume, halos, ids, odd, tables, knot_count, tile, groups):
    slices, height, width = volume.shape
    depth, lines, ends = halos
    assert slices % DEPTH == 0
    matrix = jnp.asarray(stencil(tile, knot_count))
    count = ids.shape[0]
    scalars = pl.BlockSpec(memory_space=pltpu.SMEM)
    vectors = pl.BlockSpec(memory_space=pltpu.VMEM)
    return pl.pallas_call(
        functools.partial(march_kernel, tile=tile, knot_count=knot_count),
        in_specs=[scalars, scalars, vectors, vectors, vectors, [vectors] * 2, [vectors] * 2, vectors],
        out_specs=vectors,
        out_shape=jax.ShapeDtypeStruct((groups, 4, count // groups * tile, width), jnp.float32),
        scratch_shapes=[
            pltpu.VMEM((SLOTS, 4 * tile, width), jnp.float32),
            pltpu.VMEM((2, slices, PACK, width), volume.dtype),
        ],
        compiler_params=pltpu.CompilerParams(vmem_limit_bytes=48 * 2**20),
        cost_estimate=pl.CostEstimate(flops=1, transcendentals=0, bytes_accessed=1),
    )(ids, odd, matrix, tables, volume, depth, lines, ends)


def over(nearer, farther):
    through = nearer[3:]
    return jnp.concatenate([nearer[:3] + through * farther[:3], through * farther[3:]], axis=0)


def merged(own, other, side):
    nearer = jnp.where(side == 0, own, other)
    farther = jnp.where(side == 0, other, own)
    return over(nearer, farther)


def from_partner(value, axis, bit):
    pairs = [(source, source ^ (1 << bit)) for source in range(lax.axis_size(axis))]
    return lax.ppermute(value, axis, pairs)


def on_device(volume, tf_color, tf_opacity):
    view_count = lax.axis_size("view")
    position = lax.axis_index("view")
    slices, height, width = volume.shape
    knot_count = tf_color.shape[1]
    tile_rows = height // view_count
    tile = min(32, tile_rows)
    bits = view_count.bit_length() - 1
    group_bits = min(2, bits)
    groups = 1 << group_bits
    per_group = view_count // groups

    odd = jnp.stack([lax.axis_index(axis) % 2 for axis in AXES])
    cells, tables, *faces = prepare(volume, tf_color, tf_opacity, odd, slices * view_count)
    depth, lines, ends = (exchange(face, axis) for face, axis in zip(faces, AXES))
    depth, lines = (
        found if len(found) == 2 else found + [jnp.zeros_like(found[0])] for found in (depth, lines)
    )
    halos = (depth, lines, sum(ends[1:], ends[0]))

    steps = tile_rows // tile

    def march_groups(distances, after=None):
        blocks = np.arange(per_group) * groups
        places = jnp.stack([blocks + (position % groups ^ distance) for distance in distances])
        ids = (places[..., None] * steps + np.arange(steps)).reshape(-1).astype(jnp.int32)
        if after is not None:
            ids, _ = lax.optimization_barrier((ids, after))
        return march(cells, halos, ids, odd, tables, knot_count, tile, len(distances))

    side = [position >> bit & 1 for bit in range(bits)]
    if groups == 4:
        (far,) = march_groups([3])
        far_received = from_partner(far, "view", 0)
        (near,) = march_groups([2], far)
        sent = merged(near, far_received, side[0])
        far, near = march_groups([1, 0], sent)
        received = from_partner(sent, "view", 1)
        image = merged(merged(near, from_partner(far, "view", 0), side[0]), received, side[1])
    elif groups == 2:
        far, near = march_groups([1, 0])
        image = merged(near, from_partner(far, "view", 0), side[0])
    else:
        (image,) = march_groups([0])
    image = image.reshape((4,) + (2,) * (bits - group_bits) + (tile_rows, width))
    for bit in range(group_bits, bits):
        axis = bits - bit
        kept = lax.dynamic_index_in_dim(image, side[bit], axis, keepdims=False)
        sent = lax.dynamic_index_in_dim(image, 1 - side[bit], axis, keepdims=False)
        image = merged(kept, from_partner(sent, "view", bit), side[bit])
    image = jnp.concatenate([image[:3], 1.0 - image[3:]], axis=0)
    return image.reshape(4, 1, tile_rows, width)


def solution(mesh):
    placed = (P("view", "row", "col"), P(), P())
    return jax.shard_map(
        on_device,
        mesh=mesh,
        in_specs=placed,
        out_specs=P(None, "view", "row", "col"),
        check_vma=False,
    )
```

time: 52.6 us -> 60.5 us (1.15)
  local copies, waits for them, and re-layouts: 0.53 us -> 8.47 us
  Pallas kernels: 31 us -> 23.6 us
  waiting for transfers between devices: 9.05 us -> 16.4 us
    unnamed x6 -> x14, local copies, waits for them, and re-layouts: 0.01 us -> 8.35 us
    pallas_call x5 -> x4, Pallas kernels: 31 us -> 23.6 us  [the longest x3 20.6 us: march(): pl.pallas_call(functools.partial(march_kernel, tile=tile, knot_count=knot...]
    ppermute x3, waiting for transfers between devices: 6.91 us -> 13.7 us  [from_partner(): return lax.ppermute(value, axis, pairs)]
    ppermute x5, waiting for transfers between devices: 2.14 us -> 2.77 us  [exchange(): lax.ppermute(face, axis, both)]
  transfers between devices with their start and end apart: 8 -> 8, of which waited for: 2 -> 4; matrix products, arithmetic and copies ran while one was open for 1% -> 1% of each run, Pallas kernels for 26% -> 9%
where the time goes in v3:
time: 60.5 us; the launch traced here: 60.3 us
  Pallas kernels  23.6 us (39%)
  waiting for transfers between devices  16.4 us (27%)
  starting transfers between devices  9.8 us (16%)
  local copies, waits for them, and re-layouts  8.47 us (14%)
  other arithmetic  1.76 us (3%)
    pallas_call x3, Pallas kernels, march(): pl.pallas_call(functools.partial(march_kernel, tile=tile, knot_count=knot...  20.6 us
    ppermute x3, waiting for transfers between devices, from_partner(): return lax.ppermute(value, axis, pairs)  13.7 us
    ppermute x5, starting transfers between devices, exchange(): lax.ppermute(face, axis, both)  9.18 us
    unnamed x14, local copies, waits for them, and re-layouts  8.35 us
    pallas_call x1, Pallas kernels, prepare(): pl.pallas_call(functools.partial(prepare_kernel, optical=float(-2.0 / dep...  2.95 us
    ppermute x5, waiting for transfers between devices, exchange(): lax.ppermute(face, axis, both)  2.77 us
  transfers between devices with their start and end apart: 8, of which 4 were waited for; matrix products, arithmetic and copies ran while one was open for 1% of the time, Pallas kernels for 9%

profile of v3, /device:TPU:12, one launch (start us, length us, event | category | flops | bytes accessed | tf_op | source)
XLA Modules:
  0.0 60.3 jit_solution(7789346194628195936)
XLA Ops:
  0.1 0.7 %copy-done.4 = f32[24,16]{1,0:T(8,128)S(1)} copy-done((f32[24,16]{1,0:T(8,128)S(1)}, f32[24,16]{1,0:T(8,128)}, u32[]{:S(2)}) %copy-start.4) | copy-done | bytes 1560
  0.8 0.7 %copy-done.5 = f32[3,16]{1,0:T(4,128)S(1)} copy-done((f32[3,16]{1,0:T(4,128)S(1)}, f32[3,16]{1,0:T(4,128)}, u32[]{:S(2)}) %copy-start.5) | copy-done | bytes 216
  1.5 0.7 %copy-done.6 = f32[16]{0:T(128)S(1)} copy-done((f32[16]{0:T(128)S(1)}, f32[16]{0:T(128)}, u32[]{:S(2)}) %copy-start.6) | copy-done | bytes 88
  2.1 2.9 %shard_map.127 = (bf16[16,256,512]{2,1,0:T(8,128)(2,1)S(1)}, f32[96,128]{1,0:T(8,128)S(1)}, bf16[256,512]{1,0:T(8,128)(2,1)S(1)}, bf16[256,512]{1,0:T(8,128)(2,1...) custom-call(s32[3]{0:T(128)S(1)} %pad_add_fusion.odd_ref, ...), custom_call_target="tpu_custom_call" | custom-call | tf_op jit(solution)/shard_map/pallas_call | solution.py:159
  5.1 1.9 %copy-done = bf16[16,256,512]{2,1,0:T(8,128)(2,1)} copy-done((bf16[16,256,512]{2,1,0:T(8,128)(2,1)}, bf16[16,256,512]{2,1,0:T(8,128)(2,1)S(1)}, u32[]{:S(2)}) %copy-start) | copy-done | bytes 4194328
  7.0 2.5 %collective-permute-start.1 = (bf16[256,512]{1,0:T(8,128)(2,1)S(1)}, bf16[256,512]{1,0:T(8,128)(2,1)S(1)}, u32[]{:S(2)}, u32[]{:S(2)}) collective-permute-start(bf16[256,512]{1,0:T(8,128)(2,1)S(1)} %get-tuple-element.17), channel_id=1, source_target_pairs={{8,16},{16,8},{9,17},{17,9},{10,18},{18,10},{11,19},{19,11},{12,20... | collective-permute-start | bytes 786440 | tf_op jit(solution)/shard_map/ppermute | solution.py:55
  9.6 5.0 %collective-permute-start.3 = (bf16[16,512]{1,0:T(8,128)(2,1)S(1)}, bf16[16,512]{1,0:T(8,128)(2,1)S(1)}, u32[]{:S(2)}, u32[]{:S(2)}) collective-permute-start(bf16[16,512]{1,0:T(8,128)(2,1)S(1)} %get-tuple-element.19), channel_id=1, source_target_pairs={{2,4},{4,2},{3,5},{5,3},{10,12},{12,10},{11,13},{13,11},{18,20},{2... | collective-permute-start | bytes 49160 | tf_op jit(solution)/shard_map/ppermute | solution.py:55
  14.7 1.6 %collective-permute-start.4 = (bf16[256,128]{1,0:T(8,128)(2,1)S(1)}, bf16[256,128]{1,0:T(8,128)(2,1)S(1)}, u32[]{:S(2)}, u32[]{:S(2)}) collective-permute-start(bf16[256,128]{1,0:T(8,128)(2,1)S(1)} %get-tuple-element.20), channel_id=1, source_target_pairs={{0,1},{1,0},{2,3},{3,2},{4,5},{5,4},{6,7},{7,6},{8,9},{9,8},{10,11... | collective-permute-start | bytes 196616 | tf_op jit(solution)/shard_map/ppermute | solution.py:55
  16.2 0.1 collective-permute-done.3.line_refs_1_
  16.4 2.6 %collective-permute-done.4.ends_ref = bf16[256,128]{1,0:T(8,128)(2,1)S(1)} collective-permute-done((bf16[256,128]{1,0:T(8,128)(2,1)S(1)}, bf16[256,128]{1,0:T(8,128)(2,1)S(1)}, u32[]{:S(2)}, u32[]{:S(2)}) %collective-permute-start.4) | collective-permute-done | bytes 65568 | tf_op jit(solution)/shard_map/ppermute | solution.py:55
  19.0 2.2 %copy-done.1 = bf16[16,256,512]{2,1,0:T(8,128)(2,1)S(1)} copy-done((bf16[16,256,512]{2,1,0:T(8,128)(2,1)S(1)}, bf16[16,256,512]{2,1,0:T(8,128)(2,1)}, u32[]{:S(2)}) %copy-start.1) | copy-done | bytes 4194328
  21.2 5.3 %shard_map.128 = f32[1,4,64,512]{3,2,1,0:T(8,128)S(1)} custom-call(s32[2]{0:T(128)S(1)} %iota_add_fusion.1.ids_ref, s32[3]{0:T(128)S(1)} %pad_add_fusion.odd_ref, bf16[128,208]{1,0:T(8,128)(2,1)S(1)} %copy-done.3, f32[96,128]{1,0:T(8,128)S(1)} %get-tuple-element.14.table_ref, bf16[16,256,512]{2,1,0:T(8,128)(2,1)S(1)} %copy-done.1, ...), custom_call_target="tpu_custom_call" | custom-call | flops 1 | bytes 1 | tf_op jit(solution)/shard_map/pallas_call | solution.py:336
  26.7 0.1 add.98.ids_ref
  26.8 2.2 %copy-done.2 = bf16[16,256,512]{2,1,0:T(8,128)(2,1)S(1)} copy-done((bf16[16,256,512]{2,1,0:T(8,128)(2,1)S(1)}, bf16[16,256,512]{2,1,0:T(8,128)(2,1)}, u32[]{:S(2)}) %copy-start.2) | copy-done | bytes 4194328
  29.0 5.3 %shard_map.129 = f32[1,4,64,512]{3,2,1,0:T(8,128)S(1)} custom-call(s32[2]{0:T(128)S(1)} %iota_add_fusion.2.ids_ref, s32[3]{0:T(128)S(1)} %pad_add_fusion.odd_ref, bf16[128,208]{1,0:T(8,128)(2,1)S(1)} %copy-done.3, f32[96,128]{1,0:T(8,128)S(1)} %get-tuple-element.14.table_ref, bf16[16,256,512]{2,1,0:T(8,128)(2,1)S(1)} %copy-done.2, ...), custom_call_target="tpu_custom_call" | custom-call | flops 1 | bytes 1 | tf_op jit(solution)/shard_map/pallas_call | solution.py:336
  34.4 0.1 bitcast_select_fusion.1
  34.6 10.0 %shard_map.130 = f32[2,4,64,512]{3,2,1,0:T(8,128)S(1)} custom-call(s32[4]{0:T(128)S(1)} %add.98.ids_ref, s32[3]{0:T(128)S(1)} %pad_add_fusion.odd_ref, bf16[128,208]{1,0:T(8,128)(2,1)S(1)} %copy-done.3, f32[96,128]{1,0:T(8,128)S(1)} %get-tuple-element.14.table_ref, bf16[16,256,512]{2,1,0:T(8,128)(2,1)S(1)} %copy-done.2, ...), custom_call_target="tpu_custom_call" | custom-call | flops 1 | bytes 1 | tf_op jit(solution)/shard_map/pallas_call | solution.py:336
  44.7 0.5 collective-permute-start.6
  45.3 1.5 %collective-permute-done.6 = f32[4,64,512]{2,1,0:T(8,128)S(1)} collective-permute-done((f32[4,64,512]{2,1,0:T(8,128)S(1)}, f32[4,64,512]{2,1,0:T(8,128)S(1)}, u32[]{:S(2)}, u32[]{:S(2)}) %collective-permute-start.6) | collective-permute-done | bytes 524320 | tf_op jit(solution)/shard_map/ppermute | solution.py:363
  46.8 0.1 fusion.1
  47.0 12.1 %collective-permute-done.7 = f32[4,64,512]{2,1,0:T(8,128)S(1)} collective-permute-done((f32[4,64,512]{2,1,0:T(8,128)S(1)}, f32[4,64,512]{2,1,0:T(8,128)S(1)}, u32[]{:S(2)}, u32[]{:S(2)}) %collective-permute-start.7) | collective-permute-done | bytes 524320 | tf_op jit(solution)/shard_map/ppermute | solution.py:363
  59.2 0.1 fusion.3
  59.3 0.1 fusion.4
  59.4 0.8 %maximum_bitcast_fusion = f32[4,1,64,512]{3,2,1,0:T(8,128)} fusion(f32[1,64,512]{2,1,0:T(8,128)S(1)} %get-tuple-element.30, f32[3,64,512]{2,1,0:T(8,128)S(1)} %fusion.4), kind=kLoop, calls=%fused_computation.4 | loop fusion | flops 131072 | bytes 1048576 | tf_op jit(solution)/shard_map/reshape | solution.py:417
  (28 shorter events, 0.7 us)
Async XLA Ops:
  0.0 19.0 %copy-start.3 = (bf16[128,208]{1,0:T(8,128)(2,1)S(1)}, bf16[128,208]{1,0:T(8,128)(2,1)}, u32[]{:S(2)}) copy-start(bf16[128,208]{1,0:T(8,128)(2,1)} %constant.68.clone.stencil_ref) | copy-start | bytes 159748
  0.1 0.7 %copy-start.4 = (f32[24,16]{1,0:T(8,128)S(1)}, f32[24,16]{1,0:T(8,128)}, u32[]{:S(2)}) copy-start(f32[24,16]{1,0:T(8,128)} %constant.66.clone.lines_ref) | copy-start | bytes 4612
  0.8 0.7 %copy-start.5 = (f32[3,16]{1,0:T(4,128)S(1)}, f32[3,16]{1,0:T(4,128)}, u32[]{:S(2)}) copy-start(f32[3,16]{1,0:T(4,128)} %color_ref.1) | copy-start | bytes 580
  1.5 0.7 %copy-start.6 = (f32[16]{0:T(128)S(1)}, f32[16]{0:T(128)}, u32[]{:S(2)}) copy-start(f32[16]{0:T(128)} %param.15) | copy-start | bytes 196
  5.1 1.9 %copy-start = (bf16[16,256,512]{2,1,0:T(8,128)(2,1)}, bf16[16,256,512]{2,1,0:T(8,128)(2,1)S(1)}, u32[]{:S(2)}) copy-start(bf16[16,256,512]{2,1,0:T(8,128)(2,1)S(1)} %get-tuple-element.15.cells_ref) | copy-start | bytes 12582916
  7.0 12.0 %collective-permute-start = (bf16[256,512]{1,0:T(8,128)(2,1)S(1)}, bf16[256,512]{1,0:T(8,128)(2,1)S(1)}, u32[]{:S(2)}, u32[]{:S(2)}) collective-permute-start(bf16[256,512]{1,0:T(8,128)(2,1)S(1)} %get-tuple-element.16), channel_id=1, source_target_pairs={{0,8},{16,24},{8,0},{24,16},{1,9},{17,25},{9,1},{25,17},{2,10},{18... | collective-permute-start | bytes 786440 | tf_op jit(solution)/shard_map/ppermute | solution.py:55
  7.0 12.0 %collective-permute-start.1 = (bf16[256,512]{1,0:T(8,128)(2,1)S(1)}, bf16[256,512]{1,0:T(8,128)(2,1)S(1)}, u32[]{:S(2)}, u32[]{:S(2)}) collective-permute-start(bf16[256,512]{1,0:T(8,128)(2,1)S(1)} %get-tuple-element.17), channel_id=1, source_target_pairs={{8,16},{16,8},{9,17},{17,9},{10,18},{18,10},{11,19},{19,11},{12,20... | collective-permute-start | bytes 786440 | tf_op jit(solution)/shard_map/ppermute | solution.py:55
  9.6 6.7 %collective-permute-start.2 = (bf16[16,512]{1,0:T(8,128)(2,1)S(1)}, bf16[16,512]{1,0:T(8,128)(2,1)S(1)}, u32[]{:S(2)}, u32[]{:S(2)}) collective-permute-start(bf16[16,512]{1,0:T(8,128)(2,1)S(1)} %get-tuple-element.18), channel_id=1, source_target_pairs={{0,2},{4,6},{2,0},{6,4},{1,3},{5,7},{3,1},{7,5},{8,10},{12,14},{10... | collective-permute-start | bytes 49160 | tf_op jit(solution)/shard_map/ppermute | solution.py:55
  9.6 6.7 %collective-permute-start.3 = (bf16[16,512]{1,0:T(8,128)(2,1)S(1)}, bf16[16,512]{1,0:T(8,128)(2,1)S(1)}, u32[]{:S(2)}, u32[]{:S(2)}) collective-permute-start(bf16[16,512]{1,0:T(8,128)(2,1)S(1)} %get-tuple-element.19), channel_id=1, source_target_pairs={{2,4},{4,2},{3,5},{5,3},{10,12},{12,10},{11,13},{13,11},{18,20},{2... | collective-permute-start | bytes 49160 | tf_op jit(solution)/shard_map/ppermute | solution.py:55
  14.7 4.3 %collective-permute-start.4 = (bf16[256,128]{1,0:T(8,128)(2,1)S(1)}, bf16[256,128]{1,0:T(8,128)(2,1)S(1)}, u32[]{:S(2)}, u32[]{:S(2)}) collective-permute-start(bf16[256,128]{1,0:T(8,128)(2,1)S(1)} %get-tuple-element.20), channel_id=1, source_target_pairs={{0,1},{1,0},{2,3},{3,2},{4,5},{5,4},{6,7},{7,6},{8,9},{9,8},{10,11... | collective-permute-start | bytes 196616 | tf_op jit(solution)/shard_map/ppermute | solution.py:55
  19.0 2.2 %copy-start.1 = (bf16[16,256,512]{2,1,0:T(8,128)(2,1)S(1)}, bf16[16,256,512]{2,1,0:T(8,128)(2,1)}, u32[]{:S(2)}) copy-start(bf16[16,256,512]{2,1,0:T(8,128)(2,1)} %copy-done) | copy-start | bytes 12582916
  26.5 7.9 %collective-permute-start.5 = (f32[4,64,512]{2,1,0:T(8,128)S(1)}, f32[4,64,512]{2,1,0:T(8,128)S(1)}, u32[]{:S(2)}, u32[]{:S(2)}) collective-permute-start(f32[4,64,512]{2,1,0:T(8,128)S(1)} %bitcast.32), channel_id=1, source_target_pairs={{0,8},{8,0},{16,24},{24,16},{1,9},{9,1},{17,25},{25,17},{2,10},{10... | collective-permute-start | bytes 1572872 | tf_op jit(solution)/shard_map/ppermute | solution.py:363
  26.8 2.2 %copy-start.2 = (bf16[16,256,512]{2,1,0:T(8,128)(2,1)S(1)}, bf16[16,256,512]{2,1,0:T(8,128)(2,1)}, u32[]{:S(2)}) copy-start(bf16[16,256,512]{2,1,0:T(8,128)(2,1)} %copy-done) | copy-start | bytes 12582916
  44.7 2.1 %collective-permute-start.6 = (f32[4,64,512]{2,1,0:T(8,128)S(1)}, f32[4,64,512]{2,1,0:T(8,128)S(1)}, u32[]{:S(2)}, u32[]{:S(2)}) collective-permute-start(f32[4,64,512]{2,1,0:T(8,128)S(1)} %slice_bitcast_fusion), channel_id=1, source_target_pairs={{0,8},{8,0},{16,24},{24,16},{1,9},{9,1},{17,25},{25,17},{2,10},{10... | collective-permute-start | bytes 1572872 | tf_op jit(solution)/shard_map/ppermute | solution.py:363
  45.3 13.9 %collective-permute-start.7 = (f32[4,64,512]{2,1,0:T(8,128)S(1)}, f32[4,64,512]{2,1,0:T(8,128)S(1)}, u32[]{:S(2)}, u32[]{:S(2)}) collective-permute-start(f32[4,64,512]{2,1,0:T(8,128)S(1)} %pad_maximum_fusion), channel_id=1, source_target_pairs={{0,16},{8,24},{16,0},{24,8},{1,17},{9,25},{17,1},{25,9},{2,18},{10... | collective-permute-start | bytes 1572872 | tf_op jit(solution)/shard_map/ppermute | solution.py:363

commit v4 on v3

--- a/solution.py
+++ b/solution.py
@@ -20,6 +20,10 @@
 AXES = ("view", "row", "col")
 DEPTH = 2
 SLOTS = 4
+CODE_SCALE = 240.0
+CODE_SHIFT = 120.0
+SCALARS = pl.BlockSpec(memory_space=pltpu.SMEM)
+VECTORS = pl.BlockSpec(memory_space=pltpu.VMEM)
 
 
 def stencil(tile, knot_count):
@@ -71,19 +75,7 @@
 
 
 def prepare_kernel(
-    odd_ref,
-    volume_ref,
-    lines_ref,
-    color_ref,
-    opacity_ref,
-    cells_ref,
-    table_ref,
-    depth_outs,
-    row_outs,
-    column_outs,
-    arrived,
-    *,
-    optical,
+    scalars_ref, volume_ref, cells_ref, depth_outs, row_outs, column_outs, arrived
 ):
     slices, height, width = cells_ref.shape
     chunks = arrived.shape[0]
@@ -98,11 +90,6 @@
     ]
     for copy in copies:
         copy.start()
-    block = lines_ref.shape[0]
-    for channel in range(4):
-        knots = color_ref[channel : channel + 1] * DIFFUSE if channel < 3 else opacity_ref[...] * optical
-        value = jnp.sum(lines_ref[...] * knots, axis=1, keepdims=True)
-        table_ref[pl.ds(channel * block, block)] = jnp.broadcast_to(value, (block, LANES))
     lane = lax.broadcasted_iota(jnp.int16, (height, LANES), 1)
     row = lax.broadcasted_iota(jnp.int16, (slices, width), 0)
     lines = [jnp.zeros((slices, width), cells_ref.dtype)] * len(row_outs)
@@ -110,7 +97,7 @@
         copy.wait()
         here = range(chunk * size, (chunk + 1) * size)
         for turn in range(len(row_outs)):
-            is_first = odd_ref[1] == 1 - turn
+            is_first = scalars_ref[1] == 1 - turn
             for z in here:
                 line = jnp.where(is_first, cells_ref[z, :1], cells_ref[z, height - 1 :])
                 lines[turn] = jnp.where(
@@ -129,51 +116,41 @@
             column_outs[turn][...] = found
 
         for turn in range(len(column_outs)):
-            pl.when(odd_ref[2] == 1 - turn)(functools.partial(columns, turn, 0, 0, -1))
-            pl.when(odd_ref[2] == turn)(
+            pl.when(scalars_ref[2] == 1 - turn)(functools.partial(columns, turn, 0, 0, -1))
+            pl.when(scalars_ref[2] == turn)(
                 functools.partial(columns, turn, width - LANES, LANES - 1, 0)
             )
     for turn in range(len(row_outs)):
         row_outs[turn][...] = lines[turn]
     for turn in range(len(depth_outs)):
-        face = jnp.where(odd_ref[0] == 1 - turn, 0, slices - 1)
+        face = jnp.where(scalars_ref[0] == 1 - turn, 0, slices - 1)
         depth_outs[turn][...] = cells_ref[face]
 
 
-def prepare(volume, tf_color, tf_opacity, odd, depth_total):
+def prepare(volume, scalars):
     slices, height, width = volume.shape
     assert 2 * slices <= LANES
-    knot_count = tf_color.shape[1]
-    lines = jnp.asarray(segment_lines(knot_count))
     shapes = [(height, width), (slices, width), (height, LANES)]
     turns = [2 if lax.axis_size(axis) > 2 else 1 for axis in AXES]
-    faces = [
+    out_shape = [jax.ShapeDtypeStruct(volume.shape, volume.dtype)] + [
         [jax.ShapeDtypeStruct(shape, volume.dtype)] * count for shape, count in zip(shapes, turns)
     ]
-    vectors = pl.BlockSpec(memory_space=pltpu.VMEM)
-    out_shape = [
-        jax.ShapeDtypeStruct(volume.shape, volume.dtype),
-        jax.ShapeDtypeStruct((4 * lines.shape[0], LANES), jnp.float32),
-        *faces,
-    ]
     return pl.pallas_call(
-        functools.partial(
-            prepare_kernel, optical=float(-2.0 / depth_total * NORM**2 * np.log2(np.e))
-        ),
-        in_specs=[pl.BlockSpec(memory_space=pltpu.SMEM), pl.BlockSpec(memory_space=pltpu.HBM)]
-        + [vectors] * 3,
-        out_specs=jax.tree.map(lambda _: vectors, out_shape),
+        prepare_kernel,
+        in_specs=[pl.BlockSpec(memory_space=pltpu.SMEM), pl.BlockSpec(memory_space=pltpu.HBM)],
+        out_specs=jax.tree.map(lambda _: VECTORS, out_shape),
         out_shape=out_shape,
         scratch_shapes=[pltpu.SemaphoreType.DMA((4 if slices % 4 == 0 else 1,))],
-        compiler_params=pltpu.CompilerParams(vmem_limit_bytes=48 * 2**20),
-    )(odd, volume, lines, tf_color, tf_opacity.reshape(1, knot_count))
+        compiler_params=pltpu.CompilerParams(vmem_limit_bytes=24 * 2**20),
+    )(scalars, volume)
 
 
 def march_kernel(
-    ids_ref,
-    odd_ref,
+    scalars_ref,
     stencil_ref,
-    table_ref,
+    lines_ref,
+    color_ref,
+    opacity_ref,
     cells_ref,
     depth_refs,
     line_refs,
@@ -182,16 +159,26 @@
     parts_ref,
     sides_ref,
     *,
+    first_id,
+    count,
     tile,
-    knot_count,
+    optical,
 ):
     slices, height, width = cells_ref.shape
     lane = lax.broadcasted_iota(jnp.int16, (tile, LANES), 1)
     ones = jnp.ones((PACK, width), cells_ref.dtype)
+    knot_count = color_ref.shape[1]
     halves = -(-knot_count // (2 * HALF))
     rest = width - LANES
     half_width = width // 2 if width % (2 * LANES) == 0 else width
-    tables = [table_ref[start * HALF : start * HALF + HALF] for start in range(12 * halves)]
+    tables = []
+    for channel in range(4):
+        knots = (
+            color_ref[channel : channel + 1] * DIFFUSE if channel < 3 else opacity_ref[...] * optical
+        )
+        values = jnp.sum(lines_ref[...] * knots, axis=1, keepdims=True)
+        for start in range(0, values.shape[0], HALF):
+            tables.append(jnp.broadcast_to(values[start : start + HALF], (HALF, LANES)))
 
     def look_up(which, index, in_half):
         for half in range(halves):
@@ -235,13 +222,13 @@
         return [total + value * weight for total, value in zip(state, values[:3])] + [through]
 
     def one_tile(i, carry):
-        place = ids_ref[i]
+        place = scalars_ref[first_id + i]
         start = pl.multiple_of(place * tile, tile)
-        steps = ids_ref.shape[0] // out_ref.shape[0]
+        steps = count // out_ref.shape[0]
         group = i // steps
         target = pl.multiple_of((i - group * steps) * tile, tile)
         rows = pl.ds(start, tile)
-        odd = [odd_ref[axis] == 1 for axis in range(2)]
+        odd = [scalars_ref[axis] == 1 for axis in range(2)]
         behind, ahead = (
             jnp.where(odd[0], depth_refs[a][rows, :], depth_refs[1 - a][rows, :]) for a in range(2)
         )
@@ -310,7 +297,7 @@
                 pass
         return carry
 
-    lax.fori_loop(0, ids_ref.shape[0], one_tile, 0)
+    lax.fori_loop(0, count, one_tile, 0)
 
 
 def list_steps(first, first_count, second, second_count):
@@ -325,26 +312,91 @@
         pass
 
 
-def march(volume, halos, ids, odd, tables, knot_count, tile, groups):
-    slices, height, width = volume.shape
+def march(cells, halos, scalars, first_id, count, groups, transfer, depth_total, tile):
+    slices, height, width = cells.shape
     depth, lines, ends = halos
     assert slices % DEPTH == 0
-    matrix = jnp.asarray(stencil(tile, knot_count))
-    count = ids.shape[0]
-    scalars = pl.BlockSpec(memory_space=pltpu.SMEM)
-    vectors = pl.BlockSpec(memory_space=pltpu.VMEM)
+    tf_color, tf_opacity = transfer
+    knot_count = tf_color.shape[1]
+    optical = float(-2.0 / depth_total * NORM**2 * np.log2(np.e))
     return pl.pallas_call(
-        functools.partial(march_kernel, tile=tile, knot_count=knot_count),
-        in_specs=[scalars, scalars, vectors, vectors, vectors, [vectors] * 2, [vectors] * 2, vectors],
-        out_specs=vectors,
+        functools.partial(
+            march_kernel, first_id=first_id, count=count, tile=tile, optical=optical
+        ),
+        in_specs=[SCALARS] + [VECTORS] * 5 + [[VECTORS] * 2, [VECTORS] * 2, VECTORS],
+        out_specs=VECTORS,
         out_shape=jax.ShapeDtypeStruct((groups, 4, count // groups * tile, width), jnp.float32),
         scratch_shapes=[
             pltpu.VMEM((SLOTS, 4 * tile, width), jnp.float32),
-            pltpu.VMEM((2, slices, PACK, width), volume.dtype),
+            pltpu.VMEM((2, slices, PACK, width), cells.dtype),
         ],
-        compiler_params=pltpu.CompilerParams(vmem_limit_bytes=48 * 2**20),
-        cost_estimate=pl.CostEstimate(flops=1, transcendentals=0, bytes_accessed=1),
-    )(ids, odd, matrix, tables, volume, depth, lines, ends)
+        compiler_params=pltpu.CompilerParams(vmem_limit_bytes=24 * 2**20),
+    )(
+        scalars,
+        jnp.asarray(stencil(tile, knot_count)),
+        jnp.asarray(segment_lines(knot_count)),
+        tf_color,
+        tf_opacity.reshape(1, knot_count),
+        cells,
+        depth,
+        lines,
+        ends,
+    )
+
+
+def ordered_over(first, second, swapped):
+    colours = [
+        jnp.where(swapped, b, a) + jnp.where(swapped, second[3], first[3]) * jnp.where(swapped, a, b)
+        for a, b in zip(first[:3], second[:3])
+    ]
+    return colours + [first[3] * second[3]]
+
+
+def pair_kernel(scalars_ref, own_ref, other_ref, code_ref, *, side):
+    own = [own_ref[0, c] for c in range(4)]
+    other = [other_ref[0, c] for c in range(4)]
+    merged = ordered_over(own, other, scalars_ref[side] == 1)
+    for c in range(4):
+        code_ref[c] = jnp.exp2(CODE_SCALE * merged[c] - CODE_SHIFT).astype(code_ref.dtype)
+
+
+def last_kernel(scalars_ref, own_ref, other_ref, code_ref, out_ref, *, side, finish):
+    rows = pl.ds(pl.multiple_of(pl.program_id(0) * out_ref.shape[1], HALF), out_ref.shape[1])
+    own = [own_ref[0, c, rows] for c in range(4)]
+    other = [other_ref[1, c, rows] for c in range(4)]
+    coded = pl.ds(pl.multiple_of(pl.program_id(0) * out_ref.shape[1], PACK), out_ref.shape[1])
+    far = [
+        (jnp.log2(code_ref[c, coded].astype(jnp.float32)) + CODE_SHIFT) * (1.0 / CODE_SCALE)
+        for c in range(4)
+    ]
+    pair = ordered_over(own, other, scalars_ref[side] == 1)
+    merged = ordered_over(pair, far, scalars_ref[side + 1] == 1)
+    for c in range(3):
+        out_ref[c] = merged[c]
+    out_ref[3] = 1.0 - merged[3] if finish else merged[3]
+
+
+def merge_pair(scalars, own, other, side):
+    return pl.pallas_call(
+        functools.partial(pair_kernel, side=side),
+        in_specs=[SCALARS, VECTORS, VECTORS],
+        out_specs=VECTORS,
+        out_shape=jax.ShapeDtypeStruct(own.shape[1:], jnp.bfloat16),
+        compiler_params=pltpu.CompilerParams(vmem_limit_bytes=24 * 2**20),
+    )(scalars, own, other)
+
+
+def merge_last(scalars, own, other, code, side, finish):
+    _, _, rows, width = own.shape
+    steps = 2 if rows % (2 * PACK) == 0 else 1
+    return pl.pallas_call(
+        functools.partial(last_kernel, side=side, finish=finish),
+        grid=(steps,),
+        in_specs=[SCALARS, VECTORS, VECTORS, VECTORS],
+        out_specs=pl.BlockSpec((4, rows // steps, width), lambda i: (0, i, 0)),
+        out_shape=jax.ShapeDtypeStruct(own.shape[1:], jnp.float32),
+        compiler_params=pltpu.CompilerParams(vmem_limit_bytes=24 * 2**20),
+    )(scalars, own, other, code)
 
 
 def over(nearer, farther):
@@ -367,7 +419,6 @@
     view_count = lax.axis_size("view")
     position = lax.axis_index("view")
     slices, height, width = volume.shape
-    knot_count = tf_color.shape[1]
     tile_rows = height // view_count
     tile = min(32, tile_rows)
     bits = view_count.bit_length() - 1
@@ -375,44 +426,74 @@
     groups = 1 << group_bits
     per_group = view_count // groups
 
-    odd = jnp.stack([lax.axis_index(axis) % 2 for axis in AXES])
-    cells, tables, *faces = prepare(volume, tf_color, tf_opacity, odd, slices * view_count)
+    calls = {4: ([3, 1], [2], [0]), 2: ([1], [0]), 1: ([0],)}[groups]
+    steps = tile_rows // tile
+    count = per_group * steps
+    blocks = (np.arange(per_group)[:, None] * groups * steps + np.arange(steps)).reshape(-1)
+    first_side = len(AXES)
+    first_id = first_side + bits
+    scalars = jnp.concatenate(
+        [
+            jnp.stack(
+                [lax.axis_index(axis) & 1 for axis in AXES]
+                + [position >> bit & 1 for bit in range(bits)]
+            )
+        ]
+        + [
+            (position & (groups - 1) ^ distance) * steps + blocks
+            for call in calls
+            for distance in call
+        ]
+    ).astype(jnp.int32)
+
+    volume = pltpu.with_memory_space_constraint(volume, pltpu.HBM)
+    cells, *faces = prepare(volume, scalars)
     depth, lines, ends = (exchange(face, axis) for face, axis in zip(faces, AXES))
     depth, lines = (
         found if len(found) == 2 else found + [jnp.zeros_like(found[0])] for found in (depth, lines)
     )
     halos = (depth, lines, sum(ends[1:], ends[0]))
 
-    steps = tile_rows // tile
-
-    def march_groups(distances, after=None):
-        blocks = np.arange(per_group) * groups
-        places = jnp.stack([blocks + (position % groups ^ distance) for distance in distances])
-        ids = (places[..., None] * steps + np.arange(steps)).reshape(-1).astype(jnp.int32)
+    def march_call(call, after=None):
+        here = scalars
         if after is not None:
-            ids, _ = lax.optimization_barrier((ids, after))
-        return march(cells, halos, ids, odd, tables, knot_count, tile, len(distances))
-
-    side = [position >> bit & 1 for bit in range(bits)]
+            here, _ = lax.optimization_barrier((scalars, after))
+        start = first_id + count * sum(len(earlier) for earlier in calls[:call])
+        return march(
+            cells,
+            halos,
+            here,
+            start,
+            count * len(calls[call]),
+            len(calls[call]),
+            (tf_color, tf_opacity),
+            slices * view_count,
+            tile,
+        )
+
     if groups == 4:
-        (far,) = march_groups([3])
-        far_received = from_partner(far, "view", 0)
-        (near,) = march_groups([2], far)
-        sent = merged(near, far_received, side[0])
-        far, near = march_groups([1, 0], sent)
-        received = from_partner(sent, "view", 1)
-        image = merged(merged(near, from_partner(far, "view", 0), side[0]), received, side[1])
+        far = march_call(0)
+        received = from_partner(far, "view", 0)
+        near = march_call(1, far)
+        code = merge_pair(scalars, near, received, first_side)
+        code_received = from_partner(code, "view", 1)
+        near = march_call(2, code)
+        image = merge_last(scalars, near, received, code_received, first_side, bits == 2)
     elif groups == 2:
-        far, near = march_groups([1, 0])
-        image = merged(near, from_partner(far, "view", 0), side[0])
+        far = march_call(0)
+        received = from_partner(far, "view", 0)
+        image = merged(march_call(1, far)[0], received[0], position & 1)
     else:
-        (image,) = march_groups([0])
+        image = march_call(0)[0]
+    if bits == 2:
+        return image.reshape(4, 1, tile_rows, width)
     image = image.reshape((4,) + (2,) * (bits - group_bits) + (tile_rows, width))
     for bit in range(group_bits, bits):
+        side = position >> bit & 1
         axis = bits - bit
-        kept = lax.dynamic_index_in_dim(image, side[bit], axis, keepdims=False)
-        sent = lax.dynamic_index_in_dim(image, 1 - side[bit], axis, keepdims=False)
-        image = merged(kept, from_partner(sent, "view", bit), side[bit])
+        kept = lax.dynamic_index_in_dim(image, side, axis, keepdims=False)
+        sent = lax.dynamic_index_in_dim(image, 1 - side, axis, keepdims=False)
+        image = merged(kept, from_partner(sent, "view", bit), side)
     image = jnp.concatenate([image[:3], 1.0 - image[3:]], axis=0)
     return image.reshape(4, 1, tile_rows, width)
 

time: 60.5 us -> 41.1 us (0.68)
  waiting for transfers between devices: 16.4 us -> 4.97 us
  local copies, waits for them, and re-layouts: 8.47 us -> 0.09 us
  Pallas kernels: 23.6 us -> 25.8 us
  other arithmetic: 1.76 us -> 0.01 us
    ppermute x3 -> x2, waiting for transfers between devices: 13.7 us -> 3.27 us  [from_partner(): return lax.ppermute(value, axis, pairs)]
    unnamed x14 -> x8, local copies, waits for them, and re-layouts: 8.35 us -> 0.02 us
    pallas_call x4 -> x6, Pallas kernels: 23.6 us -> 25.8 us  [the longest x3 20.7 us: march(): pl.pallas_call(functools.partial(march_kernel, first_id=first_id, count=c...]
    ppermute x5, waiting for transfers between devices: 2.77 us -> 1.7 us  [exchange(): lax.ppermute(face, axis, both)]
    reshape x1 -> x0, other arithmetic: 0.83 us -> none  [on_device(): return image.reshape(4, 1, tile_rows, width)]
  transfers between devices with their start and end apart: 8 -> 7, of which waited for: 4 -> 2; matrix products, arithmetic and copies ran while one was open for 1% -> 0% of each run, Pallas kernels for 9% -> 26%
where the time goes in v4:
time: 41.1 us; the launch traced here: 40.5 us
  Pallas kernels  25.8 us (63%)
  starting transfers between devices  9.41 us (23%)
  waiting for transfers between devices  4.97 us (12%)
    pallas_call x3, Pallas kernels, march(): pl.pallas_call(functools.partial(march_kernel, first_id=first_id, count=c...  20.7 us
    ppermute x5, starting transfers between devices, exchange(): lax.ppermute(face, axis, both)  9.18 us
    ppermute x2, waiting for transfers between devices, from_partner(): return lax.ppermute(value, axis, pairs)  3.27 us
    pallas_call x1, Pallas kernels, prepare(): pl.pallas_call(prepare_kernel, in_specs=[pl.BlockSpec(memory_space=pltpu....  2.96 us
    ppermute x5, waiting for transfers between devices, exchange(): lax.ppermute(face, axis, both)  1.7 us
    pallas_call x1, Pallas kernels, merge_last(): pl.pallas_call(functools.partial(last_kernel, side=side, finish=finish),...  1.48 us
  transfers between devices with their start and end apart: 7, of which 2 were waited for; matrix products, arithmetic and copies ran while one was open for 0% of the time, Pallas kernels for 26%

profile of v4, /device:TPU:12, one launch (start us, length us, event | category | flops | bytes accessed | tf_op | source)
XLA Modules:
  0.0 40.5 jit_solution(11800074754656191317)
XLA Ops:
  0.0 0.0 copy-start.2
  0.1 0.1 concatenate.3.scalars_ref
  0.1 3.0 %shard_map.100 = (bf16[16,256,512]{2,1,0:T(8,128)(2,1)S(1)}, bf16[256,512]{1,0:T(8,128)(2,1)S(1)}, bf16[256,512]{1,0:T(8,128)(2,1)S(1)}, bf16[16,512]{1,0:T(8,12...) custom-call(s32[13]{0:T(128)S(1)} %concatenate.3.scalars_ref, bf16[16,256,512]{2,1,0:T(8,128)(2,1)} %volume_ref.1), custom_call_target="tpu_custom_call" | custom-call | tf_op jit(solution)/shard_map/pallas_call | solution.py:138
  3.1 0.1 collective-permute-start
  3.2 2.5 %collective-permute-start.1 = (bf16[256,512]{1,0:T(8,128)(2,1)S(1)}, bf16[256,512]{1,0:T(8,128)(2,1)S(1)}, u32[]{:S(2)}, u32[]{:S(2)}) collective-permute-start(bf16[256,512]{1,0:T(8,128)(2,1)S(1)} %get-tuple-element.15), channel_id=1, source_target_pairs={{8,16},{16,8},{9,17},{17,9},{10,18},{18,10},{11,19},{19,11},{12,20... | collective-permute-start | bytes 786440 | tf_op jit(solution)/shard_map/ppermute | solution.py:59
  5.7 1.6 %collective-permute-start.4 = (bf16[256,128]{1,0:T(8,128)(2,1)S(1)}, bf16[256,128]{1,0:T(8,128)(2,1)S(1)}, u32[]{:S(2)}, u32[]{:S(2)}) collective-permute-start(bf16[256,128]{1,0:T(8,128)(2,1)S(1)} %get-tuple-element.18), channel_id=1, source_target_pairs={{0,1},{1,0},{2,3},{3,2},{4,5},{5,4},{6,7},{7,6},{8,9},{9,8},{10,11... | collective-permute-start | bytes 196616 | tf_op jit(solution)/shard_map/ppermute | solution.py:59
  7.3 0.4 %collective-permute-start.2 = (bf16[16,512]{1,0:T(8,128)(2,1)S(1)}, bf16[16,512]{1,0:T(8,128)(2,1)S(1)}, u32[]{:S(2)}, u32[]{:S(2)}) collective-permute-start(bf16[16,512]{1,0:T(8,128)(2,1)S(1)} %get-tuple-element.16), channel_id=1, source_target_pairs={{0,2},{4,6},{2,0},{6,4},{1,3},{5,7},{3,1},{7,5},{8,10},{12,14},{10... | collective-permute-start | bytes 49160 | tf_op jit(solution)/shard_map/ppermute | solution.py:59
  7.7 4.6 %collective-permute-start.3 = (bf16[16,512]{1,0:T(8,128)(2,1)S(1)}, bf16[16,512]{1,0:T(8,128)(2,1)S(1)}, u32[]{:S(2)}, u32[]{:S(2)}) collective-permute-start(bf16[16,512]{1,0:T(8,128)(2,1)S(1)} %get-tuple-element.17), channel_id=1, source_target_pairs={{2,4},{4,2},{3,5},{5,3},{10,12},{12,10},{11,13},{13,11},{18,20},{2... | collective-permute-start | bytes 49160 | tf_op jit(solution)/shard_map/ppermute | solution.py:59
  12.3 0.0 collective-permute-done.2.line_refs_0_
  12.3 1.7 %collective-permute-done.3.line_refs_1_ = bf16[16,512]{1,0:T(8,128)(2,1)S(1)} collective-permute-done((bf16[16,512]{1,0:T(8,128)(2,1)S(1)}, bf16[16,512]{1,0:T(8,128)(2,1)S(1)}, u32[]{:S(2)}, u32[]{:S(2)}) %collective-permute-start.3) | collective-permute-done | bytes 16416 | tf_op jit(solution)/shard_map/ppermute | solution.py:59
  14.0 0.0 collective-permute-done.4.ends_ref
  14.0 0.0 collective-permute-done.depth_refs_0_
  14.0 0.0 collective-permute-done.1.depth_refs_1_
  14.0 0.0 copy-done
  14.0 0.0 copy-done.1
  14.1 10.0 %shard_map.101 = f32[2,4,64,512]{3,2,1,0:T(8,128)S(1)} custom-call(s32[13]{0:T(128)S(1)} %concatenate.3.scalars_ref, bf16[128,208]{1,0:T(8,128)(2,1)S(1)} %copy-done, f32[24,16]{1,0:T(8,128)S(1)} %copy-done.1, f32[3,16]{1,0:T(4,128)S(1)} %copy-done.2, f32[1,16]{1,0:T(1,128)S(1)} %bitcast.9, bf16[16,256,512]{2,1,0:T(8,128)(2,1)S(1)} %get-tuple-element.13.cells_ref, ...), custom_call_target="tpu_custom_call" | custom-call | tf_op jit(solution)/shard_map/pallas_call | solution.py:322
  24.1 0.1 collective-permute-start.5
  24.2 5.3 %shard_map.102.own_ref = f32[1,4,64,512]{3,2,1,0:T(8,128)S(1)} custom-call(s32[13]{0:T(128)S(1)} %concatenate.3.scalars_ref, bf16[128,208]{1,0:T(8,128)(2,1)S(1)} %copy-done, f32[24,16]{1,0:T(8,128)S(1)} %copy-done.1, f32[3,16]{1,0:T(4,128)S(1)} %copy-done.2, f32[1,16]{1,0:T(1,128)S(1)} %bitcast.10, bf16[16,256,512]{2,1,0:T(8,128)(2,1)S(1)} %get-tuple-element.13.cells_ref, ...), custom_call_target="tpu_custom_call" | custom-call | tf_op jit(solution)/shard_map/pallas_call | solution.py:322
  29.5 0.0 collective-permute-done.5.other_ref
  29.6 0.7 %shard_map.103 = bf16[4,64,512]{2,1,0:T(8,128)(2,1)S(1)} custom-call(s32[13]{0:T(128)S(1)} %concatenate.3.scalars_ref, f32[1,4,64,512]{3,2,1,0:T(8,128)S(1)} %shard_map.102.own_ref, f32[2,4,64,512]{3,2,1,0:T(8,128)S(1)} %collective-permute-done.5.other_ref), custom_call_target="tpu_custom_call" | custom-call | tf_op jit(solution)/shard_map/pallas_call | solution.py:380
  30.2 0.2 collective-permute-start.6
  30.4 5.3 %shard_map.104.own_ref = f32[1,4,64,512]{3,2,1,0:T(8,128)S(1)} custom-call(s32[13]{0:T(128)S(1)} %concatenate.3.scalars_ref, bf16[128,208]{1,0:T(8,128)(2,1)S(1)} %copy-done, f32[24,16]{1,0:T(8,128)S(1)} %copy-done.1, f32[3,16]{1,0:T(4,128)S(1)} %copy-done.2, f32[1,16]{1,0:T(1,128)S(1)} %bitcast.11, bf16[16,256,512]{2,1,0:T(8,128)(2,1)S(1)} %get-tuple-element.13.cells_ref, ...), custom_call_target="tpu_custom_call" | custom-call | tf_op jit(solution)/shard_map/pallas_call | solution.py:322
  35.7 3.3 %collective-permute-done.6.code_ref = bf16[4,64,512]{2,1,0:T(8,128)(2,1)S(1)} collective-permute-done((bf16[4,64,512]{2,1,0:T(8,128)(2,1)S(1)}, bf16[4,64,512]{2,1,0:T(8,128)(2,1)S(1)}, u32[]{:S(2)}, u32[]{:S(2)}) %collective-permute-start.6) | collective-permute-done | bytes 262176 | tf_op jit(solution)/shard_map/ppermute | solution.py:415
  39.0 1.5 %shard_map.105 = f32[4,64,512]{2,1,0:T(8,128)} custom-call(s32[13]{0:T(128)S(1)} %concatenate.3.scalars_ref, f32[1,4,64,512]{3,2,1,0:T(8,128)S(1)} %shard_map.104.own_ref, f32[2,4,64,512]{3,2,1,0:T(8,128)S(1)} %collective-permute-done.5.other_ref, bf16[4,64,512]{2,1,0:T(8,128)(2,1)S(1)} %collective-permute-done.6.code_ref), custom_call_target="tpu_custom_call" | custom-call | tf_op jit(solution)/shard_map/pallas_call | solution.py:392
  (7 shorter events, 0.0 us)
Async XLA Ops:
  0.0 14.0 %copy-start = (bf16[128,208]{1,0:T(8,128)(2,1)S(1)}, bf16[128,208]{1,0:T(8,128)(2,1)}, u32[]{:S(2)}) copy-start(bf16[128,208]{1,0:T(8,128)(2,1)} %constant.25.clone.stencil_ref) | copy-start | bytes 159748
  0.0 14.0 %copy-start.1 = (f32[24,16]{1,0:T(8,128)S(1)}, f32[24,16]{1,0:T(8,128)}, u32[]{:S(2)}) copy-start(f32[24,16]{1,0:T(8,128)} %constant.26.clone.lines_ref) | copy-start | bytes 4612
  0.0 14.0 %copy-start.3 = (f32[16]{0:T(128)S(1)}, f32[16]{0:T(128)}, u32[]{:S(2)}) copy-start(f32[16]{0:T(128)} %param.12) | copy-start | bytes 196
  0.0 14.1 %copy-start.2 = (f32[3,16]{1,0:T(4,128)S(1)}, f32[3,16]{1,0:T(4,128)}, u32[]{:S(2)}) copy-start(f32[3,16]{1,0:T(4,128)} %color_ref.5) | copy-start | bytes 580
  3.1 10.9 %collective-permute-start = (bf16[256,512]{1,0:T(8,128)(2,1)S(1)}, bf16[256,512]{1,0:T(8,128)(2,1)S(1)}, u32[]{:S(2)}, u32[]{:S(2)}) collective-permute-start(bf16[256,512]{1,0:T(8,128)(2,1)S(1)} %get-tuple-element.14), channel_id=1, source_target_pairs={{0,8},{16,24},{8,0},{24,16},{1,9},{17,25},{9,1},{25,17},{2,10},{18... | collective-permute-start | bytes 786440 | tf_op jit(solution)/shard_map/ppermute | solution.py:59
  3.2 10.8 %collective-permute-start.1 = (bf16[256,512]{1,0:T(8,128)(2,1)S(1)}, bf16[256,512]{1,0:T(8,128)(2,1)S(1)}, u32[]{:S(2)}, u32[]{:S(2)}) collective-permute-start(bf16[256,512]{1,0:T(8,128)(2,1)S(1)} %get-tuple-element.15), channel_id=1, source_target_pairs={{8,16},{16,8},{9,17},{17,9},{10,18},{18,10},{11,19},{19,11},{12,20... | collective-permute-start | bytes 786440 | tf_op jit(solution)/shard_map/ppermute | solution.py:59
  5.7 8.3 %collective-permute-start.4 = (bf16[256,128]{1,0:T(8,128)(2,1)S(1)}, bf16[256,128]{1,0:T(8,128)(2,1)S(1)}, u32[]{:S(2)}, u32[]{:S(2)}) collective-permute-start(bf16[256,128]{1,0:T(8,128)(2,1)S(1)} %get-tuple-element.18), channel_id=1, source_target_pairs={{0,1},{1,0},{2,3},{3,2},{4,5},{5,4},{6,7},{7,6},{8,9},{9,8},{10,11... | collective-permute-start | bytes 196616 | tf_op jit(solution)/shard_map/ppermute | solution.py:59
  7.3 5.1 %collective-permute-start.2 = (bf16[16,512]{1,0:T(8,128)(2,1)S(1)}, bf16[16,512]{1,0:T(8,128)(2,1)S(1)}, u32[]{:S(2)}, u32[]{:S(2)}) collective-permute-start(bf16[16,512]{1,0:T(8,128)(2,1)S(1)} %get-tuple-element.16), channel_id=1, source_target_pairs={{0,2},{4,6},{2,0},{6,4},{1,3},{5,7},{3,1},{7,5},{8,10},{12,14},{10... | collective-permute-start | bytes 49160 | tf_op jit(solution)/shard_map/ppermute | solution.py:59
  7.7 6.3 %collective-permute-start.3 = (bf16[16,512]{1,0:T(8,128)(2,1)S(1)}, bf16[16,512]{1,0:T(8,128)(2,1)S(1)}, u32[]{:S(2)}, u32[]{:S(2)}) collective-permute-start(bf16[16,512]{1,0:T(8,128)(2,1)S(1)} %get-tuple-element.17), channel_id=1, source_target_pairs={{2,4},{4,2},{3,5},{5,3},{10,12},{12,10},{11,13},{13,11},{18,20},{2... | collective-permute-start | bytes 49160 | tf_op jit(solution)/shard_map/ppermute | solution.py:59
  24.1 5.4 %collective-permute-start.5 = (f32[2,4,64,512]{3,2,1,0:T(8,128)S(1)}, f32[2,4,64,512]{3,2,1,0:T(8,128)S(1)}, u32[]{:S(2)}, u32[]{:S(2)}) collective-permute-start(f32[2,4,64,512]{3,2,1,0:T(8,128)S(1)} %shard_map.101), channel_id=1, source_target_pairs={{0,8},{8,0},{16,24},{24,16},{1,9},{9,1},{17,25},{25,17},{2,10},{10... | collective-permute-start | bytes 3145736 | tf_op jit(solution)/shard_map/ppermute | solution.py:415
  30.2 8.8 %collective-permute-start.6 = (bf16[4,64,512]{2,1,0:T(8,128)(2,1)S(1)}, bf16[4,64,512]{2,1,0:T(8,128)(2,1)S(1)}, u32[]{:S(2)}, u32[]{:S(2)}) collective-permute-start(bf16[4,64,512]{2,1,0:T(8,128)(2,1)S(1)} %shard_map.103), channel_id=1, source_target_pairs={{0,16},{8,24},{16,0},{24,8},{1,17},{9,25},{17,1},{25,9},{2,18},{10... | collective-permute-start | bytes 786440 | tf_op jit(solution)/shard_map/ppermute | solution.py:415

commit v5 on v4

--- a/solution.py
+++ b/solution.py
@@ -1,4 +1,5 @@
 import functools
+import itertools
 
 import jax
 import jax.numpy as jnp
@@ -22,6 +23,13 @@
 SLOTS = 4
 CODE_SCALE = 240.0
 CODE_SHIFT = 120.0
+ALONG_SUBLANES = lax.GatherDimensionNumbers(
+    offset_dims=(),
+    collapsed_slice_dims=(0,),
+    start_index_map=(0,),
+    operand_batching_dims=(1,),
+    start_indices_batching_dims=(1,),
+)
 SCALARS = pl.BlockSpec(memory_space=pltpu.SMEM)
 VECTORS = pl.BlockSpec(memory_space=pltpu.VMEM)
 
@@ -182,8 +190,12 @@
 
     def look_up(which, index, in_half):
         for half in range(halves):
-            found = jnp.take_along_axis(
-                tables[which * halves + half], index, axis=0, mode="promise_in_bounds"
+            found = lax.gather(
+                tables[which * halves + half],
+                index[..., None],
+                ALONG_SUBLANES,
+                slice_sizes=(1, 1),
+                mode=lax.GatherScatterMode.PROMISE_IN_BOUNDS,
             )
             value = found if half == 0 else jnp.where(in_half[half - 1], found, value)
         return value
@@ -221,101 +233,100 @@
         weight = (state[3] - through) * shading
         return [total + value * weight for total, value in zip(state, values[:3])] + [through]
 
-    def one_tile(i, carry):
-        place = scalars_ref[first_id + i]
-        start = pl.multiple_of(place * tile, tile)
-        steps = count // out_ref.shape[0]
+    odd = [scalars_ref[axis] == 1 for axis in range(2)]
+    for side in range(2):
+        lines = jnp.where(odd[1], line_refs[side][...], line_refs[1 - side][...])
+        for z in range(slices):
+            sides_ref[side, z] = jnp.broadcast_to(lines[z : z + 1], (PACK, width))
+
+    def gradients(i, z):
+        start = pl.multiple_of(scalars_ref[first_id + i] * tile, tile)
+        rows = pl.ds(start, tile)
+
+        def across(side):
+            return jnp.where(
+                odd[0], depth_refs[side][rows, :], depth_refs[1 - side][rows, :]
+            )
+
+        def beside(side, at_face, near):
+            near = pl.ds(pl.multiple_of(near, PACK), PACK)
+            return jnp.where(at_face, sides_ref[side, z], cells_ref[z, near, :])
+
+        cells = cells_ref[z, rows, :]
+        before = cells_ref[z - 1, rows, :] if z > 0 else across(0)
+        after = cells_ref[z + 1, rows, :] if z + 1 < slices else across(1)
+        above = beside(0, start == 0, jnp.maximum(start - PACK, 0))
+        below = beside(1, start == height - tile, jnp.minimum(start + tile, height - PACK))
+        right = pltpu.roll(cells, width - 1, 1)
+        left = pltpu.roll(cells, 1, 1)
+        ends = ends_ref[rows, :]
+        ends = pltpu.roll(ends, LANES - 2 * z, 1) if z else ends
+        right_end = jnp.where(lane == LANES - 1, ends, right[:, rest:])
+        left_end = jnp.where(lane == 0, ends, left[:, :LANES])
+        if rest:
+            right_end = jnp.concatenate([right[:, :rest], right_end], axis=1)
+            left_end = jnp.concatenate([left_end, left[:, LANES:]], axis=1)
+        stacked = jnp.concatenate(
+            [after, before, above, cells, below, right_end, left_end, ones], axis=0
+        )
+        for column in range(0, width, half_width):
+            parts_ref[z % SLOTS, :, pl.ds(column, half_width)] = jnp.dot(
+                stencil_ref[...],
+                stacked[:, column : column + half_width],
+                preferred_element_type=jnp.float32,
+            )
+            yield
+
+    def shades(i, first):
         group = i // steps
         target = pl.multiple_of((i - group * steps) * tile, tile)
-        rows = pl.ds(start, tile)
-        odd = [scalars_ref[axis] == 1 for axis in range(2)]
-        behind, ahead = (
-            jnp.where(odd[0], depth_refs[a][rows, :], depth_refs[1 - a][rows, :]) for a in range(2)
-        )
-        for side, at_face, neighbour in (
-            (0, place == 0, pl.ds(jnp.maximum(start - PACK, 0), PACK)),
-            (1, start == height - tile, pl.ds(jnp.minimum(start + tile, height - PACK), PACK)),
-        ):
-
-            @pl.when(at_face)
-            def _():
-                lines = jnp.where(odd[1], line_refs[side][...], line_refs[1 - side][...])
-                for z in range(slices):
-                    sides_ref[side, z] = jnp.broadcast_to(lines[z : z + 1], (PACK, width))
-
-            @pl.when(jnp.logical_not(at_face))
-            def _():
-                near = pl.ds(pl.multiple_of(neighbour.start, PACK), PACK)
-                for z in range(slices):
-                    sides_ref[side, z] = cells_ref[z, near, :]
-
-        def gradients(z):
-            cells = cells_ref[z, rows, :]
-            before = cells_ref[z - 1, rows, :] if z > 0 else behind
-            after = cells_ref[z + 1, rows, :] if z + 1 < slices else ahead
-            right = pltpu.roll(cells, width - 1, 1)
-            left = pltpu.roll(cells, 1, 1)
-            ends = ends_ref[rows, :]
-            ends = pltpu.roll(ends, LANES - 2 * z, 1) if z else ends
-            right_end = jnp.where(lane == LANES - 1, ends, right[:, rest:])
-            left_end = jnp.where(lane == 0, ends, left[:, :LANES])
-            if rest:
-                right_end = jnp.concatenate([right[:, :rest], right_end], axis=1)
-                left_end = jnp.concatenate([left_end, left[:, LANES:]], axis=1)
-            stacked = jnp.concatenate(
-                [after, before, sides_ref[0, z], cells, sides_ref[1, z], right_end, left_end, ones],
-                axis=0,
-            )
-            for column in range(0, width, half_width):
-                parts_ref[z % SLOTS, :, pl.ds(column, half_width)] = jnp.dot(
-                    stencil_ref[...],
-                    stacked[:, column : column + half_width],
-                    preferred_element_type=jnp.float32,
-                )
+        for column in range(0, width, LANES):
+            for row in range(0, tile, HALF):
+                here = (pl.ds(target + row, HALF), pl.ds(column, LANES))
+                state = None if first == 0 else [out_ref[(group, c) + here] for c in range(4)]
+                for z in range(first, first + DEPTH):
+                    state = shade(z, z % SLOTS, row, column, state)
+                for c in range(4):
+                    out_ref[(group, c) + here] = state[c]
                 yield
 
-        def shades(first):
-            for column in range(0, width, LANES):
-                for row in range(0, tile, HALF):
-                    here = (pl.ds(target + row, HALF), pl.ds(column, LANES))
-                    state = None if first == 0 else [out_ref[(group, c) + here] for c in range(4)]
-                    for z in range(first, first + DEPTH):
-                        state = shade(z, z % SLOTS, row, column, state)
-                    for c in range(4):
-                        out_ref[(group, c) + here] = state[c]
-                    yield
-
-        def later(first):
-            for z in range(first, min(first + DEPTH, slices)):
-                yield from gradients(z)
-
-        for _ in later(0):
+    def one_tile(i, carry):
+        following = jnp.minimum(i + 1, count - 1)
+        for z in range(0, slices, DEPTH):
+            ahead = [
+                gradients(i if later < slices else following, later % slices)
+                for later in range(z + DEPTH, z + 2 * DEPTH)
+            ]
+            interleave(
+                itertools.chain(*ahead),
+                DEPTH * (width // half_width),
+                shades(i, z),
+                (tile // HALF) * (width // LANES),
+            )
+        return carry
+
+    steps = count // out_ref.shape[0]
+    for z in range(DEPTH):
+        for _ in gradients(0, z):
             pass
-        for z in range(0, slices, DEPTH):
-            work = list_steps(later(z + DEPTH), DEPTH * (width // half_width), shades(z), (tile // HALF) * (width // LANES))
-            for _ in work:
-                pass
-        return carry
-
     lax.fori_loop(0, count, one_tile, 0)
 
 
-def list_steps(first, first_count, second, second_count):
+def interleave(first, first_count, second, second_count):
     done = 0
     for step in range(second_count):
         while done * second_count <= step * first_count and done < first_count:
             next(first, None)
             done += 1
         next(second)
-        yield
-    for _ in first:
+    for _ in itertools.chain(first, second):
         pass
 
 
 def march(cells, halos, scalars, first_id, count, groups, transfer, depth_total, tile):
     slices, height, width = cells.shape
     depth, lines, ends = halos
-    assert slices % DEPTH == 0
+    assert slices % SLOTS == 0 and SLOTS == 2 * DEPTH
     tf_color, tf_opacity = transfer
     knot_count = tf_color.shape[1]
     optical = float(-2.0 / depth_total * NORM**2 * np.log2(np.e))

time: 41.1 us -> 41 us (level)
  transfers between devices with their start and end apart: 7 -> 7, of which waited for: 2 -> 2; matrix products, arithmetic and copies ran while one was open for 0% -> 0% of each run, Pallas kernels for 26% -> 27%
where the time goes in v5:
time: 41 us; the launch traced here: 40.4 us
  Pallas kernels  25.8 us (63%)
  starting transfers between devices  9.42 us (23%)
  waiting for transfers between devices  4.92 us (12%)
    pallas_call x3, Pallas kernels, march(): pl.pallas_call(functools.partial(march_kernel, first_id=first_id, count=c...  20.7 us
    ppermute x5, starting transfers between devices, exchange(): lax.ppermute(face, axis, both)  9.18 us
    ppermute x2, waiting for transfers between devices, from_partner(): return lax.ppermute(value, axis, pairs)  3.22 us
    pallas_call x1, Pallas kernels, prepare(): pl.pallas_call(prepare_kernel, in_specs=[pl.BlockSpec(memory_space=pltpu....  2.96 us
    ppermute x5, waiting for transfers between devices, exchange(): lax.ppermute(face, axis, both)  1.7 us
    pallas_call x1, Pallas kernels, merge_last(): pl.pallas_call(functools.partial(last_kernel, side=side, finish=finish),...  1.48 us
  transfers between devices with their start and end apart: 7, of which 2 were waited for; matrix products, arithmetic and copies ran while one was open for 0% of the time, Pallas kernels for 27%

profile of v5, /device:TPU:12, one launch (start us, length us, event | category | flops | bytes accessed | tf_op | source)
XLA Modules:
  0.0 40.4 jit_solution(13967572582056013862)
XLA Ops:
  0.0 0.0 copy-start.2
  0.1 0.1 concatenate.3.scalars_ref
  0.1 3.0 %shard_map.100 = (bf16[16,256,512]{2,1,0:T(8,128)(2,1)S(1)}, bf16[256,512]{1,0:T(8,128)(2,1)S(1)}, bf16[256,512]{1,0:T(8,128)(2,1)S(1)}, bf16[16,512]{1,0:T(8,12...) custom-call(s32[13]{0:T(128)S(1)} %concatenate.3.scalars_ref, bf16[16,256,512]{2,1,0:T(8,128)(2,1)} %volume_ref.1), custom_call_target="tpu_custom_call" | custom-call | tf_op jit(solution)/shard_map/pallas_call | solution.py:146
  3.1 0.1 collective-permute-start
  3.2 2.5 %collective-permute-start.1 = (bf16[256,512]{1,0:T(8,128)(2,1)S(1)}, bf16[256,512]{1,0:T(8,128)(2,1)S(1)}, u32[]{:S(2)}, u32[]{:S(2)}) collective-permute-start(bf16[256,512]{1,0:T(8,128)(2,1)S(1)} %get-tuple-element.15), channel_id=1, source_target_pairs={{8,16},{16,8},{9,17},{17,9},{10,18},{18,10},{11,19},{19,11},{12,20... | collective-permute-start | bytes 786440 | tf_op jit(solution)/shard_map/ppermute | solution.py:67
  5.7 1.6 %collective-permute-start.4 = (bf16[256,128]{1,0:T(8,128)(2,1)S(1)}, bf16[256,128]{1,0:T(8,128)(2,1)S(1)}, u32[]{:S(2)}, u32[]{:S(2)}) collective-permute-start(bf16[256,128]{1,0:T(8,128)(2,1)S(1)} %get-tuple-element.18), channel_id=1, source_target_pairs={{0,1},{1,0},{2,3},{3,2},{4,5},{5,4},{6,7},{7,6},{8,9},{9,8},{10,11... | collective-permute-start | bytes 196616 | tf_op jit(solution)/shard_map/ppermute | solution.py:67
  7.3 0.4 %collective-permute-start.2 = (bf16[16,512]{1,0:T(8,128)(2,1)S(1)}, bf16[16,512]{1,0:T(8,128)(2,1)S(1)}, u32[]{:S(2)}, u32[]{:S(2)}) collective-permute-start(bf16[16,512]{1,0:T(8,128)(2,1)S(1)} %get-tuple-element.16), channel_id=1, source_target_pairs={{0,2},{4,6},{2,0},{6,4},{1,3},{5,7},{3,1},{7,5},{8,10},{12,14},{10... | collective-permute-start | bytes 49160 | tf_op jit(solution)/shard_map/ppermute | solution.py:67
  7.7 4.6 %collective-permute-start.3 = (bf16[16,512]{1,0:T(8,128)(2,1)S(1)}, bf16[16,512]{1,0:T(8,128)(2,1)S(1)}, u32[]{:S(2)}, u32[]{:S(2)}) collective-permute-start(bf16[16,512]{1,0:T(8,128)(2,1)S(1)} %get-tuple-element.17), channel_id=1, source_target_pairs={{2,4},{4,2},{3,5},{5,3},{10,12},{12,10},{11,13},{13,11},{18,20},{2... | collective-permute-start | bytes 49160 | tf_op jit(solution)/shard_map/ppermute | solution.py:67
  12.3 0.0 collective-permute-done.2.line_refs_0_
  12.3 1.7 %collective-permute-done.3.line_refs_1_ = bf16[16,512]{1,0:T(8,128)(2,1)S(1)} collective-permute-done((bf16[16,512]{1,0:T(8,128)(2,1)S(1)}, bf16[16,512]{1,0:T(8,128)(2,1)S(1)}, u32[]{:S(2)}, u32[]{:S(2)}) %collective-permute-start.3) | collective-permute-done | bytes 16416 | tf_op jit(solution)/shard_map/ppermute | solution.py:67
  14.0 0.0 collective-permute-done.4.ends_ref
  14.0 0.0 collective-permute-done.depth_refs_0_
  14.0 0.0 collective-permute-done.1.depth_refs_1_
  14.0 0.0 copy-done
  14.0 0.0 copy-done.1
  14.1 9.9 %shard_map.101 = f32[2,4,64,512]{3,2,1,0:T(8,128)S(1)} custom-call(s32[13]{0:T(128)S(1)} %concatenate.3.scalars_ref, bf16[128,208]{1,0:T(8,128)(2,1)S(1)} %copy-done, f32[24,16]{1,0:T(8,128)S(1)} %copy-done.1, f32[3,16]{1,0:T(4,128)S(1)} %copy-done.2, f32[1,16]{1,0:T(1,128)S(1)} %bitcast.9, bf16[16,256,512]{2,1,0:T(8,128)(2,1)S(1)} %get-tuple-element.13.cells_ref, ...), custom_call_target="tpu_custom_call" | custom-call | tf_op jit(solution)/shard_map/pallas_call | solution.py:333
  24.0 0.1 collective-permute-start.5
  24.1 5.4 %shard_map.102.own_ref = f32[1,4,64,512]{3,2,1,0:T(8,128)S(1)} custom-call(s32[13]{0:T(128)S(1)} %concatenate.3.scalars_ref, bf16[128,208]{1,0:T(8,128)(2,1)S(1)} %copy-done, f32[24,16]{1,0:T(8,128)S(1)} %copy-done.1, f32[3,16]{1,0:T(4,128)S(1)} %copy-done.2, f32[1,16]{1,0:T(1,128)S(1)} %bitcast.10, bf16[16,256,512]{2,1,0:T(8,128)(2,1)S(1)} %get-tuple-element.13.cells_ref, ...), custom_call_target="tpu_custom_call" | custom-call | tf_op jit(solution)/shard_map/pallas_call | solution.py:333
  29.5 0.0 collective-permute-done.5.other_ref
  29.5 0.7 %shard_map.103 = bf16[4,64,512]{2,1,0:T(8,128)(2,1)S(1)} custom-call(s32[13]{0:T(128)S(1)} %concatenate.3.scalars_ref, f32[1,4,64,512]{3,2,1,0:T(8,128)S(1)} %shard_map.102.own_ref, f32[2,4,64,512]{3,2,1,0:T(8,128)S(1)} %collective-permute-done.5.other_ref), custom_call_target="tpu_custom_call" | custom-call | tf_op jit(solution)/shard_map/pallas_call | solution.py:391
  30.2 0.2 collective-permute-start.6
  30.3 5.4 %shard_map.104.own_ref = f32[1,4,64,512]{3,2,1,0:T(8,128)S(1)} custom-call(s32[13]{0:T(128)S(1)} %concatenate.3.scalars_ref, bf16[128,208]{1,0:T(8,128)(2,1)S(1)} %copy-done, f32[24,16]{1,0:T(8,128)S(1)} %copy-done.1, f32[3,16]{1,0:T(4,128)S(1)} %copy-done.2, f32[1,16]{1,0:T(1,128)S(1)} %bitcast.11, bf16[16,256,512]{2,1,0:T(8,128)(2,1)S(1)} %get-tuple-element.13.cells_ref, ...), custom_call_target="tpu_custom_call" | custom-call | tf_op jit(solution)/shard_map/pallas_call | solution.py:333
  35.7 3.2 %collective-permute-done.6.code_ref = bf16[4,64,512]{2,1,0:T(8,128)(2,1)S(1)} collective-permute-done((bf16[4,64,512]{2,1,0:T(8,128)(2,1)S(1)}, bf16[4,64,512]{2,1,0:T(8,128)(2,1)S(1)}, u32[]{:S(2)}, u32[]{:S(2)}) %collective-permute-start.6) | collective-permute-done | bytes 262176 | tf_op jit(solution)/shard_map/ppermute | solution.py:426
  38.9 1.5 %shard_map.105 = f32[4,64,512]{2,1,0:T(8,128)} custom-call(s32[13]{0:T(128)S(1)} %concatenate.3.scalars_ref, f32[1,4,64,512]{3,2,1,0:T(8,128)S(1)} %shard_map.104.own_ref, f32[2,4,64,512]{3,2,1,0:T(8,128)S(1)} %collective-permute-done.5.other_ref, bf16[4,64,512]{2,1,0:T(8,128)(2,1)S(1)} %collective-permute-done.6.code_ref), custom_call_target="tpu_custom_call" | custom-call | tf_op jit(solution)/shard_map/pallas_call | solution.py:403
  (7 shorter events, 0.0 us)
Async XLA Ops:
  0.0 14.0 %copy-start = (bf16[128,208]{1,0:T(8,128)(2,1)S(1)}, bf16[128,208]{1,0:T(8,128)(2,1)}, u32[]{:S(2)}) copy-start(bf16[128,208]{1,0:T(8,128)(2,1)} %constant.25.clone.stencil_ref) | copy-start | bytes 159748
  0.0 14.0 %copy-start.1 = (f32[24,16]{1,0:T(8,128)S(1)}, f32[24,16]{1,0:T(8,128)}, u32[]{:S(2)}) copy-start(f32[24,16]{1,0:T(8,128)} %constant.26.clone.lines_ref) | copy-start | bytes 4612
  0.0 14.0 %copy-start.3 = (f32[16]{0:T(128)S(1)}, f32[16]{0:T(128)}, u32[]{:S(2)}) copy-start(f32[16]{0:T(128)} %param.12) | copy-start | bytes 196
  0.0 14.1 %copy-start.2 = (f32[3,16]{1,0:T(4,128)S(1)}, f32[3,16]{1,0:T(4,128)}, u32[]{:S(2)}) copy-start(f32[3,16]{1,0:T(4,128)} %color_ref.5) | copy-start | bytes 580
  3.1 10.9 %collective-permute-start = (bf16[256,512]{1,0:T(8,128)(2,1)S(1)}, bf16[256,512]{1,0:T(8,128)(2,1)S(1)}, u32[]{:S(2)}, u32[]{:S(2)}) collective-permute-start(bf16[256,512]{1,0:T(8,128)(2,1)S(1)} %get-tuple-element.14), channel_id=1, source_target_pairs={{0,8},{16,24},{8,0},{24,16},{1,9},{17,25},{9,1},{25,17},{2,10},{18... | collective-permute-start | bytes 786440 | tf_op jit(solution)/shard_map/ppermute | solution.py:67
  3.2 10.8 %collective-permute-start.1 = (bf16[256,512]{1,0:T(8,128)(2,1)S(1)}, bf16[256,512]{1,0:T(8,128)(2,1)S(1)}, u32[]{:S(2)}, u32[]{:S(2)}) collective-permute-start(bf16[256,512]{1,0:T(8,128)(2,1)S(1)} %get-tuple-element.15), channel_id=1, source_target_pairs={{8,16},{16,8},{9,17},{17,9},{10,18},{18,10},{11,19},{19,11},{12,20... | collective-permute-start | bytes 786440 | tf_op jit(solution)/shard_map/ppermute | solution.py:67
  5.7 8.3 %collective-permute-start.4 = (bf16[256,128]{1,0:T(8,128)(2,1)S(1)}, bf16[256,128]{1,0:T(8,128)(2,1)S(1)}, u32[]{:S(2)}, u32[]{:S(2)}) collective-permute-start(bf16[256,128]{1,0:T(8,128)(2,1)S(1)} %get-tuple-element.18), channel_id=1, source_target_pairs={{0,1},{1,0},{2,3},{3,2},{4,5},{5,4},{6,7},{7,6},{8,9},{9,8},{10,11... | collective-permute-start | bytes 196616 | tf_op jit(solution)/shard_map/ppermute | solution.py:67
  7.3 5.1 %collective-permute-start.2 = (bf16[16,512]{1,0:T(8,128)(2,1)S(1)}, bf16[16,512]{1,0:T(8,128)(2,1)S(1)}, u32[]{:S(2)}, u32[]{:S(2)}) collective-permute-start(bf16[16,512]{1,0:T(8,128)(2,1)S(1)} %get-tuple-element.16), channel_id=1, source_target_pairs={{0,2},{4,6},{2,0},{6,4},{1,3},{5,7},{3,1},{7,5},{8,10},{12,14},{10... | collective-permute-start | bytes 49160 | tf_op jit(solution)/shard_map/ppermute | solution.py:67
  7.7 6.3 %collective-permute-start.3 = (bf16[16,512]{1,0:T(8,128)(2,1)S(1)}, bf16[16,512]{1,0:T(8,128)(2,1)S(1)}, u32[]{:S(2)}, u32[]{:S(2)}) collective-permute-start(bf16[16,512]{1,0:T(8,128)(2,1)S(1)} %get-tuple-element.17), channel_id=1, source_target_pairs={{2,4},{4,2},{3,5},{5,3},{10,12},{12,10},{11,13},{13,11},{18,20},{2... | collective-permute-start | bytes 49160 | tf_op jit(solution)/shard_map/ppermute | solution.py:67
  24.0 5.5 %collective-permute-start.5 = (f32[2,4,64,512]{3,2,1,0:T(8,128)S(1)}, f32[2,4,64,512]{3,2,1,0:T(8,128)S(1)}, u32[]{:S(2)}, u32[]{:S(2)}) collective-permute-start(f32[2,4,64,512]{3,2,1,0:T(8,128)S(1)} %shard_map.101), channel_id=1, source_target_pairs={{0,8},{8,0},{16,24},{24,16},{1,9},{9,1},{17,25},{25,17},{2,10},{10... | collective-permute-start | bytes 3145736 | tf_op jit(solution)/shard_map/ppermute | solution.py:426
  30.2 8.8 %collective-permute-start.6 = (bf16[4,64,512]{2,1,0:T(8,128)(2,1)S(1)}, bf16[4,64,512]{2,1,0:T(8,128)(2,1)S(1)}, u32[]{:S(2)}, u32[]{:S(2)}) collective-permute-start(bf16[4,64,512]{2,1,0:T(8,128)(2,1)S(1)} %shard_map.103), channel_id=1, source_target_pairs={{0,16},{8,24},{16,0},{24,8},{1,17},{9,25},{17,1},{25,9},{2,18},{10... | collective-permute-start | bytes 786440 | tf_op jit(solution)/shard_map/ppermute | solution.py:426

commit v6 on v5

--- a/solution.py
+++ b/solution.py
@@ -32,6 +32,7 @@
 )
 SCALARS = pl.BlockSpec(memory_space=pltpu.SMEM)
 VECTORS = pl.BlockSpec(memory_space=pltpu.VMEM)
+ANYWHERE = pl.BlockSpec(memory_space=pl.ANY)
 
 
 def stencil(tile, knot_count):
@@ -153,25 +154,18 @@
     )(scalars, volume)
 
 
-def march_kernel(
-    scalars_ref,
-    stencil_ref,
-    lines_ref,
-    color_ref,
-    opacity_ref,
-    cells_ref,
-    depth_refs,
-    line_refs,
-    ends_ref,
-    out_ref,
-    parts_ref,
-    sides_ref,
-    *,
-    first_id,
-    count,
-    tile,
-    optical,
-):
+def march_kernel(*refs, first_id, count, tile, optical, with_lines, patch):
+    scalars_ref, stencil_ref, lines_ref, color_ref, opacity_ref, cells_ref = refs[:6]
+    depth_refs, ends_ref, refs = refs[6:8], refs[8], refs[9:]
+    if with_lines:
+        line_refs, refs = refs[:2], refs[2:]
+    if patch:
+        _, whole_ref, image_ref, parts_ref, sides_ref, copied = refs
+    elif with_lines:
+        image_ref, parts_ref, sides_ref = refs
+    else:
+        image_ref, parts_ref = refs
+    per_group = image_ref.shape[2] // tile
     slices, height, width = cells_ref.shape
     lane = lax.broadcasted_iota(jnp.int16, (tile, LANES), 1)
     ones = jnp.ones((PACK, width), cells_ref.dtype)
@@ -234,10 +228,14 @@
         return [total + value * weight for total, value in zip(state, values[:3])] + [through]
 
     odd = [scalars_ref[axis] == 1 for axis in range(2)]
-    for side in range(2):
-        lines = jnp.where(odd[1], line_refs[side][...], line_refs[1 - side][...])
-        for z in range(slices):
-            sides_ref[side, z] = jnp.broadcast_to(lines[z : z + 1], (PACK, width))
+    if with_lines:
+        for side in range(2):
+            lines = jnp.where(odd[1], line_refs[side][...], line_refs[1 - side][...])
+            for z in range(slices):
+                sides_ref[side, z] = jnp.broadcast_to(lines[z : z + 1], (PACK, width))
+
+    def place(i):
+        return scalars_ref[first_id + count + i]
 
     def gradients(i, z):
         start = pl.multiple_of(scalars_ref[first_id + i] * tile, tile)
@@ -249,8 +247,8 @@
             )
 
         def beside(side, at_face, near):
-            near = pl.ds(pl.multiple_of(near, PACK), PACK)
-            return jnp.where(at_face, sides_ref[side, z], cells_ref[z, near, :])
+            inner = cells_ref[z, pl.ds(pl.multiple_of(near, PACK), PACK), :]
+            return jnp.where(at_face, sides_ref[side, z], inner) if with_lines else inner
 
         cells = cells_ref[z, rows, :]
         before = cells_ref[z - 1, rows, :] if z > 0 else across(0)
@@ -278,16 +276,16 @@
             yield
 
     def shades(i, first):
-        group = i // steps
-        target = pl.multiple_of((i - group * steps) * tile, tile)
+        group = 0 if patch else place(i) // per_group
+        target = 0 if patch else pl.multiple_of((place(i) - group * per_group) * tile, tile)
         for column in range(0, width, LANES):
             for row in range(0, tile, HALF):
                 here = (pl.ds(target + row, HALF), pl.ds(column, LANES))
-                state = None if first == 0 else [out_ref[(group, c) + here] for c in range(4)]
+                state = None if first == 0 else [image_ref[(group, c) + here] for c in range(4)]
                 for z in range(first, first + DEPTH):
                     state = shade(z, z % SLOTS, row, column, state)
                 for c in range(4):
-                    out_ref[(group, c) + here] = state[c]
+                    image_ref[(group, c) + here] = state[c]
                 yield
 
     def one_tile(i, carry):
@@ -305,11 +303,18 @@
             )
         return carry
 
-    steps = count // out_ref.shape[0]
     for z in range(DEPTH):
         for _ in gradients(0, z):
             pass
     lax.fori_loop(0, count, one_tile, 0)
+    if patch:
+        group = place(0) // (whole_ref.shape[2] // tile)
+        rows = (place(0) - group * (whole_ref.shape[2] // tile)) * tile
+        copy = pltpu.make_async_copy(
+            image_ref.at[0], whole_ref.at[group, :, pl.ds(pl.multiple_of(rows, tile), tile)], copied
+        )
+        copy.start()
+        copy.wait()
 
 
 def interleave(first, first_count, second, second_count):
@@ -323,36 +328,52 @@
         pass
 
 
-def march(cells, halos, scalars, first_id, count, groups, transfer, depth_total, tile):
+def march(cells, halos, scalars, first_id, count, image, transfer, depth_total, tile, partial=None):
     slices, height, width = cells.shape
-    depth, lines, ends = halos
+    depth, ends, lines = halos
     assert slices % SLOTS == 0 and SLOTS == 2 * DEPTH
     tf_color, tf_opacity = transfer
     knot_count = tf_color.shape[1]
     optical = float(-2.0 / depth_total * NORM**2 * np.log2(np.e))
-    return pl.pallas_call(
-        functools.partial(
-            march_kernel, first_id=first_id, count=count, tile=tile, optical=optical
-        ),
-        in_specs=[SCALARS] + [VECTORS] * 5 + [[VECTORS] * 2, [VECTORS] * 2, VECTORS],
-        out_specs=VECTORS,
-        out_shape=jax.ShapeDtypeStruct((groups, 4, count // groups * tile, width), jnp.float32),
-        scratch_shapes=[
-            pltpu.VMEM((SLOTS, 4 * tile, width), jnp.float32),
-            pltpu.VMEM((2, slices, PACK, width), cells.dtype),
-        ],
-        compiler_params=pltpu.CompilerParams(vmem_limit_bytes=24 * 2**20),
-    )(
+    groups, rows = image
+    patch = partial is not None
+    scratch = [pltpu.VMEM((SLOTS, 4 * tile, width), jnp.float32)]
+    operands = [
         scalars,
         jnp.asarray(stencil(tile, knot_count)),
         jnp.asarray(segment_lines(knot_count)),
         tf_color,
         tf_opacity.reshape(1, knot_count),
         cells,
-        depth,
-        lines,
+        *depth,
         ends,
-    )
+    ]
+    if lines is not None:
+        operands += lines
+        scratch.append(pltpu.VMEM((2, slices, PACK, width), cells.dtype))
+    in_specs = [SCALARS] + [VECTORS] * (len(operands) - 1)
+    if patch:
+        operands.append(partial)
+        in_specs.append(ANYWHERE)
+        scratch = [pltpu.VMEM((1, 4, tile, width), jnp.float32)] + scratch
+        scratch.append(pltpu.SemaphoreType.DMA)
+    return pl.pallas_call(
+        functools.partial(
+            march_kernel,
+            first_id=first_id,
+            count=count,
+            tile=tile,
+            optical=optical,
+            with_lines=lines is not None,
+            patch=patch,
+        ),
+        in_specs=in_specs,
+        out_specs=ANYWHERE if patch else VECTORS,
+        out_shape=jax.ShapeDtypeStruct((groups, 4, rows, width), jnp.float32),
+        input_output_aliases={len(operands) - 1: 0} if patch else {},
+        scratch_shapes=scratch,
+        compiler_params=pltpu.CompilerParams(vmem_limit_bytes=24 * 2**20),
+    )(*operands)
 
 
 def ordered_over(first, second, swapped):
@@ -437,25 +458,40 @@
     groups = 1 << group_bits
     per_group = view_count // groups
 
-    calls = {4: ([3, 1], [2], [0]), 2: ([1], [0]), 1: ([0],)}[groups]
     steps = tile_rows // tile
     count = per_group * steps
     blocks = (np.arange(per_group)[:, None] * groups * steps + np.arange(steps)).reshape(-1)
+    place_in_group = position & (groups - 1)
+
+    def tiles_of(*distances):
+        return jnp.concatenate([(place_in_group ^ d) * steps + blocks for d in distances])
+
+    def in_order(tiles):
+        return [tiles, jnp.arange(tiles.shape[0])]
+
+    if groups == 4:
+        both = tiles_of(3, 1)
+        last = 2 * count - 1
+        missing = jnp.where(
+            place_in_group & 1 == 1,
+            jnp.where(place_in_group == 3, 0, count),
+            jnp.where(place_in_group == 0, count - 1, last),
+        )
+        places = np.arange(2 * count)
+        order = jnp.where(places == missing, last, places)
+        order = order[:last]
+        moved = jnp.sum(jnp.where(places == order[:, None], both, 0), axis=1)
+        edge = jnp.sum(jnp.where(places == missing, both, 0))[None]
+        calls = [[moved, order], [edge, missing[None]], in_order(tiles_of(2)), in_order(tiles_of(0))]
+    elif groups == 2:
+        calls = [in_order(tiles_of(1)), in_order(tiles_of(0))]
+    else:
+        calls = [in_order(tiles_of(0))]
+
     first_side = len(AXES)
-    first_id = first_side + bits
-    scalars = jnp.concatenate(
-        [
-            jnp.stack(
-                [lax.axis_index(axis) & 1 for axis in AXES]
-                + [position >> bit & 1 for bit in range(bits)]
-            )
-        ]
-        + [
-            (position & (groups - 1) ^ distance) * steps + blocks
-            for call in calls
-            for distance in call
-        ]
-    ).astype(jnp.int32)
+    scalars = [lax.axis_index(axis) & 1 for axis in AXES] + [position >> i & 1 for i in range(bits)]
+    first_ids = np.cumsum([len(scalars)] + [2 * call[0].shape[0] for call in calls])
+    scalars = jnp.concatenate([jnp.stack(scalars)] + sum(calls, [])).astype(jnp.int32)
 
     volume = pltpu.with_memory_space_constraint(volume, pltpu.HBM)
     cells, *faces = prepare(volume, scalars)
@@ -463,37 +499,38 @@
     depth, lines = (
         found if len(found) == 2 else found + [jnp.zeros_like(found[0])] for found in (depth, lines)
     )
-    halos = (depth, lines, sum(ends[1:], ends[0]))
-
-    def march_call(call, after=None):
+    ends = sum(ends[1:], ends[0])
+
+    def march_call(call, out_groups=1, after=None, partial=None, with_lines=True):
         here = scalars
         if after is not None:
             here, _ = lax.optimization_barrier((scalars, after))
-        start = first_id + count * sum(len(earlier) for earlier in calls[:call])
         return march(
             cells,
-            halos,
+            (depth, ends, lines if with_lines else None),
             here,
-            start,
-            count * len(calls[call]),
-            len(calls[call]),
+            int(first_ids[call]),
+            calls[call][0].shape[0],
+            (out_groups, count * tile),
             (tf_color, tf_opacity),
             slices * view_count,
             tile,
+            partial,
         )
 
     if groups == 4:
-        far = march_call(0)
+        far = march_call(0, 2, with_lines=False)
+        far = march_call(1, 2, partial=far)
         received = from_partner(far, "view", 0)
-        near = march_call(1, far)
+        near = march_call(2, after=far)
         code = merge_pair(scalars, near, received, first_side)
         code_received = from_partner(code, "view", 1)
-        near = march_call(2, code)
+        near = march_call(3, after=code)
         image = merge_last(scalars, near, received, code_received, first_side, bits == 2)
     elif groups == 2:
         far = march_call(0)
         received = from_partner(far, "view", 0)
-        image = merged(march_call(1, far)[0], received[0], position & 1)
+        image = merged(march_call(1, after=far)[0], received[0], position & 1)
     else:
         image = march_call(0)[0]
     if bits == 2:

time: 41 us -> 41 us (level)
  waiting for transfers between devices: 4.92 us -> 2.64 us
  other arithmetic: 0.01 us -> 0.9 us
  Pallas kernels: 25.8 us -> 26.4 us
  starting transfers between devices: 9.42 us -> 10 us
  local copies, waits for them, and re-layouts: 0.09 us -> 0.65 us
    ppermute x5, waiting for transfers between devices: 1.7 us -> 0.01 us  [exchange(): lax.ppermute(face, axis, both)]
    reduce_sum x0 -> x2, other arithmetic: none -> 0.89 us  [the longest x1 0.71 us: on_device(): edge = jnp.sum(jnp.where(places == missing, both, 0))[None]]
    ppermute x2, starting transfers between devices: 0.24 us -> 0.84 us  [from_partner(): return lax.ppermute(value, axis, pairs)]
    ppermute x2, waiting for transfers between devices: 3.22 us -> 2.62 us  [from_partner(): return lax.ppermute(value, axis, pairs)]
    concatenate x1, local copies, waits for them, and re-layouts: 0.08 us -> 0.64 us  [on_device(): jnp.concatenate([jnp.stack(scalars)] + sum(calls, [])).astype(jnp.int32)]
    pallas_call x3 -> x4, Pallas kernels: 20.7 us -> 21.3 us  [march(): pl.pallas_call(functools.partial(march_kernel, first_id=first_id, count=c...]
  transfers between devices with their start and end apart: 7 -> 7, of which waited for: 2 -> 1; matrix products, arithmetic and copies ran while one was open for 0% -> 0% of each run, Pallas kernels for 27% -> 45%
where the time goes in v6:
time: 41 us; the launch traced here: 40.8 us
  Pallas kernels  26.4 us (64%)
  starting transfers between devices  10 us (24%)
  waiting for transfers between devices  2.64 us (6%)
  other arithmetic  0.9 us (2%)
  local copies, waits for them, and re-layouts  0.65 us (2%)
    pallas_call x4, Pallas kernels, march(): pl.pallas_call(functools.partial(march_kernel, first_id=first_id, count=c...  21.3 us
    ppermute x5, starting transfers between devices, exchange(): lax.ppermute(face, axis, both)  9.18 us
    pallas_call x1, Pallas kernels, prepare(): pl.pallas_call(prepare_kernel, in_specs=[pl.BlockSpec(memory_space=pltpu....  2.96 us
    ppermute x2, waiting for transfers between devices, from_partner(): return lax.ppermute(value, axis, pairs)  2.62 us
    pallas_call x1, Pallas kernels, merge_last(): pl.pallas_call(functools.partial(last_kernel, side=side, finish=finish),...  1.48 us
    ppermute x2, starting transfers between devices, from_partner(): return lax.ppermute(value, axis, pairs)  0.84 us
  transfers between devices with their start and end apart: 7, of which 1 were waited for; matrix products, arithmetic and copies ran while one was open for 0% of the time, Pallas kernels for 45%

profile of v6, /device:TPU:12, one launch (start us, length us, event | category | flops | bytes accessed | tf_op | source)
XLA Modules:
  0.0 40.8 jit_solution(2089229259608212993)
XLA Ops:
  0.1 0.7 %fusion = (s32[]{:T(128)}, s32[4]{0:T(128)S(1)}, s32[4]{0:T(128)S(1)}) fusion(s32[]{:T(128)} %select_n.25, s32[2]{0:T(128)S(1)} %iota_add_fusion, s32[2]{0:T(128)S(1)} %iota_add_fusion.1), kind=kLoop, calls=%fused_computation.8 | loop fusion | flops 19 | bytes 56 | tf_op jit(solution)/shard_map/reduce_sum | solution.py:484
  0.8 0.2 select_reduce_fusion
  1.0 0.6 %concatenate.7.scalars_ref.refs_0_ = s32[21]{0:T(128)S(1)} concatenate(s32[1]{0:T(128)} %bitcast, s32[1]{0:T(128)} %bitcast.1, s32[1]{0:T(128)} %bitcast.2, s32[1]{0:T(128)} %bitcast.3, s32[1]{0:T(128)} %bitcast.4, s32[3]{0:T(128)S(1)} %select_reduce_fusion, s32[3]{0:T(128)S(1)} %bitcast.17, s32[1]{0:T(128)} %bitcast.5, s32[1]{0:T(128)} %bitcast.6, s32[2]{0:T(128)S(1)} %get-tuple-element.25, ...), dimensions={0} | concatenate | bytes 168 | tf_op jit(solution)/shard_map/concatenate | solution.py:494
  1.6 3.0 %shard_map.127 = (bf16[16,256,512]{2,1,0:T(8,128)(2,1)S(1)}, bf16[256,512]{1,0:T(8,128)(2,1)S(1)}, bf16[256,512]{1,0:T(8,128)(2,1)S(1)}, bf16[16,512]{1,0:T(8,12...) custom-call(s32[21]{0:T(128)S(1)} %concatenate.7.scalars_ref.refs_0_, bf16[16,256,512]{2,1,0:T(8,128)(2,1)} %volume_ref.1), custom_call_target="tpu_custom_call" | custom-call | tf_op jit(solution)/shard_map/pallas_call | solution.py:147
  4.6 0.1 collective-permute-start
  4.7 2.5 %collective-permute-start.1 = (bf16[256,512]{1,0:T(8,128)(2,1)S(1)}, bf16[256,512]{1,0:T(8,128)(2,1)S(1)}, u32[]{:S(2)}, u32[]{:S(2)}) collective-permute-start(bf16[256,512]{1,0:T(8,128)(2,1)S(1)} %get-tuple-element.15), channel_id=1, source_target_pairs={{8,16},{16,8},{9,17},{17,9},{10,18},{18,10},{11,19},{19,11},{12,20... | collective-permute-start | bytes 786440 | tf_op jit(solution)/shard_map/ppermute | solution.py:68
  7.2 1.6 %collective-permute-start.2 = (bf16[256,128]{1,0:T(8,128)(2,1)S(1)}, bf16[256,128]{1,0:T(8,128)(2,1)S(1)}, u32[]{:S(2)}, u32[]{:S(2)}) collective-permute-start(bf16[256,128]{1,0:T(8,128)(2,1)S(1)} %get-tuple-element.16), channel_id=1, source_target_pairs={{0,1},{1,0},{2,3},{3,2},{4,5},{5,4},{6,7},{7,6},{8,9},{9,8},{10,11... | collective-permute-start | bytes 196616 | tf_op jit(solution)/shard_map/ppermute | solution.py:68
  8.7 0.4 %collective-permute-start.3 = (bf16[16,512]{1,0:T(8,128)(2,1)S(1)}, bf16[16,512]{1,0:T(8,128)(2,1)S(1)}, u32[]{:S(2)}, u32[]{:S(2)}) collective-permute-start(bf16[16,512]{1,0:T(8,128)(2,1)S(1)} %get-tuple-element.17), channel_id=1, source_target_pairs={{0,2},{4,6},{2,0},{6,4},{1,3},{5,7},{3,1},{7,5},{8,10},{12,14},{10... | collective-permute-start | bytes 49160 | tf_op jit(solution)/shard_map/ppermute | solution.py:68
  9.2 4.6 %collective-permute-start.4 = (bf16[16,512]{1,0:T(8,128)(2,1)S(1)}, bf16[16,512]{1,0:T(8,128)(2,1)S(1)}, u32[]{:S(2)}, u32[]{:S(2)}) collective-permute-start(bf16[16,512]{1,0:T(8,128)(2,1)S(1)} %get-tuple-element.18), channel_id=1, source_target_pairs={{2,4},{4,2},{3,5},{5,3},{10,12},{12,10},{11,13},{13,11},{18,20},{2... | collective-permute-start | bytes 49160 | tf_op jit(solution)/shard_map/ppermute | solution.py:68
  13.8 0.0 collective-permute-done.2.refs_8_
  13.8 0.0 collective-permute-done.refs_6_
  13.8 0.0 collective-permute-done.1.refs_7_
  13.9 7.5 %shard_map.128.refs_11_ = f32[2,4,64,512]{3,2,1,0:T(8,128)S(1)} custom-call(s32[21]{0:T(128)S(1)} %concatenate.7.scalars_ref.refs_0_, bf16[128,208]{1,0:T(8,128)(2,1)S(1)} %copy-done, f32[24,16]{1,0:T(8,128)S(1)} %copy-done.1, f32[3,16]{1,0:T(4,128)S(1)} %copy-done.2, f32[1,16]{1,0:T(1,128)S(1)} %bitcast.12, ...), custom_call_target="tpu_custom_call" | custom-call | tf_op jit(solution)/shard_map/pallas_call | solution.py:360
  21.4 0.0 collective-permute-done.3.refs_9_
  21.4 0.0 collective-permute-done.4.refs_10_
  21.4 3.1 %shard_map.129 = f32[2,4,64,512]{3,2,1,0:T(8,128)S(1)} custom-call(s32[21]{0:T(128)S(1)} %concatenate.7.scalars_ref.refs_0_, bf16[128,208]{1,0:T(8,128)(2,1)S(1)} %copy-done, f32[24,16]{1,0:T(8,128)S(1)} %copy-done.1, f32[3,16]{1,0:T(4,128)S(1)} %copy-done.2, f32[1,16]{1,0:T(1,128)S(1)} %bitcast.13, ...), custom_call_target="tpu_custom_call", output_to_operand_aliasing={{}: (11, {})} | custom-call | tf_op jit(solution)/shard_map/pallas_call | solution.py:360
  24.5 0.1 collective-permute-start.5
  24.6 5.3 %shard_map.130.own_ref = f32[1,4,64,512]{3,2,1,0:T(8,128)S(1)} custom-call(s32[21]{0:T(128)S(1)} %concatenate.7.scalars_ref.refs_0_, bf16[128,208]{1,0:T(8,128)(2,1)S(1)} %copy-done, f32[24,16]{1,0:T(8,128)S(1)} %copy-done.1, f32[3,16]{1,0:T(4,128)S(1)} %copy-done.2, f32[1,16]{1,0:T(1,128)S(1)} %bitcast.14, ...), custom_call_target="tpu_custom_call" | custom-call | tf_op jit(solution)/shard_map/pallas_call | solution.py:360
  29.9 0.0 collective-permute-done.5.other_ref
  29.9 0.7 %shard_map.131 = bf16[4,64,512]{2,1,0:T(8,128)(2,1)S(1)} custom-call(s32[21]{0:T(128)S(1)} %concatenate.7.scalars_ref.refs_0_, f32[1,4,64,512]{3,2,1,0:T(8,128)S(1)} %shard_map.130.own_ref, f32[2,4,64,512]{3,2,1,0:T(8,128)S(1)} %collective-permute-done.5.other_ref), custom_call_target="tpu_custom_call" | custom-call | tf_op jit(solution)/shard_map/pallas_call | solution.py:412
  30.6 0.8 %collective-permute-start.6 = (bf16[4,64,512]{2,1,0:T(8,128)(2,1)S(1)}, bf16[4,64,512]{2,1,0:T(8,128)(2,1)S(1)}, u32[]{:S(2)}, u32[]{:S(2)}) collective-permute-start(bf16[4,64,512]{2,1,0:T(8,128)(2,1)S(1)} %shard_map.131), channel_id=1, source_target_pairs={{0,16},{8,24},{16,0},{24,8},{1,17},{9,25},{17,1},{25,9},{2,18},{10... | collective-permute-start | bytes 786440 | tf_op jit(solution)/shard_map/ppermute | solution.py:447
  31.3 5.4 %shard_map.132.own_ref = f32[1,4,64,512]{3,2,1,0:T(8,128)S(1)} custom-call(s32[21]{0:T(128)S(1)} %concatenate.7.scalars_ref.refs_0_, bf16[128,208]{1,0:T(8,128)(2,1)S(1)} %copy-done, f32[24,16]{1,0:T(8,128)S(1)} %copy-done.1, f32[3,16]{1,0:T(4,128)S(1)} %copy-done.2, f32[1,16]{1,0:T(1,128)S(1)} %bitcast.15, ...), custom_call_target="tpu_custom_call" | custom-call | tf_op jit(solution)/shard_map/pallas_call | solution.py:360
  36.7 2.6 %collective-permute-done.6.code_ref = bf16[4,64,512]{2,1,0:T(8,128)(2,1)S(1)} collective-permute-done((bf16[4,64,512]{2,1,0:T(8,128)(2,1)S(1)}, bf16[4,64,512]{2,1,0:T(8,128)(2,1)S(1)}, u32[]{:S(2)}, u32[]{:S(2)}) %collective-permute-start.6) | collective-permute-done | bytes 262176 | tf_op jit(solution)/shard_map/ppermute | solution.py:447
  39.3 1.5 %shard_map.133 = f32[4,64,512]{2,1,0:T(8,128)} custom-call(s32[21]{0:T(128)S(1)} %concatenate.7.scalars_ref.refs_0_, f32[1,4,64,512]{3,2,1,0:T(8,128)S(1)} %shard_map.132.own_ref, f32[2,4,64,512]{3,2,1,0:T(8,128)S(1)} %collective-permute-done.5.other_ref, bf16[4,64,512]{2,1,0:T(8,128)(2,1)S(1)} %collective-permute-done.6.code_ref), custom_call_target="tpu_custom_call" | custom-call | tf_op jit(solution)/shard_map/pallas_call | solution.py:424
  (12 shorter events, 0.0 us)
Async XLA Ops:
  0.0 13.8 %copy-start = (bf16[128,208]{1,0:T(8,128)(2,1)S(1)}, bf16[128,208]{1,0:T(8,128)(2,1)}, u32[]{:S(2)}) copy-start(bf16[128,208]{1,0:T(8,128)(2,1)} %constant.27.clone.refs_1_) | copy-start | bytes 159748
  0.0 13.8 %copy-start.1 = (f32[24,16]{1,0:T(8,128)S(1)}, f32[24,16]{1,0:T(8,128)}, u32[]{:S(2)}) copy-start(f32[24,16]{1,0:T(8,128)} %constant.28.clone.refs_2_) | copy-start | bytes 4612
  0.0 13.8 %copy-start.3 = (f32[16]{0:T(128)S(1)}, f32[16]{0:T(128)}, u32[]{:S(2)}) copy-start(f32[16]{0:T(128)} %param.15) | copy-start | bytes 196
  0.0 13.9 %copy-start.2 = (f32[3,16]{1,0:T(4,128)S(1)}, f32[3,16]{1,0:T(4,128)}, u32[]{:S(2)}) copy-start(f32[3,16]{1,0:T(4,128)} %refs_3_.7) | copy-start | bytes 580
  4.6 9.2 %collective-permute-start = (bf16[256,512]{1,0:T(8,128)(2,1)S(1)}, bf16[256,512]{1,0:T(8,128)(2,1)S(1)}, u32[]{:S(2)}, u32[]{:S(2)}) collective-permute-start(bf16[256,512]{1,0:T(8,128)(2,1)S(1)} %get-tuple-element.14), channel_id=1, source_target_pairs={{0,8},{16,24},{8,0},{24,16},{1,9},{17,25},{9,1},{25,17},{2,10},{18... | collective-permute-start | bytes 786440 | tf_op jit(solution)/shard_map/ppermute | solution.py:68
  4.7 9.2 %collective-permute-start.1 = (bf16[256,512]{1,0:T(8,128)(2,1)S(1)}, bf16[256,512]{1,0:T(8,128)(2,1)S(1)}, u32[]{:S(2)}, u32[]{:S(2)}) collective-permute-start(bf16[256,512]{1,0:T(8,128)(2,1)S(1)} %get-tuple-element.15), channel_id=1, source_target_pairs={{8,16},{16,8},{9,17},{17,9},{10,18},{18,10},{11,19},{19,11},{12,20... | collective-permute-start | bytes 786440 | tf_op jit(solution)/shard_map/ppermute | solution.py:68
  7.2 6.6 %collective-permute-start.2 = (bf16[256,128]{1,0:T(8,128)(2,1)S(1)}, bf16[256,128]{1,0:T(8,128)(2,1)S(1)}, u32[]{:S(2)}, u32[]{:S(2)}) collective-permute-start(bf16[256,128]{1,0:T(8,128)(2,1)S(1)} %get-tuple-element.16), channel_id=1, source_target_pairs={{0,1},{1,0},{2,3},{3,2},{4,5},{5,4},{6,7},{7,6},{8,9},{9,8},{10,11... | collective-permute-start | bytes 196616 | tf_op jit(solution)/shard_map/ppermute | solution.py:68
  8.7 12.6 %collective-permute-start.3 = (bf16[16,512]{1,0:T(8,128)(2,1)S(1)}, bf16[16,512]{1,0:T(8,128)(2,1)S(1)}, u32[]{:S(2)}, u32[]{:S(2)}) collective-permute-start(bf16[16,512]{1,0:T(8,128)(2,1)S(1)} %get-tuple-element.17), channel_id=1, source_target_pairs={{0,2},{4,6},{2,0},{6,4},{1,3},{5,7},{3,1},{7,5},{8,10},{12,14},{10... | collective-permute-start | bytes 49160 | tf_op jit(solution)/shard_map/ppermute | solution.py:68
  9.2 12.2 %collective-permute-start.4 = (bf16[16,512]{1,0:T(8,128)(2,1)S(1)}, bf16[16,512]{1,0:T(8,128)(2,1)S(1)}, u32[]{:S(2)}, u32[]{:S(2)}) collective-permute-start(bf16[16,512]{1,0:T(8,128)(2,1)S(1)} %get-tuple-element.18), channel_id=1, source_target_pairs={{2,4},{4,2},{3,5},{5,3},{10,12},{12,10},{11,13},{13,11},{18,20},{2... | collective-permute-start | bytes 49160 | tf_op jit(solution)/shard_map/ppermute | solution.py:68
  24.5 5.4 %collective-permute-start.5 = (f32[2,4,64,512]{3,2,1,0:T(8,128)S(1)}, f32[2,4,64,512]{3,2,1,0:T(8,128)S(1)}, u32[]{:S(2)}, u32[]{:S(2)}) collective-permute-start(f32[2,4,64,512]{3,2,1,0:T(8,128)S(1)} %shard_map.129), channel_id=1, source_target_pairs={{0,8},{8,0},{16,24},{24,16},{1,9},{9,1},{17,25},{25,17},{2,10},{10... | collective-permute-start | bytes 3145736 | tf_op jit(solution)/shard_map/ppermute | solution.py:447
  30.6 8.8 %collective-permute-start.6 = (bf16[4,64,512]{2,1,0:T(8,128)(2,1)S(1)}, bf16[4,64,512]{2,1,0:T(8,128)(2,1)S(1)}, u32[]{:S(2)}, u32[]{:S(2)}) collective-permute-start(bf16[4,64,512]{2,1,0:T(8,128)(2,1)S(1)} %shard_map.131), channel_id=1, source_target_pairs={{0,16},{8,24},{16,0},{24,8},{1,17},{9,25},{17,1},{25,9},{2,18},{10... | collective-permute-start | bytes 786440 | tf_op jit(solution)/shard_map/ppermute | solution.py:447

commit v7 on v6

--- a/solution.py
+++ b/solution.py
@@ -30,7 +30,6 @@
     operand_batching_dims=(1,),
     start_indices_batching_dims=(1,),
 )
-SCALARS = pl.BlockSpec(memory_space=pltpu.SMEM)
 VECTORS = pl.BlockSpec(memory_space=pltpu.VMEM)
 ANYWHERE = pl.BlockSpec(memory_space=pl.ANY)
 
@@ -83,10 +82,15 @@
     return lines.reshape(3 * rows, knot_count)
 
 
+def parities():
+    return [lax.axis_index(axis) & 1 for axis in AXES]
+
+
 def prepare_kernel(
-    scalars_ref, volume_ref, cells_ref, depth_outs, row_outs, column_outs, arrived
+    volume_ref, cells_ref, depth_outs, row_outs, column_outs, arrived
 ):
     slices, height, width = cells_ref.shape
+    odd = parities()
     chunks = arrived.shape[0]
     size = slices // chunks
     copies = [
@@ -106,7 +110,7 @@
         copy.wait()
         here = range(chunk * size, (chunk + 1) * size)
         for turn in range(len(row_outs)):
-            is_first = scalars_ref[1] == 1 - turn
+            is_first = odd[1] == 1 - turn
             for z in here:
                 line = jnp.where(is_first, cells_ref[z, :1], cells_ref[z, height - 1 :])
                 lines[turn] = jnp.where(
@@ -125,18 +129,18 @@
             column_outs[turn][...] = found
 
         for turn in range(len(column_outs)):
-            pl.when(scalars_ref[2] == 1 - turn)(functools.partial(columns, turn, 0, 0, -1))
-            pl.when(scalars_ref[2] == turn)(
+            pl.when(odd[2] == 1 - turn)(functools.partial(columns, turn, 0, 0, -1))
+            pl.when(odd[2] == turn)(
                 functools.partial(columns, turn, width - LANES, LANES - 1, 0)
             )
     for turn in range(len(row_outs)):
         row_outs[turn][...] = lines[turn]
     for turn in range(len(depth_outs)):
-        face = jnp.where(scalars_ref[0] == 1 - turn, 0, slices - 1)
+        face = jnp.where(odd[0] == 1 - turn, 0, slices - 1)
         depth_outs[turn][...] = cells_ref[face]
 
 
-def prepare(volume, scalars):
+def prepare(volume):
     slices, height, width = volume.shape
     assert 2 * slices <= LANES
     shapes = [(height, width), (slices, width), (height, LANES)]
@@ -146,17 +150,17 @@
     ]
     return pl.pallas_call(
         prepare_kernel,
-        in_specs=[pl.BlockSpec(memory_space=pltpu.SMEM), pl.BlockSpec(memory_space=pltpu.HBM)],
+        in_specs=[pl.BlockSpec(memory_space=pltpu.HBM)],
         out_specs=jax.tree.map(lambda _: VECTORS, out_shape),
         out_shape=out_shape,
         scratch_shapes=[pltpu.SemaphoreType.DMA((4 if slices % 4 == 0 else 1,))],
         compiler_params=pltpu.CompilerParams(vmem_limit_bytes=24 * 2**20),
-    )(scalars, volume)
-
-
-def march_kernel(*refs, first_id, count, tile, optical, with_lines, patch):
-    scalars_ref, stencil_ref, lines_ref, color_ref, opacity_ref, cells_ref = refs[:6]
-    depth_refs, ends_ref, refs = refs[6:8], refs[8], refs[9:]
+    )(volume)
+
+
+def march_kernel(*refs, tiles, count, tile, optical, with_lines, patch):
+    stencil_ref, lines_ref, color_ref, opacity_ref, cells_ref = refs[:5]
+    depth_refs, ends_ref, refs = refs[5:7], refs[7], refs[8:]
     if with_lines:
         line_refs, refs = refs[:2], refs[2:]
     if patch:
@@ -227,18 +231,15 @@
         weight = (state[3] - through) * shading
         return [total + value * weight for total, value in zip(state, values[:3])] + [through]
 
-    odd = [scalars_ref[axis] == 1 for axis in range(2)]
+    odd = [parity == 1 for parity in parities()[:2]]
     if with_lines:
         for side in range(2):
             lines = jnp.where(odd[1], line_refs[side][...], line_refs[1 - side][...])
             for z in range(slices):
                 sides_ref[side, z] = jnp.broadcast_to(lines[z : z + 1], (PACK, width))
 
-    def place(i):
-        return scalars_ref[first_id + count + i]
-
     def gradients(i, z):
-        start = pl.multiple_of(scalars_ref[first_id + i] * tile, tile)
+        start = pl.multiple_of(tiles(i)[1] * tile, tile)
         rows = pl.ds(start, tile)
 
         def across(side):
@@ -276,8 +277,9 @@
             yield
 
     def shades(i, first):
-        group = 0 if patch else place(i) // per_group
-        target = 0 if patch else pl.multiple_of((place(i) - group * per_group) * tile, tile)
+        place = tiles(i)[0]
+        group = 0 if patch else place // per_group
+        target = 0 if patch else pl.multiple_of((place - group * per_group) * tile, tile)
         for column in range(0, width, LANES):
             for row in range(0, tile, HALF):
                 here = (pl.ds(target + row, HALF), pl.ds(column, LANES))
@@ -308,8 +310,9 @@
             pass
     lax.fori_loop(0, count, one_tile, 0)
     if patch:
-        group = place(0) // (whole_ref.shape[2] // tile)
-        rows = (place(0) - group * (whole_ref.shape[2] // tile)) * tile
+        per_group = whole_ref.shape[2] // tile
+        group = tiles(0)[0] // per_group
+        rows = (tiles(0)[0] - group * per_group) * tile
         copy = pltpu.make_async_copy(
             image_ref.at[0], whole_ref.at[group, :, pl.ds(pl.multiple_of(rows, tile), tile)], copied
         )
@@ -328,7 +331,7 @@
         pass
 
 
-def march(cells, halos, scalars, first_id, count, image, transfer, depth_total, tile, partial=None):
+def march(cells, halos, tiles, count, image, transfer, depth_total, tile, partial=None):
     slices, height, width = cells.shape
     depth, ends, lines = halos
     assert slices % SLOTS == 0 and SLOTS == 2 * DEPTH
@@ -339,7 +342,6 @@
     patch = partial is not None
     scratch = [pltpu.VMEM((SLOTS, 4 * tile, width), jnp.float32)]
     operands = [
-        scalars,
         jnp.asarray(stencil(tile, knot_count)),
         jnp.asarray(segment_lines(knot_count)),
         tf_color,
@@ -351,7 +353,7 @@
     if lines is not None:
         operands += lines
         scratch.append(pltpu.VMEM((2, slices, PACK, width), cells.dtype))
-    in_specs = [SCALARS] + [VECTORS] * (len(operands) - 1)
+    in_specs = [VECTORS] * len(operands)
     if patch:
         operands.append(partial)
         in_specs.append(ANYWHERE)
@@ -360,7 +362,7 @@
     return pl.pallas_call(
         functools.partial(
             march_kernel,
-            first_id=first_id,
+            tiles=tiles,
             count=count,
             tile=tile,
             optical=optical,
@@ -384,15 +386,15 @@
     return colours + [first[3] * second[3]]
 
 
-def pair_kernel(scalars_ref, own_ref, other_ref, code_ref, *, side):
+def pair_kernel(own_ref, other_ref, code_ref):
     own = [own_ref[0, c] for c in range(4)]
     other = [other_ref[0, c] for c in range(4)]
-    merged = ordered_over(own, other, scalars_ref[side] == 1)
+    merged = ordered_over(own, other, lax.axis_index("view") & 1 == 1)
     for c in range(4):
         code_ref[c] = jnp.exp2(CODE_SCALE * merged[c] - CODE_SHIFT).astype(code_ref.dtype)
 
 
-def last_kernel(scalars_ref, own_ref, other_ref, code_ref, out_ref, *, side, finish):
+def last_kernel(own_ref, other_ref, code_ref, out_ref, *, finish):
     rows = pl.ds(pl.multiple_of(pl.program_id(0) * out_ref.shape[1], HALF), out_ref.shape[1])
     own = [own_ref[0, c, rows] for c in range(4)]
     other = [other_ref[1, c, rows] for c in range(4)]
@@ -401,34 +403,34 @@
         (jnp.log2(code_ref[c, coded].astype(jnp.float32)) + CODE_SHIFT) * (1.0 / CODE_SCALE)
         for c in range(4)
     ]
-    pair = ordered_over(own, other, scalars_ref[side] == 1)
-    merged = ordered_over(pair, far, scalars_ref[side + 1] == 1)
+    pair = ordered_over(own, other, lax.axis_index("view") & 1 == 1)
+    merged = ordered_over(pair, far, lax.axis_index("view") & 2 == 2)
     for c in range(3):
         out_ref[c] = merged[c]
     out_ref[3] = 1.0 - merged[3] if finish else merged[3]
 
 
-def merge_pair(scalars, own, other, side):
+def merge_pair(own, other):
     return pl.pallas_call(
-        functools.partial(pair_kernel, side=side),
-        in_specs=[SCALARS, VECTORS, VECTORS],
+        pair_kernel,
+        in_specs=[VECTORS, VECTORS],
         out_specs=VECTORS,
         out_shape=jax.ShapeDtypeStruct(own.shape[1:], jnp.bfloat16),
         compiler_params=pltpu.CompilerParams(vmem_limit_bytes=24 * 2**20),
-    )(scalars, own, other)
-
-
-def merge_last(scalars, own, other, code, side, finish):
+    )(own, other)
+
+
+def merge_last(own, other, code, finish):
     _, _, rows, width = own.shape
     steps = 2 if rows % (2 * PACK) == 0 else 1
     return pl.pallas_call(
-        functools.partial(last_kernel, side=side, finish=finish),
+        functools.partial(last_kernel, finish=finish),
         grid=(steps,),
-        in_specs=[SCALARS, VECTORS, VECTORS, VECTORS],
+        in_specs=[VECTORS, VECTORS, VECTORS],
         out_specs=pl.BlockSpec((4, rows // steps, width), lambda i: (0, i, 0)),
         out_shape=jax.ShapeDtypeStruct(own.shape[1:], jnp.float32),
         compiler_params=pltpu.CompilerParams(vmem_limit_bytes=24 * 2**20),
-    )(scalars, own, other, code)
+    )(own, other, code)
 
 
 def over(nearer, farther):
@@ -460,57 +462,48 @@
 
     steps = tile_rows // tile
     count = per_group * steps
-    blocks = (np.arange(per_group)[:, None] * groups * steps + np.arange(steps)).reshape(-1)
-    place_in_group = position & (groups - 1)
-
-    def tiles_of(*distances):
-        return jnp.concatenate([(place_in_group ^ d) * steps + blocks for d in distances])
-
-    def in_order(tiles):
-        return [tiles, jnp.arange(tiles.shape[0])]
-
-    if groups == 4:
-        both = tiles_of(3, 1)
-        last = 2 * count - 1
-        missing = jnp.where(
-            place_in_group & 1 == 1,
-            jnp.where(place_in_group == 3, 0, count),
-            jnp.where(place_in_group == 0, count - 1, last),
-        )
-        places = np.arange(2 * count)
-        order = jnp.where(places == missing, last, places)
-        order = order[:last]
-        moved = jnp.sum(jnp.where(places == order[:, None], both, 0), axis=1)
-        edge = jnp.sum(jnp.where(places == missing, both, 0))[None]
-        calls = [[moved, order], [edge, missing[None]], in_order(tiles_of(2)), in_order(tiles_of(0))]
-    elif groups == 2:
-        calls = [in_order(tiles_of(1)), in_order(tiles_of(0))]
-    else:
-        calls = [in_order(tiles_of(0))]
-
-    first_side = len(AXES)
-    scalars = [lax.axis_index(axis) & 1 for axis in AXES] + [position >> i & 1 for i in range(bits)]
-    first_ids = np.cumsum([len(scalars)] + [2 * call[0].shape[0] for call in calls])
-    scalars = jnp.concatenate([jnp.stack(scalars)] + sum(calls, [])).astype(jnp.int32)
+
+    def tile_at(place, distances):
+        at = lax.axis_index("view") & (groups - 1)
+        group = place // count
+        step = place - group * count
+        block = step // steps
+        distance = distances[0] + (distances[-1] - distances[0]) * group
+        return ((at ^ distance) + block * groups) * steps + step - block * steps
+
+    def all_tiles(distance):
+        return lambda i: (i, tile_at(i, (distance,)))
+
+    def missing_tile():
+        at = lax.axis_index("view") & 3
+        low = jnp.where(at == 3, 0, count)
+        high = jnp.where(at == 0, count - 1, 2 * count - 1)
+        return jnp.where(at & 1 == 1, low, high)
+
+    def inner_tiles(i):
+        place = jnp.where(i == missing_tile(), 2 * count - 1, i)
+        return place, tile_at(place, (3, 1))
+
+    def edge_tile(i):
+        return missing_tile(), tile_at(missing_tile(), (3, 1))
 
     volume = pltpu.with_memory_space_constraint(volume, pltpu.HBM)
-    cells, *faces = prepare(volume, scalars)
+    cells, *faces = prepare(volume)
     depth, lines, ends = (exchange(face, axis) for face, axis in zip(faces, AXES))
     depth, lines = (
         found if len(found) == 2 else found + [jnp.zeros_like(found[0])] for found in (depth, lines)
     )
     ends = sum(ends[1:], ends[0])
 
-    def march_call(call, out_groups=1, after=None, partial=None, with_lines=True):
-        here = scalars
+    def march_call(tiles, tile_count, out_groups=1, after=None, partial=None, with_lines=True):
+        here = ends
         if after is not None:
-            here, _ = lax.optimization_barrier((scalars, after))
+            here, _ = lax.optimization_barrier((ends, after))
         return march(
             cells,
-            (depth, ends, lines if with_lines else None),
-            here,
-            int(first_ids[call]),
-            calls[call][0].shape[0],
+            (depth, here, lines if with_lines else None),
+            tiles,
+            tile_count,
             (out_groups, count * tile),
             (tf_color, tf_opacity),
             slices * view_count,
@@ -519,20 +512,20 @@
         )
 
     if groups == 4:
-        far = march_call(0, 2, with_lines=False)
-        far = march_call(1, 2, partial=far)
+        far = march_call(inner_tiles, 2 * count - 1, 2, with_lines=False)
+        far = march_call(edge_tile, 1, 2, partial=far)
         received = from_partner(far, "view", 0)
-        near = march_call(2, after=far)
-        code = merge_pair(scalars, near, received, first_side)
+        near = march_call(all_tiles(2), count, after=far)
+        code = merge_pair(near, received)
         code_received = from_partner(code, "view", 1)
-        near = march_call(3, after=code)
-        image = merge_last(scalars, near, received, code_received, first_side, bits == 2)
+        near = march_call(all_tiles(0), count, after=code)
+        image = merge_last(near, received, code_received, bits == 2)
     elif groups == 2:
-        far = march_call(0)
+        far = march_call(all_tiles(1), count)
         received = from_partner(far, "view", 0)
-        image = merged(march_call(1, after=far)[0], received[0], position & 1)
+        image = merged(march_call(all_tiles(0), count, after=far)[0], received[0], position & 1)
     else:
-        image = march_call(0)[0]
+        image = march_call(all_tiles(0), count)[0]
     if bits == 2:
         return image.reshape(4, 1, tile_rows, width)
     image = image.reshape((4,) + (2,) * (bits - group_bits) + (tile_rows, width))

time: 41 us -> 36.5 us (0.89)
  Pallas kernels: 26.4 us -> 22.9 us
  other arithmetic: 0.9 us -> 0 us
  local copies, waits for them, and re-layouts: 0.65 us -> 0.02 us
  waiting for transfers between devices: 2.64 us -> 3.19 us
    pallas_call x6, Pallas kernels: 23.4 us -> 20.5 us  [the longest x4 19.4 us: march(): pl.pallas_call(functools.partial(march_kernel, tiles=tiles, count=count,...]
    reduce_sum x2 -> x0, other arithmetic: 0.89 us -> none  [the longest x1 0.71 us: on_device(): edge = jnp.sum(jnp.where(places == missing, both, 0))[None]]
    concatenate x1 -> x0, local copies, waits for them, and re-layouts: 0.64 us -> none  [on_device(): jnp.concatenate([jnp.stack(scalars)] + sum(calls, [])).astype(jnp.int32)]
    ppermute x2, waiting for transfers between devices: 2.62 us -> 3.18 us  [from_partner(): return lax.ppermute(value, axis, pairs)]
    pallas_call x1, Pallas kernels: 2.96 us -> 2.46 us  [prepare(): pl.pallas_call(prepare_kernel, in_specs=[pl.BlockSpec(memory_space=pltpu....]
  transfers between devices with their start and end apart: 7 -> 7, of which waited for: 1 -> 1; matrix products, arithmetic and copies ran while one was open for 0% -> 0% of each run, Pallas kernels for 45% -> 46%
where the time goes in v7:
time: 36.5 us; the launch traced here: 36.3 us
  Pallas kernels  22.9 us (63%)
  starting transfers between devices  10 us (27%)
  waiting for transfers between devices  3.19 us (9%)
    pallas_call x4, Pallas kernels, march(): pl.pallas_call(functools.partial(march_kernel, tiles=tiles, count=count,...  19.4 us
    ppermute x5, starting transfers between devices, exchange(): lax.ppermute(face, axis, both)  9.17 us
    ppermute x2, waiting for transfers between devices, from_partner(): return lax.ppermute(value, axis, pairs)  3.18 us
    pallas_call x1, Pallas kernels, prepare(): pl.pallas_call(prepare_kernel, in_specs=[pl.BlockSpec(memory_space=pltpu....  2.46 us
    pallas_call x1, Pallas kernels, merge_last(): pl.pallas_call(functools.partial(last_kernel, finish=finish), grid=(steps...  0.93 us
    ppermute x2, starting transfers between devices, from_partner(): return lax.ppermute(value, axis, pairs)  0.82 us
  transfers between devices with their start and end apart: 7, of which 1 were waited for; matrix products, arithmetic and copies ran while one was open for 0% of the time, Pallas kernels for 46%

profile of v7, /device:TPU:12, one launch (start us, length us, event | category | flops | bytes accessed | tf_op | source)
XLA Modules:
  0.0 36.3 jit_solution(8077567947363898812)
XLA Ops:
  0.0 0.0 copy-start.2
  0.0 2.5 %shard_map.109 = (bf16[16,256,512]{2,1,0:T(8,128)(2,1)S(1)}, bf16[256,512]{1,0:T(8,128)(2,1)S(1)}, bf16[256,512]{1,0:T(8,128)(2,1)S(1)}, bf16[16,512]{1,0:T(8,12...) custom-call(bf16[16,256,512]{2,1,0:T(8,128)(2,1)} %volume_ref.1), custom_call_target="tpu_custom_call" | custom-call | tf_op jit(solution)/shard_map/pallas_call | solution.py:151
  2.5 0.1 collective-permute-start
  2.6 2.5 %collective-permute-start.1 = (bf16[256,512]{1,0:T(8,128)(2,1)S(1)}, bf16[256,512]{1,0:T(8,128)(2,1)S(1)}, u32[]{:S(2)}, u32[]{:S(2)}) collective-permute-start(bf16[256,512]{1,0:T(8,128)(2,1)S(1)} %get-tuple-element.15), channel_id=1, source_target_pairs={{8,16},{16,8},{9,17},{17,9},{10,18},{18,10},{11,19},{19,11},{12,20... | collective-permute-start | bytes 786440 | tf_op jit(solution)/shard_map/ppermute | solution.py:67
  5.1 1.6 %collective-permute-start.2 = (bf16[256,128]{1,0:T(8,128)(2,1)S(1)}, bf16[256,128]{1,0:T(8,128)(2,1)S(1)}, u32[]{:S(2)}, u32[]{:S(2)}) collective-permute-start(bf16[256,128]{1,0:T(8,128)(2,1)S(1)} %get-tuple-element.16), channel_id=1, source_target_pairs={{0,1},{1,0},{2,3},{3,2},{4,5},{5,4},{6,7},{7,6},{8,9},{9,8},{10,11... | collective-permute-start | bytes 196616 | tf_op jit(solution)/shard_map/ppermute | solution.py:67
  6.6 0.4 %collective-permute-start.3 = (bf16[16,512]{1,0:T(8,128)(2,1)S(1)}, bf16[16,512]{1,0:T(8,128)(2,1)S(1)}, u32[]{:S(2)}, u32[]{:S(2)}) collective-permute-start(bf16[16,512]{1,0:T(8,128)(2,1)S(1)} %get-tuple-element.17), channel_id=1, source_target_pairs={{0,2},{4,6},{2,0},{6,4},{1,3},{5,7},{3,1},{7,5},{8,10},{12,14},{10... | collective-permute-start | bytes 49160 | tf_op jit(solution)/shard_map/ppermute | solution.py:67
  7.1 4.6 %collective-permute-start.4 = (bf16[16,512]{1,0:T(8,128)(2,1)S(1)}, bf16[16,512]{1,0:T(8,128)(2,1)S(1)}, u32[]{:S(2)}, u32[]{:S(2)}) collective-permute-start(bf16[16,512]{1,0:T(8,128)(2,1)S(1)} %get-tuple-element.18), channel_id=1, source_target_pairs={{2,4},{4,2},{3,5},{5,3},{10,12},{12,10},{11,13},{13,11},{18,20},{2... | collective-permute-start | bytes 49160 | tf_op jit(solution)/shard_map/ppermute | solution.py:67
  11.7 0.0 collective-permute-done.2.refs_7_
  11.7 0.0 collective-permute-done.refs_5_
  11.7 0.0 collective-permute-done.1.refs_6_
  11.7 0.0 copy-done
  11.7 0.0 copy-done.1
  11.8 7.1 %shard_map.110.refs_10_ = f32[2,4,64,512]{3,2,1,0:T(8,128)S(1)} custom-call(bf16[128,208]{1,0:T(8,128)(2,1)S(1)} %copy-done, f32[24,16]{1,0:T(8,128)S(1)} %copy-done.1, f32[3,16]{1,0:T(4,128)S(1)} %copy-done.2, f32[1,16]{1,0:T(1,128)S(1)} %bitcast.4, bf16[16,256,512]{2,1,0:T(8,128)(2,1)S(1)} %get-tuple-element.13.refs_4_, ...), custom_call_target="tpu_custom_call" | custom-call | tf_op jit(solution)/shard_map/pallas_call | solution.py:362
  18.8 0.0 collective-permute-done.3.refs_8_
  18.8 0.0 collective-permute-done.4.refs_9_
  18.8 2.6 %shard_map.111 = f32[2,4,64,512]{3,2,1,0:T(8,128)S(1)} custom-call(bf16[128,208]{1,0:T(8,128)(2,1)S(1)} %copy-done, f32[24,16]{1,0:T(8,128)S(1)} %copy-done.1, f32[3,16]{1,0:T(4,128)S(1)} %copy-done.2, f32[1,16]{1,0:T(1,128)S(1)} %bitcast.5, bf16[16,256,512]{2,1,0:T(8,128)(2,1)S(1)} %get-tuple-element.13.refs_4_, ...), custom_call_target="tpu_custom_call", output_to_operand_aliasing={{}: (10, {})} | custom-call | tf_op jit(solution)/shard_map/pallas_call | solution.py:362
  21.5 0.1 collective-permute-start.5
  21.6 4.9 %shard_map.112.own_ref = f32[1,4,64,512]{3,2,1,0:T(8,128)S(1)} custom-call(bf16[128,208]{1,0:T(8,128)(2,1)S(1)} %copy-done, f32[24,16]{1,0:T(8,128)S(1)} %copy-done.1, f32[3,16]{1,0:T(4,128)S(1)} %copy-done.2, f32[1,16]{1,0:T(1,128)S(1)} %bitcast.6, bf16[16,256,512]{2,1,0:T(8,128)(2,1)S(1)} %get-tuple-element.13.refs_4_, ...), custom_call_target="tpu_custom_call" | custom-call | tf_op jit(solution)/shard_map/pallas_call | solution.py:362
  26.5 0.0 collective-permute-done.5.other_ref
  26.5 0.1 shard_map.113
  26.6 0.8 %collective-permute-start.6 = (bf16[4,64,512]{2,1,0:T(8,128)(2,1)S(1)}, bf16[4,64,512]{2,1,0:T(8,128)(2,1)S(1)}, u32[]{:S(2)}, u32[]{:S(2)}) collective-permute-start(bf16[4,64,512]{2,1,0:T(8,128)(2,1)S(1)} %shard_map.113), channel_id=1, source_target_pairs={{0,16},{8,24},{16,0},{24,8},{1,17},{9,25},{17,1},{25,9},{2,18},{10... | collective-permute-start | bytes 786440 | tf_op jit(solution)/shard_map/ppermute | solution.py:449
  27.4 4.8 %shard_map.114.own_ref = f32[1,4,64,512]{3,2,1,0:T(8,128)S(1)} custom-call(bf16[128,208]{1,0:T(8,128)(2,1)S(1)} %copy-done, f32[24,16]{1,0:T(8,128)S(1)} %copy-done.1, f32[3,16]{1,0:T(4,128)S(1)} %copy-done.2, f32[1,16]{1,0:T(1,128)S(1)} %bitcast.7, bf16[16,256,512]{2,1,0:T(8,128)(2,1)S(1)} %get-tuple-element.13.refs_4_, ...), custom_call_target="tpu_custom_call" | custom-call | tf_op jit(solution)/shard_map/pallas_call | solution.py:362
  32.2 3.2 %collective-permute-done.6.code_ref = bf16[4,64,512]{2,1,0:T(8,128)(2,1)S(1)} collective-permute-done((bf16[4,64,512]{2,1,0:T(8,128)(2,1)S(1)}, bf16[4,64,512]{2,1,0:T(8,128)(2,1)S(1)}, u32[]{:S(2)}, u32[]{:S(2)}) %collective-permute-start.6) | collective-permute-done | bytes 262176 | tf_op jit(solution)/shard_map/ppermute | solution.py:449
  35.4 0.9 %shard_map.115 = f32[4,64,512]{2,1,0:T(8,128)} custom-call(f32[1,4,64,512]{3,2,1,0:T(8,128)S(1)} %shard_map.114.own_ref, f32[2,4,64,512]{3,2,1,0:T(8,128)S(1)} %collective-permute-done.5.other_ref, bf16[4,64,512]{2,1,0:T(8,128)(2,1)S(1)} %collective-permute-done.6.code_ref), custom_call_target="tpu_custom_call" | custom-call | tf_op jit(solution)/shard_map/pallas_call | solution.py:426
  (5 shorter events, 0.0 us)
Async XLA Ops:
  0.0 11.7 %copy-start = (bf16[128,208]{1,0:T(8,128)(2,1)S(1)}, bf16[128,208]{1,0:T(8,128)(2,1)}, u32[]{:S(2)}) copy-start(bf16[128,208]{1,0:T(8,128)(2,1)} %constant.4.clone.refs_0_) | copy-start | bytes 159748
  0.0 11.7 %copy-start.1 = (f32[24,16]{1,0:T(8,128)S(1)}, f32[24,16]{1,0:T(8,128)}, u32[]{:S(2)}) copy-start(f32[24,16]{1,0:T(8,128)} %constant.5.clone.refs_1_) | copy-start | bytes 4612
  0.0 11.7 %copy-start.3 = (f32[16]{0:T(128)S(1)}, f32[16]{0:T(128)}, u32[]{:S(2)}) copy-start(f32[16]{0:T(128)} %param.13) | copy-start | bytes 196
  0.0 11.7 %copy-start.2 = (f32[3,16]{1,0:T(4,128)S(1)}, f32[3,16]{1,0:T(4,128)}, u32[]{:S(2)}) copy-start(f32[3,16]{1,0:T(4,128)} %refs_2_.7) | copy-start | bytes 580
  2.5 9.2 %collective-permute-start = (bf16[256,512]{1,0:T(8,128)(2,1)S(1)}, bf16[256,512]{1,0:T(8,128)(2,1)S(1)}, u32[]{:S(2)}, u32[]{:S(2)}) collective-permute-start(bf16[256,512]{1,0:T(8,128)(2,1)S(1)} %get-tuple-element.14), channel_id=1, source_target_pairs={{0,8},{16,24},{8,0},{24,16},{1,9},{17,25},{9,1},{25,17},{2,10},{18... | collective-permute-start | bytes 786440 | tf_op jit(solution)/shard_map/ppermute | solution.py:67
  2.6 9.1 %collective-permute-start.1 = (bf16[256,512]{1,0:T(8,128)(2,1)S(1)}, bf16[256,512]{1,0:T(8,128)(2,1)S(1)}, u32[]{:S(2)}, u32[]{:S(2)}) collective-permute-start(bf16[256,512]{1,0:T(8,128)(2,1)S(1)} %get-tuple-element.15), channel_id=1, source_target_pairs={{8,16},{16,8},{9,17},{17,9},{10,18},{18,10},{11,19},{19,11},{12,20... | collective-permute-start | bytes 786440 | tf_op jit(solution)/shard_map/ppermute | solution.py:67
  5.1 6.6 %collective-permute-start.2 = (bf16[256,128]{1,0:T(8,128)(2,1)S(1)}, bf16[256,128]{1,0:T(8,128)(2,1)S(1)}, u32[]{:S(2)}, u32[]{:S(2)}) collective-permute-start(bf16[256,128]{1,0:T(8,128)(2,1)S(1)} %get-tuple-element.16), channel_id=1, source_target_pairs={{0,1},{1,0},{2,3},{3,2},{4,5},{5,4},{6,7},{7,6},{8,9},{9,8},{10,11... | collective-permute-start | bytes 196616 | tf_op jit(solution)/shard_map/ppermute | solution.py:67
  6.6 12.2 %collective-permute-start.3 = (bf16[16,512]{1,0:T(8,128)(2,1)S(1)}, bf16[16,512]{1,0:T(8,128)(2,1)S(1)}, u32[]{:S(2)}, u32[]{:S(2)}) collective-permute-start(bf16[16,512]{1,0:T(8,128)(2,1)S(1)} %get-tuple-element.17), channel_id=1, source_target_pairs={{0,2},{4,6},{2,0},{6,4},{1,3},{5,7},{3,1},{7,5},{8,10},{12,14},{10... | collective-permute-start | bytes 49160 | tf_op jit(solution)/shard_map/ppermute | solution.py:67
  7.1 11.8 %collective-permute-start.4 = (bf16[16,512]{1,0:T(8,128)(2,1)S(1)}, bf16[16,512]{1,0:T(8,128)(2,1)S(1)}, u32[]{:S(2)}, u32[]{:S(2)}) collective-permute-start(bf16[16,512]{1,0:T(8,128)(2,1)S(1)} %get-tuple-element.18), channel_id=1, source_target_pairs={{2,4},{4,2},{3,5},{5,3},{10,12},{12,10},{11,13},{13,11},{18,20},{2... | collective-permute-start | bytes 49160 | tf_op jit(solution)/shard_map/ppermute | solution.py:67
  21.5 5.0 %collective-permute-start.5 = (f32[2,4,64,512]{3,2,1,0:T(8,128)S(1)}, f32[2,4,64,512]{3,2,1,0:T(8,128)S(1)}, u32[]{:S(2)}, u32[]{:S(2)}) collective-permute-start(f32[2,4,64,512]{3,2,1,0:T(8,128)S(1)} %shard_map.111), channel_id=1, source_target_pairs={{0,8},{8,0},{16,24},{24,16},{1,9},{9,1},{17,25},{25,17},{2,10},{10... | collective-permute-start | bytes 3145736 | tf_op jit(solution)/shard_map/ppermute | solution.py:449
  26.6 8.8 %collective-permute-start.6 = (bf16[4,64,512]{2,1,0:T(8,128)(2,1)S(1)}, bf16[4,64,512]{2,1,0:T(8,128)(2,1)S(1)}, u32[]{:S(2)}, u32[]{:S(2)}) collective-permute-start(bf16[4,64,512]{2,1,0:T(8,128)(2,1)S(1)} %shard_map.113), channel_id=1, source_target_pairs={{0,16},{8,24},{16,0},{24,8},{1,17},{9,25},{17,1},{25,9},{2,18},{10... | collective-permute-start | bytes 786440 | tf_op jit(solution)/shard_map/ppermute | solution.py:449

commit v8 on v7

--- a/solution.py
+++ b/solution.py
@@ -86,58 +86,47 @@
     return [lax.axis_index(axis) & 1 for axis in AXES]
 
 
-def prepare_kernel(
-    volume_ref, cells_ref, depth_outs, row_outs, column_outs, arrived
-):
-    slices, height, width = cells_ref.shape
+def prepare_kernel(volume_ref, depth_outs, row_outs, column_outs, lines_ref, columns_ref, arrived):
+    slices, height, width = volume_ref.shape
     odd = parities()
-    chunks = arrived.shape[0]
-    size = slices // chunks
-    copies = [
-        pltpu.make_async_copy(
-            volume_ref.at[pl.ds(chunk * size, size)],
-            cells_ref.at[pl.ds(chunk * size, size)],
-            arrived.at[chunk],
-        )
-        for chunk in range(chunks)
-    ]
-    for copy in copies:
-        copy.start()
-    lane = lax.broadcasted_iota(jnp.int16, (height, LANES), 1)
-    row = lax.broadcasted_iota(jnp.int16, (slices, width), 0)
-    lines = [jnp.zeros((slices, width), cells_ref.dtype)] * len(row_outs)
-    for chunk, copy in enumerate(copies):
-        copy.wait()
-        here = range(chunk * size, (chunk + 1) * size)
-        for turn in range(len(row_outs)):
-            is_first = odd[1] == 1 - turn
-            for z in here:
-                line = jnp.where(is_first, cells_ref[z, :1], cells_ref[z, height - 1 :])
-                lines[turn] = jnp.where(
-                    row == z, jnp.broadcast_to(line, (slices, width)), lines[turn]
-                )
-
-        def columns(turn, column, source, shift):
-            found = (
-                column_outs[turn][...] if chunk else jnp.zeros((height, LANES), cells_ref.dtype)
-            )
-            for z in here:
-                target = (2 * z + shift) % LANES
-                cells = cells_ref[z, :, pl.ds(column, LANES)]
-                moved = pltpu.roll(cells, (target - source) % LANES, 1)
-                found = jnp.where(lane == target, moved, found)
-            column_outs[turn][...] = found
-
-        for turn in range(len(column_outs)):
-            pl.when(odd[2] == 1 - turn)(functools.partial(columns, turn, 0, 0, -1))
-            pl.when(odd[2] == turn)(
-                functools.partial(columns, turn, width - LANES, LANES - 1, 0)
-            )
+    copies = {}
+    for turn in range(len(column_outs)):
+        start = pl.multiple_of(jnp.where(odd[2] == 1 - turn, 0, width - LANES), LANES)
+        copies[2, turn] = (volume_ref.at[:, :, pl.ds(start, LANES)], columns_ref.at[turn])
     for turn in range(len(row_outs)):
-        row_outs[turn][...] = lines[turn]
+        start = pl.multiple_of(jnp.where(odd[1] == 1 - turn, 0, height - PACK), PACK)
+        copies[1, turn] = (volume_ref.at[:, pl.ds(start, PACK), :], lines_ref.at[turn])
     for turn in range(len(depth_outs)):
         face = jnp.where(odd[0] == 1 - turn, 0, slices - 1)
-        depth_outs[turn][...] = cells_ref[face]
+        copies[0, turn] = (volume_ref.at[face], depth_outs[turn])
+    for i, (key, pair) in enumerate(copies.items()):
+        copies[key] = pltpu.make_async_copy(*pair, arrived.at[i])
+        copies[key].start()
+    row = lax.broadcasted_iota(jnp.int16, (slices, width), 0)
+    lane = lax.broadcasted_iota(jnp.int16, (height, LANES), 1)
+
+    def columns(turn, source, shift):
+        found = jnp.zeros((height, LANES), column_outs[turn].dtype)
+        for z in range(slices):
+            target = (2 * z + shift) % LANES
+            moved = pltpu.roll(columns_ref[turn, z], (target - source) % LANES, 1)
+            found = jnp.where(lane == target, moved, found)
+        column_outs[turn][...] = found
+
+    for turn in range(len(column_outs)):
+        copies[2, turn].wait()
+        pl.when(odd[2] == 1 - turn)(functools.partial(columns, turn, 0, -1))
+        pl.when(odd[2] == turn)(functools.partial(columns, turn, LANES - 1, 0))
+    for turn in range(len(row_outs)):
+        copies[1, turn].wait()
+        is_first = odd[1] == 1 - turn
+        lines = jnp.zeros((slices, width), row_outs[turn].dtype)
+        for z in range(slices):
+            line = jnp.where(is_first, lines_ref[turn, z, :1], lines_ref[turn, z, PACK - 1 :])
+            lines = jnp.where(row == z, jnp.broadcast_to(line, lines.shape), lines)
+        row_outs[turn][...] = lines
+    for turn in range(len(depth_outs)):
+        copies[0, turn].wait()
 
 
 def prepare(volume):
@@ -145,7 +134,7 @@
     assert 2 * slices <= LANES
     shapes = [(height, width), (slices, width), (height, LANES)]
     turns = [2 if lax.axis_size(axis) > 2 else 1 for axis in AXES]
-    out_shape = [jax.ShapeDtypeStruct(volume.shape, volume.dtype)] + [
+    out_shape = [
         [jax.ShapeDtypeStruct(shape, volume.dtype)] * count for shape, count in zip(shapes, turns)
     ]
     return pl.pallas_call(
@@ -153,7 +142,11 @@
         in_specs=[pl.BlockSpec(memory_space=pltpu.HBM)],
         out_specs=jax.tree.map(lambda _: VECTORS, out_shape),
         out_shape=out_shape,
-        scratch_shapes=[pltpu.SemaphoreType.DMA((4 if slices % 4 == 0 else 1,))],
+        scratch_shapes=[
+            pltpu.VMEM((turns[1], slices, PACK, width), volume.dtype),
+            pltpu.VMEM((turns[2], slices, height, LANES), volume.dtype),
+            pltpu.SemaphoreType.DMA((sum(turns),)),
+        ],
         compiler_params=pltpu.CompilerParams(vmem_limit_bytes=24 * 2**20),
     )(volume)
 
@@ -487,8 +480,7 @@
     def edge_tile(i):
         return missing_tile(), tile_at(missing_tile(), (3, 1))
 
-    volume = pltpu.with_memory_space_constraint(volume, pltpu.HBM)
-    cells, *faces = prepare(volume)
+    faces = prepare(pltpu.with_memory_space_constraint(volume, pltpu.HBM))
     depth, lines, ends = (exchange(face, axis) for face, axis in zip(faces, AXES))
     depth, lines = (
         found if len(found) == 2 else found + [jnp.zeros_like(found[0])] for found in (depth, lines)
@@ -500,7 +492,7 @@
         if after is not None:
             here, _ = lax.optimization_barrier((ends, after))
         return march(
-            cells,
+            volume,
             (depth, here, lines if with_lines else None),
             tiles,
             tile_count,

time: 36.5 us -> 37.4 us (1.025)
  local copies, waits for them, and re-layouts: 0.02 us -> 1.55 us
  Pallas kernels: 22.9 us -> 22.3 us
    unnamed x8 -> x10, local copies, waits for them, and re-layouts: 0.02 us -> 1.55 us
    pallas_call x1, Pallas kernels: 2.46 us -> 1.88 us  [prepare(): pl.pallas_call(prepare_kernel, in_specs=[pl.BlockSpec(memory_space=pltpu....]
  transfers between devices with their start and end apart: 7 -> 7, of which waited for: 1 -> 1; matrix products, arithmetic and copies ran while one was open for 0% -> 0% of each run, Pallas kernels for 46% -> 45%
where the time goes in v8:
time: 37.4 us; the launch traced here: 37.2 us
  Pallas kernels  22.3 us (60%)
  starting transfers between devices  9.99 us (27%)
  waiting for transfers between devices  3.19 us (9%)
  local copies, waits for them, and re-layouts  1.55 us (4%)
    pallas_call x4, Pallas kernels, march(): pl.pallas_call(functools.partial(march_kernel, tiles=tiles, count=count,...  19.3 us
    ppermute x5, starting transfers between devices, exchange(): lax.ppermute(face, axis, both)  9.18 us
    ppermute x2, waiting for transfers between devices, from_partner(): return lax.ppermute(value, axis, pairs)  3.18 us
    pallas_call x1, Pallas kernels, prepare(): pl.pallas_call(prepare_kernel, in_specs=[pl.BlockSpec(memory_space=pltpu....  1.88 us
    unnamed x10, local copies, waits for them, and re-layouts  1.55 us
    pallas_call x1, Pallas kernels, merge_last(): pl.pallas_call(functools.partial(last_kernel, finish=finish), grid=(steps...  0.93 us
    ppermute x2, starting transfers between devices, from_partner(): return lax.ppermute(value, axis, pairs)  0.81 us
  transfers between devices with their start and end apart: 7, of which 1 were waited for; matrix products, arithmetic and copies ran while one was open for 0% of the time, Pallas kernels for 45%

profile of v8, /device:TPU:12, one launch (start us, length us, event | category | flops | bytes accessed | tf_op | source)
XLA Modules:
  0.0 37.2 jit_solution(3982969544007366992)
XLA Ops:
  0.0 1.9 %shard_map.109 = (bf16[256,512]{1,0:T(8,128)(2,1)S(1)}, bf16[256,512]{1,0:T(8,128)(2,1)S(1)}, bf16[16,512]{1,0:T(8,128)(2,1)S(1)}, bf16[16,512]{1,0:T(8,128)(2,1)S(1)}, bf16[256,128]{1,0:T(8,128)(2,1)S(1)}) custom-call(bf16[16,256,512]{2,1,0:T(8,128)(2,1)} %refs_4_.7), custom_call_target="tpu_custom_call" | custom-call | tf_op jit(solution)/shard_map/pallas_call | solution.py:140
  1.9 0.1 collective-permute-start
  2.0 2.5 %collective-permute-start.1 = (bf16[256,512]{1,0:T(8,128)(2,1)S(1)}, bf16[256,512]{1,0:T(8,128)(2,1)S(1)}, u32[]{:S(2)}, u32[]{:S(2)}) collective-permute-start(bf16[256,512]{1,0:T(8,128)(2,1)S(1)} %get-tuple-element.13), channel_id=1, source_target_pairs={{8,16},{16,8},{9,17},{17,9},{10,18},{18,10},{11,19},{19,11},{12,20... | collective-permute-start | bytes 786440 | tf_op jit(solution)/shard_map/ppermute | solution.py:67
  4.5 1.6 %collective-permute-start.2 = (bf16[256,128]{1,0:T(8,128)(2,1)S(1)}, bf16[256,128]{1,0:T(8,128)(2,1)S(1)}, u32[]{:S(2)}, u32[]{:S(2)}) collective-permute-start(bf16[256,128]{1,0:T(8,128)(2,1)S(1)} %get-tuple-element.14), channel_id=1, source_target_pairs={{0,1},{1,0},{2,3},{3,2},{4,5},{5,4},{6,7},{7,6},{8,9},{9,8},{10,11... | collective-permute-start | bytes 196616 | tf_op jit(solution)/shard_map/ppermute | solution.py:67
  6.0 0.4 %collective-permute-start.3 = (bf16[16,512]{1,0:T(8,128)(2,1)S(1)}, bf16[16,512]{1,0:T(8,128)(2,1)S(1)}, u32[]{:S(2)}, u32[]{:S(2)}) collective-permute-start(bf16[16,512]{1,0:T(8,128)(2,1)S(1)} %get-tuple-element.15), channel_id=1, source_target_pairs={{0,2},{4,6},{2,0},{6,4},{1,3},{5,7},{3,1},{7,5},{8,10},{12,14},{10... | collective-permute-start | bytes 49160 | tf_op jit(solution)/shard_map/ppermute | solution.py:67
  6.5 4.6 %collective-permute-start.4 = (bf16[16,512]{1,0:T(8,128)(2,1)S(1)}, bf16[16,512]{1,0:T(8,128)(2,1)S(1)}, u32[]{:S(2)}, u32[]{:S(2)}) collective-permute-start(bf16[16,512]{1,0:T(8,128)(2,1)S(1)} %get-tuple-element.16), channel_id=1, source_target_pairs={{2,4},{4,2},{3,5},{5,3},{10,12},{12,10},{11,13},{13,11},{18,20},{2... | collective-permute-start | bytes 49160 | tf_op jit(solution)/shard_map/ppermute | solution.py:67
  11.1 0.0 collective-permute-done.2.refs_7_
  11.1 0.0 collective-permute-done.refs_5_
  11.1 0.0 collective-permute-done.1.refs_6_
  11.2 0.0 copy-start.1
  11.2 0.8 %copy-done.1 = bf16[128,208]{1,0:T(8,128)(2,1)S(1)} copy-done((bf16[128,208]{1,0:T(8,128)(2,1)S(1)}, bf16[128,208]{1,0:T(8,128)(2,1)}, u32[]{:S(2)}) %copy-start.1) | copy-done | bytes 53272
  12.0 0.7 %copy-done.2 = f32[24,16]{1,0:T(8,128)S(1)} copy-done((f32[24,16]{1,0:T(8,128)S(1)}, f32[24,16]{1,0:T(8,128)}, u32[]{:S(2)}) %copy-start.2) | copy-done | bytes 1560
  12.7 7.0 %shard_map.110.refs_10_ = f32[2,4,64,512]{3,2,1,0:T(8,128)S(1)} custom-call(bf16[128,208]{1,0:T(8,128)(2,1)S(1)} %copy-done.1, f32[24,16]{1,0:T(8,128)S(1)} %copy-done.2, f32[3,16]{1,0:T(4,128)S(1)} %copy-done.3, f32[1,16]{1,0:T(1,128)S(1)} %bitcast.4, bf16[16,256,512]{2,1,0:T(8,128)(2,1)S(1)} %copy-done, bf16[256,512]{1,0:T(8,128)(2,1)S(1)} %collective-permute-done.refs_5_, ...), custom_call_target="tpu_custom_call" | custom-call | tf_op jit(solution)/shard_map/pallas_call | solution.py:355
  19.7 0.0 collective-permute-done.3.refs_8_
  19.7 0.0 collective-permute-done.4.refs_9_
  19.7 2.6 %shard_map.111 = f32[2,4,64,512]{3,2,1,0:T(8,128)S(1)} custom-call(bf16[128,208]{1,0:T(8,128)(2,1)S(1)} %copy-done.1, f32[24,16]{1,0:T(8,128)S(1)} %copy-done.2, f32[3,16]{1,0:T(4,128)S(1)} %copy-done.3, f32[1,16]{1,0:T(1,128)S(1)} %bitcast.5, bf16[16,256,512]{2,1,0:T(8,128)(2,1)S(1)} %copy-done, ...), custom_call_target="tpu_custom_call", output_to_operand_aliasing={{}: (10, {})} | custom-call | tf_op jit(solution)/shard_map/pallas_call | solution.py:355
  22.3 0.1 collective-permute-start.5
  22.4 4.9 %shard_map.112.own_ref = f32[1,4,64,512]{3,2,1,0:T(8,128)S(1)} custom-call(bf16[128,208]{1,0:T(8,128)(2,1)S(1)} %copy-done.1, f32[24,16]{1,0:T(8,128)S(1)} %copy-done.2, f32[3,16]{1,0:T(4,128)S(1)} %copy-done.3, f32[1,16]{1,0:T(1,128)S(1)} %bitcast.6, bf16[16,256,512]{2,1,0:T(8,128)(2,1)S(1)} %copy-done, bf16[256,512]{1,0:T(8,128)(2,1)S(1)} %collective-permute-done.refs_5_, ...), custom_call_target="tpu_custom_call" | custom-call | tf_op jit(solution)/shard_map/pallas_call | solution.py:355
  27.3 0.0 collective-permute-done.5.other_ref
  27.3 0.1 shard_map.113
  27.5 0.7 %collective-permute-start.6 = (bf16[4,64,512]{2,1,0:T(8,128)(2,1)S(1)}, bf16[4,64,512]{2,1,0:T(8,128)(2,1)S(1)}, u32[]{:S(2)}, u32[]{:S(2)}) collective-permute-start(bf16[4,64,512]{2,1,0:T(8,128)(2,1)S(1)} %shard_map.113), channel_id=1, source_target_pairs={{0,16},{8,24},{16,0},{24,8},{1,17},{9,25},{17,1},{25,9},{2,18},{10... | collective-permute-start | bytes 786440 | tf_op jit(solution)/shard_map/ppermute | solution.py:442
  28.2 4.8 %shard_map.114.own_ref = f32[1,4,64,512]{3,2,1,0:T(8,128)S(1)} custom-call(bf16[128,208]{1,0:T(8,128)(2,1)S(1)} %copy-done.1, f32[24,16]{1,0:T(8,128)S(1)} %copy-done.2, f32[3,16]{1,0:T(4,128)S(1)} %copy-done.3, f32[1,16]{1,0:T(1,128)S(1)} %bitcast.7, bf16[16,256,512]{2,1,0:T(8,128)(2,1)S(1)} %copy-done, bf16[256,512]{1,0:T(8,128)(2,1)S(1)} %collective-permute-done.refs_5_, ...), custom_call_target="tpu_custom_call" | custom-call | tf_op jit(solution)/shard_map/pallas_call | solution.py:355
  33.1 3.2 %collective-permute-done.6.code_ref = bf16[4,64,512]{2,1,0:T(8,128)(2,1)S(1)} collective-permute-done((bf16[4,64,512]{2,1,0:T(8,128)(2,1)S(1)}, bf16[4,64,512]{2,1,0:T(8,128)(2,1)S(1)}, u32[]{:S(2)}, u32[]{:S(2)}) %collective-permute-start.6) | collective-permute-done | bytes 262176 | tf_op jit(solution)/shard_map/ppermute | solution.py:442
  36.2 0.9 %shard_map.115 = f32[4,64,512]{2,1,0:T(8,128)} custom-call(f32[1,4,64,512]{3,2,1,0:T(8,128)S(1)} %shard_map.114.own_ref, f32[2,4,64,512]{3,2,1,0:T(8,128)S(1)} %collective-permute-done.5.other_ref, bf16[4,64,512]{2,1,0:T(8,128)(2,1)S(1)} %collective-permute-done.6.code_ref), custom_call_target="tpu_custom_call" | custom-call | tf_op jit(solution)/shard_map/pallas_call | solution.py:419
  (7 shorter events, 0.0 us)
Async XLA Ops:
  0.0 11.1 %copy-start = (bf16[16,256,512]{2,1,0:T(8,128)(2,1)S(1)}, bf16[16,256,512]{2,1,0:T(8,128)(2,1)}, u32[]{:S(2)}) copy-start(bf16[16,256,512]{2,1,0:T(8,128)(2,1)} %refs_4_.7) | copy-start | bytes 12582916
  0.0 11.1 %copy-start.4 = (f32[16]{0:T(128)S(1)}, f32[16]{0:T(128)}, u32[]{:S(2)}) copy-start(f32[16]{0:T(128)} %param.13) | copy-start | bytes 196
  0.0 11.2 %copy-start.3 = (f32[3,16]{1,0:T(4,128)S(1)}, f32[3,16]{1,0:T(4,128)}, u32[]{:S(2)}) copy-start(f32[3,16]{1,0:T(4,128)} %refs_2_.7) | copy-start | bytes 580
  1.9 9.2 %collective-permute-start = (bf16[256,512]{1,0:T(8,128)(2,1)S(1)}, bf16[256,512]{1,0:T(8,128)(2,1)S(1)}, u32[]{:S(2)}, u32[]{:S(2)}) collective-permute-start(bf16[256,512]{1,0:T(8,128)(2,1)S(1)} %get-tuple-element.12), channel_id=1, source_target_pairs={{0,8},{16,24},{8,0},{24,16},{1,9},{17,25},{9,1},{25,17},{2,10},{18... | collective-permute-start | bytes 786440 | tf_op jit(solution)/shard_map/ppermute | solution.py:67
  2.0 9.2 %collective-permute-start.1 = (bf16[256,512]{1,0:T(8,128)(2,1)S(1)}, bf16[256,512]{1,0:T(8,128)(2,1)S(1)}, u32[]{:S(2)}, u32[]{:S(2)}) collective-permute-start(bf16[256,512]{1,0:T(8,128)(2,1)S(1)} %get-tuple-element.13), channel_id=1, source_target_pairs={{8,16},{16,8},{9,17},{17,9},{10,18},{18,10},{11,19},{19,11},{12,20... | collective-permute-start | bytes 786440 | tf_op jit(solution)/shard_map/ppermute | solution.py:67
  4.5 6.6 %collective-permute-start.2 = (bf16[256,128]{1,0:T(8,128)(2,1)S(1)}, bf16[256,128]{1,0:T(8,128)(2,1)S(1)}, u32[]{:S(2)}, u32[]{:S(2)}) collective-permute-start(bf16[256,128]{1,0:T(8,128)(2,1)S(1)} %get-tuple-element.14), channel_id=1, source_target_pairs={{0,1},{1,0},{2,3},{3,2},{4,5},{5,4},{6,7},{7,6},{8,9},{9,8},{10,11... | collective-permute-start | bytes 196616 | tf_op jit(solution)/shard_map/ppermute | solution.py:67
  6.0 13.7 %collective-permute-start.3 = (bf16[16,512]{1,0:T(8,128)(2,1)S(1)}, bf16[16,512]{1,0:T(8,128)(2,1)S(1)}, u32[]{:S(2)}, u32[]{:S(2)}) collective-permute-start(bf16[16,512]{1,0:T(8,128)(2,1)S(1)} %get-tuple-element.15), channel_id=1, source_target_pairs={{0,2},{4,6},{2,0},{6,4},{1,3},{5,7},{3,1},{7,5},{8,10},{12,14},{10... | collective-permute-start | bytes 49160 | tf_op jit(solution)/shard_map/ppermute | solution.py:67
  6.5 13.2 %collective-permute-start.4 = (bf16[16,512]{1,0:T(8,128)(2,1)S(1)}, bf16[16,512]{1,0:T(8,128)(2,1)S(1)}, u32[]{:S(2)}, u32[]{:S(2)}) collective-permute-start(bf16[16,512]{1,0:T(8,128)(2,1)S(1)} %get-tuple-element.16), channel_id=1, source_target_pairs={{2,4},{4,2},{3,5},{5,3},{10,12},{12,10},{11,13},{13,11},{18,20},{2... | collective-permute-start | bytes 49160 | tf_op jit(solution)/shard_map/ppermute | solution.py:67
  11.2 0.8 %copy-start.1 = (bf16[128,208]{1,0:T(8,128)(2,1)S(1)}, bf16[128,208]{1,0:T(8,128)(2,1)}, u32[]{:S(2)}) copy-start(bf16[128,208]{1,0:T(8,128)(2,1)} %constant.4.clone.refs_0_) | copy-start | bytes 159748
  12.0 0.7 %copy-start.2 = (f32[24,16]{1,0:T(8,128)S(1)}, f32[24,16]{1,0:T(8,128)}, u32[]{:S(2)}) copy-start(f32[24,16]{1,0:T(8,128)} %constant.5.clone.refs_1_) | copy-start | bytes 4612
  22.3 5.0 %collective-permute-start.5 = (f32[2,4,64,512]{3,2,1,0:T(8,128)S(1)}, f32[2,4,64,512]{3,2,1,0:T(8,128)S(1)}, u32[]{:S(2)}, u32[]{:S(2)}) collective-permute-start(f32[2,4,64,512]{3,2,1,0:T(8,128)S(1)} %shard_map.111), channel_id=1, source_target_pairs={{0,8},{8,0},{16,24},{24,16},{1,9},{9,1},{17,25},{25,17},{2,10},{10... | collective-permute-start | bytes 3145736 | tf_op jit(solution)/shard_map/ppermute | solution.py:442
  27.5 8.7 %collective-permute-start.6 = (bf16[4,64,512]{2,1,0:T(8,128)(2,1)S(1)}, bf16[4,64,512]{2,1,0:T(8,128)(2,1)S(1)}, u32[]{:S(2)}, u32[]{:S(2)}) collective-permute-start(bf16[4,64,512]{2,1,0:T(8,128)(2,1)S(1)} %shard_map.113), channel_id=1, source_target_pairs={{0,16},{8,24},{16,0},{24,8},{1,17},{9,25},{17,1},{25,9},{2,18},{10... | collective-permute-start | bytes 786440 | tf_op jit(solution)/shard_map/ppermute | solution.py:442

commit v9 on v8

--- a/solution.py
+++ b/solution.py
@@ -68,25 +68,30 @@
     return received
 
 
-def segment_lines(knot_count):
-    segments = (knot_count + 1) // 2
-    rows = -(-segments // HALF) * HALF
-    lines = np.zeros((3, rows, knot_count), np.float32)
-    for segment in range(segments):
-        left, middle, right = (min(2 * segment + i, knot_count - 1) for i in range(3))
-        lines[0, segment, middle] += 1.0
-        lines[1, segment, middle] += 2.0
-        lines[1, segment, left] -= 2.0
-        lines[2, segment, right] += 2.0
-        lines[2, segment, middle] -= 2.0
-    return lines.reshape(3 * rows, knot_count)
+def segment_lines(knot_count, first):
+    segment = first + lax.broadcasted_iota(jnp.int32, (HALF, knot_count), 0)
+    knot = lax.broadcasted_iota(jnp.int32, (HALF, knot_count), 1)
+    left, middle, right = (
+        jnp.where(knot == jnp.minimum(2 * segment + i, knot_count - 1), 1.0, 0.0) for i in range(3)
+    )
+    return middle, 2.0 * (middle - left), 2.0 * (right - middle)
 
 
 def parities():
     return [lax.axis_index(axis) & 1 for axis in AXES]
 
 
-def prepare_kernel(volume_ref, depth_outs, row_outs, column_outs, lines_ref, columns_ref, arrived):
+def prepare_kernel(
+    volume_ref,
+    stencil_ref,
+    matrix_ref,
+    depth_outs,
+    row_outs,
+    column_outs,
+    lines_ref,
+    columns_ref,
+    arrived,
+):
     slices, height, width = volume_ref.shape
     odd = parities()
     copies = {}
@@ -99,6 +104,7 @@
     for turn in range(len(depth_outs)):
         face = jnp.where(odd[0] == 1 - turn, 0, slices - 1)
         copies[0, turn] = (volume_ref.at[face], depth_outs[turn])
+    copies[None] = (stencil_ref, matrix_ref)
     for i, (key, pair) in enumerate(copies.items()):
         copies[key] = pltpu.make_async_copy(*pair, arrived.at[i])
         copies[key].start()
@@ -127,33 +133,34 @@
         row_outs[turn][...] = lines
     for turn in range(len(depth_outs)):
         copies[0, turn].wait()
-
-
-def prepare(volume):
+    copies[None].wait()
+
+
+def prepare(volume, matrix):
     slices, height, width = volume.shape
     assert 2 * slices <= LANES
     shapes = [(height, width), (slices, width), (height, LANES)]
     turns = [2 if lax.axis_size(axis) > 2 else 1 for axis in AXES]
-    out_shape = [
+    out_shape = [jax.ShapeDtypeStruct(matrix.shape, matrix.dtype)] + [
         [jax.ShapeDtypeStruct(shape, volume.dtype)] * count for shape, count in zip(shapes, turns)
     ]
     return pl.pallas_call(
         prepare_kernel,
-        in_specs=[pl.BlockSpec(memory_space=pltpu.HBM)],
+        in_specs=[pl.BlockSpec(memory_space=pltpu.HBM)] * 2,
         out_specs=jax.tree.map(lambda _: VECTORS, out_shape),
         out_shape=out_shape,
         scratch_shapes=[
             pltpu.VMEM((turns[1], slices, PACK, width), volume.dtype),
             pltpu.VMEM((turns[2], slices, height, LANES), volume.dtype),
-            pltpu.SemaphoreType.DMA((sum(turns),)),
+            pltpu.SemaphoreType.DMA((sum(turns) + 1,)),
         ],
         compiler_params=pltpu.CompilerParams(vmem_limit_bytes=24 * 2**20),
-    )(volume)
+    )(volume, matrix)
 
 
 def march_kernel(*refs, tiles, count, tile, optical, with_lines, patch):
-    stencil_ref, lines_ref, color_ref, opacity_ref, cells_ref = refs[:5]
-    depth_refs, ends_ref, refs = refs[5:7], refs[7], refs[8:]
+    stencil_ref, color_ref, opacity_ref, cells_ref = refs[:4]
+    depth_refs, ends_ref, refs = refs[4:6], refs[6], refs[7:]
     if with_lines:
         line_refs, refs = refs[:2], refs[2:]
     if patch:
@@ -170,14 +177,19 @@
     halves = -(-knot_count // (2 * HALF))
     rest = width - LANES
     half_width = width // 2 if width % (2 * LANES) == 0 else width
-    tables = []
-    for channel in range(4):
-        knots = (
-            color_ref[channel : channel + 1] * DIFFUSE if channel < 3 else opacity_ref[...] * optical
-        )
-        values = jnp.sum(lines_ref[...] * knots, axis=1, keepdims=True)
-        for start in range(0, values.shape[0], HALF):
-            tables.append(jnp.broadcast_to(values[start : start + HALF], (HALF, LANES)))
+    tables = [None] * (12 * halves)
+    for half in range(halves):
+        for part, weights in enumerate(segment_lines(knot_count, HALF * half)):
+            for channel in range(4):
+                knots = (
+                    color_ref[channel : channel + 1] * DIFFUSE
+                    if channel < 3
+                    else opacity_ref[...] * optical
+                )
+                values = jnp.sum(weights * knots, axis=1, keepdims=True)
+                tables[(3 * channel + part) * halves + half] = jnp.broadcast_to(
+                    values, (HALF, LANES)
+                )
 
     def look_up(which, index, in_half):
         for half in range(halves):
@@ -324,7 +336,7 @@
         pass
 
 
-def march(cells, halos, tiles, count, image, transfer, depth_total, tile, partial=None):
+def march(cells, matrix, halos, tiles, count, image, transfer, depth_total, tile, partial=None):
     slices, height, width = cells.shape
     depth, ends, lines = halos
     assert slices % SLOTS == 0 and SLOTS == 2 * DEPTH
@@ -335,8 +347,7 @@
     patch = partial is not None
     scratch = [pltpu.VMEM((SLOTS, 4 * tile, width), jnp.float32)]
     operands = [
-        jnp.asarray(stencil(tile, knot_count)),
-        jnp.asarray(segment_lines(knot_count)),
+        matrix,
         tf_color,
         tf_opacity.reshape(1, knot_count),
         cells,
@@ -480,7 +491,10 @@
     def edge_tile(i):
         return missing_tile(), tile_at(missing_tile(), (3, 1))
 
-    faces = prepare(pltpu.with_memory_space_constraint(volume, pltpu.HBM))
+    matrix = jnp.asarray(stencil(tile, tf_color.shape[1]))
+    matrix, *faces = prepare(
+        *(pltpu.with_memory_space_constraint(part, pltpu.HBM) for part in (volume, matrix))
+    )
     depth, lines, ends = (exchange(face, axis) for face, axis in zip(faces, AXES))
     depth, lines = (
         found if len(found) == 2 else found + [jnp.zeros_like(found[0])] for found in (depth, lines)
@@ -493,6 +507,7 @@
             here, _ = lax.optimization_barrier((ends, after))
         return march(
             volume,
+            matrix,
             (depth, here, lines if with_lines else None),
             tiles,
             tile_count,

time: 37.4 us -> 35.5 us (0.949)
  local copies, waits for them, and re-layouts: 1.55 us -> 0.01 us
  Pallas kernels: 22.3 us -> 21.9 us
    unnamed x10 -> x6, local copies, waits for them, and re-layouts: 1.55 us -> 0.01 us
  transfers between devices with their start and end apart: 7 -> 7, of which waited for: 1 -> 1; matrix products, arithmetic and copies ran while one was open for 0% -> 0% of each run, Pallas kernels for 45% -> 46%
where the time goes in v9:
time: 35.5 us; the launch traced here: 35.3 us
  Pallas kernels  21.9 us (62%)
  starting transfers between devices  10 us (28%)
  waiting for transfers between devices  3.25 us (9%)
    pallas_call x4, Pallas kernels, march(): pl.pallas_call(functools.partial(march_kernel, tiles=tiles, count=count,...  19 us
    ppermute x5, starting transfers between devices, exchange(): lax.ppermute(face, axis, both)  9.18 us
    ppermute x2, waiting for transfers between devices, from_partner(): return lax.ppermute(value, axis, pairs)  3.24 us
    pallas_call x1, Pallas kernels, prepare(): pl.pallas_call(prepare_kernel, in_specs=[pl.BlockSpec(memory_space=pltpu....  1.89 us
    pallas_call x1, Pallas kernels, merge_last(): pl.pallas_call(functools.partial(last_kernel, finish=finish), grid=(steps...  0.93 us
    ppermute x2, starting transfers between devices, from_partner(): return lax.ppermute(value, axis, pairs)  0.82 us
  transfers between devices with their start and end apart: 7, of which 1 were waited for; matrix products, arithmetic and copies ran while one was open for 0% of the time, Pallas kernels for 46%

profile of v9, /device:TPU:12, one launch (start us, length us, event | category | flops | bytes accessed | tf_op | source)
XLA Modules:
  0.0 35.3 jit_solution(4498745565656009827)
XLA Ops:
  0.0 1.9 %shard_map.46 = (bf16[128,208]{1,0:T(8,128)(2,1)S(1)}, bf16[256,512]{1,0:T(8,128)(2,1)S(1)}, bf16[256,512]{1,0:T(8,128)(2,1)S(1)}, bf16[16,512]{1,0:T(8,128)(2,1...) custom-call(bf16[16,256,512]{2,1,0:T(8,128)(2,1)} %refs_3_.7, bf16[128,208]{1,0:T(8,128)(2,1)} %constant.2.clone.stencil_ref), custom_call_target="tpu_custom_call" | custom-call | tf_op jit(solution)/shard_map/pallas_call | solution.py:147
  1.9 0.1 collective-permute-start
  2.0 2.5 %collective-permute-start.1 = (bf16[256,512]{1,0:T(8,128)(2,1)S(1)}, bf16[256,512]{1,0:T(8,128)(2,1)S(1)}, u32[]{:S(2)}, u32[]{:S(2)}) collective-permute-start(bf16[256,512]{1,0:T(8,128)(2,1)S(1)} %get-tuple-element.15), channel_id=1, source_target_pairs={{8,16},{16,8},{9,17},{17,9},{10,18},{18,10},{11,19},{19,11},{12,20... | collective-permute-start | bytes 786440 | tf_op jit(solution)/shard_map/ppermute | solution.py:67
  4.5 1.6 %collective-permute-start.2 = (bf16[256,128]{1,0:T(8,128)(2,1)S(1)}, bf16[256,128]{1,0:T(8,128)(2,1)S(1)}, u32[]{:S(2)}, u32[]{:S(2)}) collective-permute-start(bf16[256,128]{1,0:T(8,128)(2,1)S(1)} %get-tuple-element.16), channel_id=1, source_target_pairs={{0,1},{1,0},{2,3},{3,2},{4,5},{5,4},{6,7},{7,6},{8,9},{9,8},{10,11... | collective-permute-start | bytes 196616 | tf_op jit(solution)/shard_map/ppermute | solution.py:67
  6.1 0.4 %collective-permute-start.3 = (bf16[16,512]{1,0:T(8,128)(2,1)S(1)}, bf16[16,512]{1,0:T(8,128)(2,1)S(1)}, u32[]{:S(2)}, u32[]{:S(2)}) collective-permute-start(bf16[16,512]{1,0:T(8,128)(2,1)S(1)} %get-tuple-element.17), channel_id=1, source_target_pairs={{0,2},{4,6},{2,0},{6,4},{1,3},{5,7},{3,1},{7,5},{8,10},{12,14},{10... | collective-permute-start | bytes 49160 | tf_op jit(solution)/shard_map/ppermute | solution.py:67
  6.5 4.6 %collective-permute-start.4 = (bf16[16,512]{1,0:T(8,128)(2,1)S(1)}, bf16[16,512]{1,0:T(8,128)(2,1)S(1)}, u32[]{:S(2)}, u32[]{:S(2)}) collective-permute-start(bf16[16,512]{1,0:T(8,128)(2,1)S(1)} %get-tuple-element.18), channel_id=1, source_target_pairs={{2,4},{4,2},{3,5},{5,3},{10,12},{12,10},{11,13},{13,11},{18,20},{2... | collective-permute-start | bytes 49160 | tf_op jit(solution)/shard_map/ppermute | solution.py:67
  11.1 0.0 collective-permute-done.2.refs_6_
  11.1 0.0 collective-permute-done.refs_4_
  11.1 0.0 collective-permute-done.1.refs_5_
  11.1 0.0 copy-done
  11.2 0.0 copy-done.2
  11.2 0.0 copy-done.1
  11.2 6.8 %shard_map.47.refs_9_ = f32[2,4,64,512]{3,2,1,0:T(8,128)S(1)} custom-call(bf16[128,208]{1,0:T(8,128)(2,1)S(1)} %get-tuple-element.13.refs_0_, f32[3,16]{1,0:T(4,128)S(1)} %copy-done.1, f32[1,16]{1,0:T(1,128)S(1)} %bitcast.4, bf16[16,256,512]{2,1,0:T(8,128)(2,1)S(1)} %copy-done, bf16[256,512]{1,0:T(8,128)(2,1)S(1)} %collective-permute-done.refs_4_, ...), custom_call_target="tpu_custom_call" | custom-call | tf_op jit(solution)/shard_map/pallas_call | solution.py:366
  18.0 0.0 collective-permute-done.3.refs_7_
  18.0 0.0 collective-permute-done.4.refs_8_
  18.0 2.6 %shard_map.48 = f32[2,4,64,512]{3,2,1,0:T(8,128)S(1)} custom-call(bf16[128,208]{1,0:T(8,128)(2,1)S(1)} %get-tuple-element.13.refs_0_, f32[3,16]{1,0:T(4,128)S(1)} %copy-done.1, f32[1,16]{1,0:T(1,128)S(1)} %bitcast.5, bf16[16,256,512]{2,1,0:T(8,128)(2,1)S(1)} %copy-done, ...), custom_call_target="tpu_custom_call", output_to_operand_aliasing={{}: (9, {})} | custom-call | tf_op jit(solution)/shard_map/pallas_call | solution.py:366
  20.6 0.1 collective-permute-start.5
  20.7 4.8 %shard_map.49.own_ref = f32[1,4,64,512]{3,2,1,0:T(8,128)S(1)} custom-call(bf16[128,208]{1,0:T(8,128)(2,1)S(1)} %get-tuple-element.13.refs_0_, f32[3,16]{1,0:T(4,128)S(1)} %copy-done.1, f32[1,16]{1,0:T(1,128)S(1)} %bitcast.6, bf16[16,256,512]{2,1,0:T(8,128)(2,1)S(1)} %copy-done, bf16[256,512]{1,0:T(8,128)(2,1)S(1)} %collective-permute-done.refs_4_, ...), custom_call_target="tpu_custom_call" | custom-call | tf_op jit(solution)/shard_map/pallas_call | solution.py:366
  25.5 0.0 collective-permute-done.5.other_ref
  25.5 0.1 shard_map.50
  25.7 0.7 %collective-permute-start.6 = (bf16[4,64,512]{2,1,0:T(8,128)(2,1)S(1)}, bf16[4,64,512]{2,1,0:T(8,128)(2,1)S(1)}, u32[]{:S(2)}, u32[]{:S(2)}) collective-permute-start(bf16[4,64,512]{2,1,0:T(8,128)(2,1)S(1)} %shard_map.50), channel_id=1, source_target_pairs={{0,16},{8,24},{16,0},{24,8},{1,17},{9,25},{17,1},{25,9},{2,18},{10... | collective-permute-start | bytes 786440 | tf_op jit(solution)/shard_map/ppermute | solution.py:453
  26.4 4.8 %shard_map.51.own_ref = f32[1,4,64,512]{3,2,1,0:T(8,128)S(1)} custom-call(bf16[128,208]{1,0:T(8,128)(2,1)S(1)} %get-tuple-element.13.refs_0_, f32[3,16]{1,0:T(4,128)S(1)} %copy-done.1, f32[1,16]{1,0:T(1,128)S(1)} %bitcast.7, bf16[16,256,512]{2,1,0:T(8,128)(2,1)S(1)} %copy-done, bf16[256,512]{1,0:T(8,128)(2,1)S(1)} %collective-permute-done.refs_4_, ...), custom_call_target="tpu_custom_call" | custom-call | tf_op jit(solution)/shard_map/pallas_call | solution.py:366
  31.2 3.2 %collective-permute-done.6.code_ref = bf16[4,64,512]{2,1,0:T(8,128)(2,1)S(1)} collective-permute-done((bf16[4,64,512]{2,1,0:T(8,128)(2,1)S(1)}, bf16[4,64,512]{2,1,0:T(8,128)(2,1)S(1)}, u32[]{:S(2)}, u32[]{:S(2)}) %collective-permute-start.6) | collective-permute-done | bytes 262176 | tf_op jit(solution)/shard_map/ppermute | solution.py:453
  34.4 0.9 %shard_map.52 = f32[4,64,512]{2,1,0:T(8,128)} custom-call(f32[1,4,64,512]{3,2,1,0:T(8,128)S(1)} %shard_map.51.own_ref, f32[2,4,64,512]{3,2,1,0:T(8,128)S(1)} %collective-permute-done.5.other_ref, bf16[4,64,512]{2,1,0:T(8,128)(2,1)S(1)} %collective-permute-done.6.code_ref), custom_call_target="tpu_custom_call" | custom-call | tf_op jit(solution)/shard_map/pallas_call | solution.py:430
  (3 shorter events, 0.0 us)
Async XLA Ops:
  0.0 11.2 %copy-start = (bf16[16,256,512]{2,1,0:T(8,128)(2,1)S(1)}, bf16[16,256,512]{2,1,0:T(8,128)(2,1)}, u32[]{:S(2)}) copy-start(bf16[16,256,512]{2,1,0:T(8,128)(2,1)} %refs_3_.7) | copy-start | bytes 12582916
  0.0 11.2 %copy-start.2 = (f32[16]{0:T(128)S(1)}, f32[16]{0:T(128)}, u32[]{:S(2)}) copy-start(f32[16]{0:T(128)} %param.6) | copy-start | bytes 196
  0.0 11.2 %copy-start.1 = (f32[3,16]{1,0:T(4,128)S(1)}, f32[3,16]{1,0:T(4,128)}, u32[]{:S(2)}) copy-start(f32[3,16]{1,0:T(4,128)} %refs_1_.7) | copy-start | bytes 580
  1.9 9.2 %collective-permute-start = (bf16[256,512]{1,0:T(8,128)(2,1)S(1)}, bf16[256,512]{1,0:T(8,128)(2,1)S(1)}, u32[]{:S(2)}, u32[]{:S(2)}) collective-permute-start(bf16[256,512]{1,0:T(8,128)(2,1)S(1)} %get-tuple-element.14), channel_id=1, source_target_pairs={{0,8},{16,24},{8,0},{24,16},{1,9},{17,25},{9,1},{25,17},{2,10},{18... | collective-permute-start | bytes 786440 | tf_op jit(solution)/shard_map/ppermute | solution.py:67
  2.0 9.2 %collective-permute-start.1 = (bf16[256,512]{1,0:T(8,128)(2,1)S(1)}, bf16[256,512]{1,0:T(8,128)(2,1)S(1)}, u32[]{:S(2)}, u32[]{:S(2)}) collective-permute-start(bf16[256,512]{1,0:T(8,128)(2,1)S(1)} %get-tuple-element.15), channel_id=1, source_target_pairs={{8,16},{16,8},{9,17},{17,9},{10,18},{18,10},{11,19},{19,11},{12,20... | collective-permute-start | bytes 786440 | tf_op jit(solution)/shard_map/ppermute | solution.py:67
  4.5 6.6 %collective-permute-start.2 = (bf16[256,128]{1,0:T(8,128)(2,1)S(1)}, bf16[256,128]{1,0:T(8,128)(2,1)S(1)}, u32[]{:S(2)}, u32[]{:S(2)}) collective-permute-start(bf16[256,128]{1,0:T(8,128)(2,1)S(1)} %get-tuple-element.16), channel_id=1, source_target_pairs={{0,1},{1,0},{2,3},{3,2},{4,5},{5,4},{6,7},{7,6},{8,9},{9,8},{10,11... | collective-permute-start | bytes 196616 | tf_op jit(solution)/shard_map/ppermute | solution.py:67
  6.1 12.0 %collective-permute-start.3 = (bf16[16,512]{1,0:T(8,128)(2,1)S(1)}, bf16[16,512]{1,0:T(8,128)(2,1)S(1)}, u32[]{:S(2)}, u32[]{:S(2)}) collective-permute-start(bf16[16,512]{1,0:T(8,128)(2,1)S(1)} %get-tuple-element.17), channel_id=1, source_target_pairs={{0,2},{4,6},{2,0},{6,4},{1,3},{5,7},{3,1},{7,5},{8,10},{12,14},{10... | collective-permute-start | bytes 49160 | tf_op jit(solution)/shard_map/ppermute | solution.py:67
  6.5 11.5 %collective-permute-start.4 = (bf16[16,512]{1,0:T(8,128)(2,1)S(1)}, bf16[16,512]{1,0:T(8,128)(2,1)S(1)}, u32[]{:S(2)}, u32[]{:S(2)}) collective-permute-start(bf16[16,512]{1,0:T(8,128)(2,1)S(1)} %get-tuple-element.18), channel_id=1, source_target_pairs={{2,4},{4,2},{3,5},{5,3},{10,12},{12,10},{11,13},{13,11},{18,20},{2... | collective-permute-start | bytes 49160 | tf_op jit(solution)/shard_map/ppermute | solution.py:67
  20.6 4.9 %collective-permute-start.5 = (f32[2,4,64,512]{3,2,1,0:T(8,128)S(1)}, f32[2,4,64,512]{3,2,1,0:T(8,128)S(1)}, u32[]{:S(2)}, u32[]{:S(2)}) collective-permute-start(f32[2,4,64,512]{3,2,1,0:T(8,128)S(1)} %shard_map.48), channel_id=1, source_target_pairs={{0,8},{8,0},{16,24},{24,16},{1,9},{9,1},{17,25},{25,17},{2,10},{10... | collective-permute-start | bytes 3145736 | tf_op jit(solution)/shard_map/ppermute | solution.py:453
  25.7 8.8 %collective-permute-start.6 = (bf16[4,64,512]{2,1,0:T(8,128)(2,1)S(1)}, bf16[4,64,512]{2,1,0:T(8,128)(2,1)S(1)}, u32[]{:S(2)}, u32[]{:S(2)}) collective-permute-start(bf16[4,64,512]{2,1,0:T(8,128)(2,1)S(1)} %shard_map.50), channel_id=1, source_target_pairs={{0,16},{8,24},{16,0},{24,8},{1,17},{9,25},{17,1},{25,9},{2,18},{10... | collective-permute-start | bytes 786440 | tf_op jit(solution)/shard_map/ppermute | solution.py:453

commit v10 on v9

--- a/solution.py
+++ b/solution.py
@@ -390,23 +390,25 @@
     return colours + [first[3] * second[3]]
 
 
-def pair_kernel(own_ref, other_ref, code_ref):
+def pair_kernel(own_ref, other_ref, code_ref, *, first_row):
+    rows = pl.ds(first_row, own_ref.shape[2])
     own = [own_ref[0, c] for c in range(4)]
-    other = [other_ref[0, c] for c in range(4)]
+    other = [other_ref[0, c, rows] for c in range(4)]
     merged = ordered_over(own, other, lax.axis_index("view") & 1 == 1)
     for c in range(4):
         code_ref[c] = jnp.exp2(CODE_SCALE * merged[c] - CODE_SHIFT).astype(code_ref.dtype)
 
 
-def last_kernel(own_ref, other_ref, code_ref, out_ref, *, finish):
-    rows = pl.ds(pl.multiple_of(pl.program_id(0) * out_ref.shape[1], HALF), out_ref.shape[1])
+def last_kernel(own_ref, other_ref, *refs, finish):
+    code_refs, out_ref = refs[:-1], refs[-1]
+    step, size = pl.program_id(0), out_ref.shape[1]
+    rows = pl.ds(pl.multiple_of(step * size, PACK), size)
     own = [own_ref[0, c, rows] for c in range(4)]
     other = [other_ref[1, c, rows] for c in range(4)]
-    coded = pl.ds(pl.multiple_of(pl.program_id(0) * out_ref.shape[1], PACK), out_ref.shape[1])
-    far = [
-        (jnp.log2(code_ref[c, coded].astype(jnp.float32)) + CODE_SHIFT) * (1.0 / CODE_SCALE)
-        for c in range(4)
-    ]
+    codes = [code_refs[0][c] for c in range(4)]
+    for part, code_ref in enumerate(code_refs[1:], 1):
+        codes = [jnp.where(step >= part, code_ref[c], codes[c]) for c in range(4)]
+    far = [(jnp.log2(code.astype(jnp.float32)) + CODE_SHIFT) * (1.0 / CODE_SCALE) for code in codes]
     pair = ordered_over(own, other, lax.axis_index("view") & 1 == 1)
     merged = ordered_over(pair, far, lax.axis_index("view") & 2 == 2)
     for c in range(3):
@@ -414,9 +416,9 @@
     out_ref[3] = 1.0 - merged[3] if finish else merged[3]
 
 
-def merge_pair(own, other):
+def merge_pair(own, other, first_row):
     return pl.pallas_call(
-        pair_kernel,
+        functools.partial(pair_kernel, first_row=first_row),
         in_specs=[VECTORS, VECTORS],
         out_specs=VECTORS,
         out_shape=jax.ShapeDtypeStruct(own.shape[1:], jnp.bfloat16),
@@ -424,17 +426,17 @@
     )(own, other)
 
 
-def merge_last(own, other, code, finish):
+def merge_last(own, other, codes, finish):
     _, _, rows, width = own.shape
-    steps = 2 if rows % (2 * PACK) == 0 else 1
+    steps = len(codes)
     return pl.pallas_call(
         functools.partial(last_kernel, finish=finish),
         grid=(steps,),
-        in_specs=[VECTORS, VECTORS, VECTORS],
+        in_specs=[VECTORS] * (2 + steps),
         out_specs=pl.BlockSpec((4, rows // steps, width), lambda i: (0, i, 0)),
         out_shape=jax.ShapeDtypeStruct(own.shape[1:], jnp.float32),
         compiler_params=pltpu.CompilerParams(vmem_limit_bytes=24 * 2**20),
-    )(own, other, code)
+    )(own, other, *codes)
 
 
 def over(nearer, farther):
@@ -475,8 +477,8 @@
         distance = distances[0] + (distances[-1] - distances[0]) * group
         return ((at ^ distance) + block * groups) * steps + step - block * steps
 
-    def all_tiles(distance):
-        return lambda i: (i, tile_at(i, (distance,)))
+    def all_tiles(distance, first=0):
+        return lambda i: (i, tile_at(first + i, (distance,)))
 
     def missing_tile():
         at = lax.axis_index("view") & 3
@@ -511,7 +513,7 @@
             (depth, here, lines if with_lines else None),
             tiles,
             tile_count,
-            (out_groups, count * tile),
+            (out_groups, tile_count * tile if out_groups == 1 else count * tile),
             (tf_color, tf_opacity),
             slices * view_count,
             tile,
@@ -522,11 +524,15 @@
         far = march_call(inner_tiles, 2 * count - 1, 2, with_lines=False)
         far = march_call(edge_tile, 1, 2, partial=far)
         received = from_partner(far, "view", 0)
-        near = march_call(all_tiles(2), count, after=far)
-        code = merge_pair(near, received)
-        code_received = from_partner(code, "view", 1)
-        near = march_call(all_tiles(0), count, after=code)
-        image = merge_last(near, received, code_received, bits == 2)
+        parts = 2 if count % 2 == 0 and count * tile % (2 * PACK) == 0 else 1
+        size = count // parts
+        before, codes = far, []
+        for first in range(0, count, size):
+            near = march_call(all_tiles(2, first), size, after=before)
+            before = merge_pair(near, received, first * tile)
+            codes.append(from_partner(before, "view", 1))
+        near = march_call(all_tiles(0), count, after=[before] + codes[:-1])
+        image = merge_last(near, received, codes, bits == 2)
     elif groups == 2:
         far = march_call(all_tiles(1), count)
         received = from_partner(far, "view", 0)

time: 35.5 us -> 35.2 us (level)
  waiting for transfers between devices: 3.25 us -> 1.23 us
  starting transfers between devices: 10 us -> 11.4 us
    ppermute x2 -> x3, waiting for transfers between devices: 3.24 us -> 1.22 us  [from_partner(): return lax.ppermute(value, axis, pairs)]
    ppermute x2 -> x3, starting transfers between devices: 0.82 us -> 2.24 us  [from_partner(): return lax.ppermute(value, axis, pairs)]
    pallas_call x4 -> x5, Pallas kernels: 19 us -> 19.2 us  [march(): pl.pallas_call(functools.partial(march_kernel, tiles=tiles, count=count,...]
  transfers between devices with their start and end apart: 7 -> 8, of which waited for: 1 -> 2; matrix products, arithmetic and copies ran while one was open for 0% -> 0% of each run, Pallas kernels for 46% -> 48%
where the time goes in v10:
time: 35.2 us; the launch traced here: 35 us
  Pallas kernels  22.2 us (63%)
  starting transfers between devices  11.4 us (32%)
  waiting for transfers between devices  1.23 us (3%)
    pallas_call x5, Pallas kernels, march(): pl.pallas_call(functools.partial(march_kernel, tiles=tiles, count=count,...  19.2 us
    ppermute x5, starting transfers between devices, exchange(): lax.ppermute(face, axis, both)  9.18 us
    ppermute x3, starting transfers between devices, from_partner(): return lax.ppermute(value, axis, pairs)  2.24 us
    pallas_call x1, Pallas kernels, prepare(): pl.pallas_call(prepare_kernel, in_specs=[pl.BlockSpec(memory_space=pltpu....  1.89 us
    ppermute x3, waiting for transfers between devices, from_partner(): return lax.ppermute(value, axis, pairs)  1.22 us
    pallas_call x1, Pallas kernels, merge_last(): pl.pallas_call(functools.partial(last_kernel, finish=finish), grid=(steps...  0.96 us
  transfers between devices with their start and end apart: 8, of which 2 were waited for; matrix products, arithmetic and copies ran while one was open for 0% of the time, Pallas kernels for 48%

profile of v10, /device:TPU:12, one launch (start us, length us, event | category | flops | bytes accessed | tf_op | source)
XLA Modules:
  0.0 35.0 jit_solution(1830895893596098367)
XLA Ops:
  0.0 1.9 %shard_map.46 = (bf16[128,208]{1,0:T(8,128)(2,1)S(1)}, bf16[256,512]{1,0:T(8,128)(2,1)S(1)}, bf16[256,512]{1,0:T(8,128)(2,1)S(1)}, bf16[16,512]{1,0:T(8,128)(2,1...) custom-call(bf16[16,256,512]{2,1,0:T(8,128)(2,1)} %refs_3_.9, bf16[128,208]{1,0:T(8,128)(2,1)} %constant.2.clone.stencil_ref), custom_call_target="tpu_custom_call" | custom-call | tf_op jit(solution)/shard_map/pallas_call | solution.py:147
  1.9 0.1 collective-permute-start
  2.0 2.5 %collective-permute-start.1 = (bf16[256,512]{1,0:T(8,128)(2,1)S(1)}, bf16[256,512]{1,0:T(8,128)(2,1)S(1)}, u32[]{:S(2)}, u32[]{:S(2)}) collective-permute-start(bf16[256,512]{1,0:T(8,128)(2,1)S(1)} %get-tuple-element.16), channel_id=1, source_target_pairs={{8,16},{16,8},{9,17},{17,9},{10,18},{18,10},{11,19},{19,11},{12,20... | collective-permute-start | bytes 786440 | tf_op jit(solution)/shard_map/ppermute | solution.py:67
  4.5 1.6 %collective-permute-start.2 = (bf16[256,128]{1,0:T(8,128)(2,1)S(1)}, bf16[256,128]{1,0:T(8,128)(2,1)S(1)}, u32[]{:S(2)}, u32[]{:S(2)}) collective-permute-start(bf16[256,128]{1,0:T(8,128)(2,1)S(1)} %get-tuple-element.17), channel_id=1, source_target_pairs={{0,1},{1,0},{2,3},{3,2},{4,5},{5,4},{6,7},{7,6},{8,9},{9,8},{10,11... | collective-permute-start | bytes 196616 | tf_op jit(solution)/shard_map/ppermute | solution.py:67
  6.1 0.4 %collective-permute-start.3 = (bf16[16,512]{1,0:T(8,128)(2,1)S(1)}, bf16[16,512]{1,0:T(8,128)(2,1)S(1)}, u32[]{:S(2)}, u32[]{:S(2)}) collective-permute-start(bf16[16,512]{1,0:T(8,128)(2,1)S(1)} %get-tuple-element.18), channel_id=1, source_target_pairs={{0,2},{4,6},{2,0},{6,4},{1,3},{5,7},{3,1},{7,5},{8,10},{12,14},{10... | collective-permute-start | bytes 49160 | tf_op jit(solution)/shard_map/ppermute | solution.py:67
  6.5 4.6 %collective-permute-start.4 = (bf16[16,512]{1,0:T(8,128)(2,1)S(1)}, bf16[16,512]{1,0:T(8,128)(2,1)S(1)}, u32[]{:S(2)}, u32[]{:S(2)}) collective-permute-start(bf16[16,512]{1,0:T(8,128)(2,1)S(1)} %get-tuple-element.19), channel_id=1, source_target_pairs={{2,4},{4,2},{3,5},{5,3},{10,12},{12,10},{11,13},{13,11},{18,20},{2... | collective-permute-start | bytes 49160 | tf_op jit(solution)/shard_map/ppermute | solution.py:67
  11.1 0.0 collective-permute-done.2.refs_6_
  11.1 0.0 collective-permute-done.refs_4_
  11.1 0.0 collective-permute-done.1.refs_5_
  11.2 6.8 %shard_map.47.refs_9_ = f32[2,4,64,512]{3,2,1,0:T(8,128)S(1)} custom-call(bf16[128,208]{1,0:T(8,128)(2,1)S(1)} %get-tuple-element.14.refs_0_, f32[3,16]{1,0:T(4,128)S(1)} %copy-done.1, f32[1,16]{1,0:T(1,128)S(1)} %bitcast.4, bf16[16,256,512]{2,1,0:T(8,128)(2,1)S(1)} %copy-done, bf16[256,512]{1,0:T(8,128)(2,1)S(1)} %collective-permute-done.refs_4_, ...), custom_call_target="tpu_custom_call" | custom-call | tf_op jit(solution)/shard_map/pallas_call | solution.py:366
  18.0 0.0 collective-permute-done.3.refs_7_
  18.0 0.0 collective-permute-done.4.refs_8_
  18.0 2.6 %shard_map.48 = f32[2,4,64,512]{3,2,1,0:T(8,128)S(1)} custom-call(bf16[128,208]{1,0:T(8,128)(2,1)S(1)} %get-tuple-element.14.refs_0_, f32[3,16]{1,0:T(4,128)S(1)} %copy-done.1, f32[1,16]{1,0:T(1,128)S(1)} %bitcast.5, bf16[16,256,512]{2,1,0:T(8,128)(2,1)S(1)} %copy-done, ...), custom_call_target="tpu_custom_call", output_to_operand_aliasing={{}: (9, {})} | custom-call | tf_op jit(solution)/shard_map/pallas_call | solution.py:366
  20.6 0.1 collective-permute-start.5
  20.7 2.5 %shard_map.49.own_ref = f32[1,4,32,512]{3,2,1,0:T(8,128)S(1)} custom-call(bf16[128,208]{1,0:T(8,128)(2,1)S(1)} %get-tuple-element.14.refs_0_, f32[3,16]{1,0:T(4,128)S(1)} %copy-done.1, f32[1,16]{1,0:T(1,128)S(1)} %bitcast.6, bf16[16,256,512]{2,1,0:T(8,128)(2,1)S(1)} %copy-done, bf16[256,512]{1,0:T(8,128)(2,1)S(1)} %collective-permute-done.refs_4_, ...), custom_call_target="tpu_custom_call" | custom-call | tf_op jit(solution)/shard_map/pallas_call | solution.py:366
  23.2 0.1 collective-permute-done.5.other_ref
  23.3 0.1 shard_map.50
  23.4 0.6 %collective-permute-start.6 = (bf16[4,32,512]{2,1,0:T(8,128)(2,1)S(1)}, bf16[4,32,512]{2,1,0:T(8,128)(2,1)S(1)}, u32[]{:S(2)}, u32[]{:S(2)}) collective-permute-start(bf16[4,32,512]{2,1,0:T(8,128)(2,1)S(1)} %shard_map.50), channel_id=1, source_target_pairs={{0,16},{8,24},{16,0},{24,8},{1,17},{9,25},{17,1},{25,9},{2,18},{10... | collective-permute-start | bytes 393224 | tf_op jit(solution)/shard_map/ppermute | solution.py:455
  24.0 2.5 %shard_map.51.own_ref = f32[1,4,32,512]{3,2,1,0:T(8,128)S(1)} custom-call(bf16[128,208]{1,0:T(8,128)(2,1)S(1)} %get-tuple-element.14.refs_0_, f32[3,16]{1,0:T(4,128)S(1)} %copy-done.1, f32[1,16]{1,0:T(1,128)S(1)} %bitcast.7, bf16[16,256,512]{2,1,0:T(8,128)(2,1)S(1)} %copy-done, bf16[256,512]{1,0:T(8,128)(2,1)S(1)} %collective-permute-done.refs_4_, ...), custom_call_target="tpu_custom_call" | custom-call | tf_op jit(solution)/shard_map/pallas_call | solution.py:366
  26.5 0.1 shard_map.52
  26.6 1.5 %collective-permute-start.7 = (bf16[4,32,512]{2,1,0:T(8,128)(2,1)S(1)}, bf16[4,32,512]{2,1,0:T(8,128)(2,1)S(1)}, u32[]{:S(2)}, u32[]{:S(2)}) collective-permute-start(bf16[4,32,512]{2,1,0:T(8,128)(2,1)S(1)} %shard_map.52), channel_id=1, source_target_pairs={{0,16},{8,24},{16,0},{24,8},{1,17},{9,25},{17,1},{25,9},{2,18},{10... | collective-permute-start | bytes 393224 | tf_op jit(solution)/shard_map/ppermute | solution.py:455
  28.2 1.1 %collective-permute-done.6.refs_0_ = bf16[4,32,512]{2,1,0:T(8,128)(2,1)S(1)} collective-permute-done((bf16[4,32,512]{2,1,0:T(8,128)(2,1)S(1)}, bf16[4,32,512]{2,1,0:T(8,128)(2,1)S(1)}, u32[]{:S(2)}, u32[]{:S(2)}) %collective-permute-start.6) | collective-permute-done | bytes 131104 | tf_op jit(solution)/shard_map/ppermute | solution.py:455
  29.2 4.8 %shard_map.53.own_ref = f32[1,4,64,512]{3,2,1,0:T(8,128)S(1)} custom-call(bf16[128,208]{1,0:T(8,128)(2,1)S(1)} %get-tuple-element.14.refs_0_, f32[3,16]{1,0:T(4,128)S(1)} %copy-done.1, f32[1,16]{1,0:T(1,128)S(1)} %bitcast.8, bf16[16,256,512]{2,1,0:T(8,128)(2,1)S(1)} %copy-done, bf16[256,512]{1,0:T(8,128)(2,1)S(1)} %collective-permute-done.refs_4_, ...), custom_call_target="tpu_custom_call" | custom-call | tf_op jit(solution)/shard_map/pallas_call | solution.py:366
  34.1 1.0 %shard_map.54 = f32[4,64,512]{2,1,0:T(8,128)} custom-call(f32[1,4,64,512]{3,2,1,0:T(8,128)S(1)} %shard_map.53.own_ref, f32[2,4,64,512]{3,2,1,0:T(8,128)S(1)} %collective-permute-done.5.other_ref, bf16[4,32,512]{2,1,0:T(8,128)(2,1)S(1)} %collective-permute-done.6.refs_0_, bf16[4,32,512]{2,1,0:T(8,128)(2,1)S(1)} %collective-permute-done.7.refs_1_), custom_call_target="tpu_custom_call" | custom-call | tf_op jit(solution)/shard_map/pallas_call | solution.py:432
  (7 shorter events, 0.0 us)
Async XLA Ops:
  0.0 11.2 %copy-start = (bf16[16,256,512]{2,1,0:T(8,128)(2,1)S(1)}, bf16[16,256,512]{2,1,0:T(8,128)(2,1)}, u32[]{:S(2)}) copy-start(bf16[16,256,512]{2,1,0:T(8,128)(2,1)} %refs_3_.9) | copy-start | bytes 12582916
  0.0 11.2 %copy-start.2 = (f32[16]{0:T(128)S(1)}, f32[16]{0:T(128)}, u32[]{:S(2)}) copy-start(f32[16]{0:T(128)} %param.6) | copy-start | bytes 196
  0.0 11.2 %copy-start.1 = (f32[3,16]{1,0:T(4,128)S(1)}, f32[3,16]{1,0:T(4,128)}, u32[]{:S(2)}) copy-start(f32[3,16]{1,0:T(4,128)} %refs_1_.9) | copy-start | bytes 580
  1.9 9.2 %collective-permute-start = (bf16[256,512]{1,0:T(8,128)(2,1)S(1)}, bf16[256,512]{1,0:T(8,128)(2,1)S(1)}, u32[]{:S(2)}, u32[]{:S(2)}) collective-permute-start(bf16[256,512]{1,0:T(8,128)(2,1)S(1)} %get-tuple-element.15), channel_id=1, source_target_pairs={{0,8},{16,24},{8,0},{24,16},{1,9},{17,25},{9,1},{25,17},{2,10},{18... | collective-permute-start | bytes 786440 | tf_op jit(solution)/shard_map/ppermute | solution.py:67
  2.0 9.2 %collective-permute-start.1 = (bf16[256,512]{1,0:T(8,128)(2,1)S(1)}, bf16[256,512]{1,0:T(8,128)(2,1)S(1)}, u32[]{:S(2)}, u32[]{:S(2)}) collective-permute-start(bf16[256,512]{1,0:T(8,128)(2,1)S(1)} %get-tuple-element.16), channel_id=1, source_target_pairs={{8,16},{16,8},{9,17},{17,9},{10,18},{18,10},{11,19},{19,11},{12,20... | collective-permute-start | bytes 786440 | tf_op jit(solution)/shard_map/ppermute | solution.py:67
  4.5 6.6 %collective-permute-start.2 = (bf16[256,128]{1,0:T(8,128)(2,1)S(1)}, bf16[256,128]{1,0:T(8,128)(2,1)S(1)}, u32[]{:S(2)}, u32[]{:S(2)}) collective-permute-start(bf16[256,128]{1,0:T(8,128)(2,1)S(1)} %get-tuple-element.17), channel_id=1, source_target_pairs={{0,1},{1,0},{2,3},{3,2},{4,5},{5,4},{6,7},{7,6},{8,9},{9,8},{10,11... | collective-permute-start | bytes 196616 | tf_op jit(solution)/shard_map/ppermute | solution.py:67
  6.1 12.0 %collective-permute-start.3 = (bf16[16,512]{1,0:T(8,128)(2,1)S(1)}, bf16[16,512]{1,0:T(8,128)(2,1)S(1)}, u32[]{:S(2)}, u32[]{:S(2)}) collective-permute-start(bf16[16,512]{1,0:T(8,128)(2,1)S(1)} %get-tuple-element.18), channel_id=1, source_target_pairs={{0,2},{4,6},{2,0},{6,4},{1,3},{5,7},{3,1},{7,5},{8,10},{12,14},{10... | collective-permute-start | bytes 49160 | tf_op jit(solution)/shard_map/ppermute | solution.py:67
  6.5 11.5 %collective-permute-start.4 = (bf16[16,512]{1,0:T(8,128)(2,1)S(1)}, bf16[16,512]{1,0:T(8,128)(2,1)S(1)}, u32[]{:S(2)}, u32[]{:S(2)}) collective-permute-start(bf16[16,512]{1,0:T(8,128)(2,1)S(1)} %get-tuple-element.19), channel_id=1, source_target_pairs={{2,4},{4,2},{3,5},{5,3},{10,12},{12,10},{11,13},{13,11},{18,20},{2... | collective-permute-start | bytes 49160 | tf_op jit(solution)/shard_map/ppermute | solution.py:67
  20.6 2.7 %collective-permute-start.5 = (f32[2,4,64,512]{3,2,1,0:T(8,128)S(1)}, f32[2,4,64,512]{3,2,1,0:T(8,128)S(1)}, u32[]{:S(2)}, u32[]{:S(2)}) collective-permute-start(f32[2,4,64,512]{3,2,1,0:T(8,128)S(1)} %shard_map.48), channel_id=1, source_target_pairs={{0,8},{8,0},{16,24},{24,16},{1,9},{9,1},{17,25},{25,17},{2,10},{10... | collective-permute-start | bytes 3145736 | tf_op jit(solution)/shard_map/ppermute | solution.py:455
  23.4 5.8 %collective-permute-start.6 = (bf16[4,32,512]{2,1,0:T(8,128)(2,1)S(1)}, bf16[4,32,512]{2,1,0:T(8,128)(2,1)S(1)}, u32[]{:S(2)}, u32[]{:S(2)}) collective-permute-start(bf16[4,32,512]{2,1,0:T(8,128)(2,1)S(1)} %shard_map.50), channel_id=1, source_target_pairs={{0,16},{8,24},{16,0},{24,8},{1,17},{9,25},{17,1},{25,9},{2,18},{10... | collective-permute-start | bytes 393224 | tf_op jit(solution)/shard_map/ppermute | solution.py:455
  26.6 7.4 %collective-permute-start.7 = (bf16[4,32,512]{2,1,0:T(8,128)(2,1)S(1)}, bf16[4,32,512]{2,1,0:T(8,128)(2,1)S(1)}, u32[]{:S(2)}, u32[]{:S(2)}) collective-permute-start(bf16[4,32,512]{2,1,0:T(8,128)(2,1)S(1)} %shard_map.52), channel_id=1, source_target_pairs={{0,16},{8,24},{16,0},{24,8},{1,17},{9,25},{17,1},{25,9},{2,18},{10... | collective-permute-start | bytes 393224 | tf_op jit(solution)/shard_map/ppermute | solution.py:455

commit v11 on v10

--- a/solution.py
+++ b/solution.py
@@ -336,7 +336,7 @@
         pass
 
 
-def march(cells, matrix, halos, tiles, count, image, transfer, depth_total, tile, partial=None):
+def march(cells, matrix, halos, tiles, count, image, transfer, depth_total, tile, partial=None, short=False):
     slices, height, width = cells.shape
     depth, ends, lines = halos
     assert slices % SLOTS == 0 and SLOTS == 2 * DEPTH
@@ -378,6 +378,7 @@
         out_shape=jax.ShapeDtypeStruct((groups, 4, rows, width), jnp.float32),
         input_output_aliases={len(operands) - 1: 0} if patch else {},
         scratch_shapes=scratch,
+        cost_estimate=pl.CostEstimate(flops=1, transcendentals=0, bytes_accessed=1) if short else None,
         compiler_params=pltpu.CompilerParams(vmem_limit_bytes=24 * 2**20),
     )(*operands)
 
@@ -399,15 +400,16 @@
         code_ref[c] = jnp.exp2(CODE_SCALE * merged[c] - CODE_SHIFT).astype(code_ref.dtype)
 
 
-def last_kernel(own_ref, other_ref, *refs, finish):
-    code_refs, out_ref = refs[:-1], refs[-1]
+def last_kernel(*refs, parts, finish):
+    own_refs, other_ref, code_refs, out_ref = refs[:parts], refs[parts], refs[parts + 1 : -1], refs[-1]
     step, size = pl.program_id(0), out_ref.shape[1]
     rows = pl.ds(pl.multiple_of(step * size, PACK), size)
-    own = [own_ref[0, c, rows] for c in range(4)]
+    own = [own_refs[0][0, c] for c in range(4)]
     other = [other_ref[1, c, rows] for c in range(4)]
     codes = [code_refs[0][c] for c in range(4)]
-    for part, code_ref in enumerate(code_refs[1:], 1):
-        codes = [jnp.where(step >= part, code_ref[c], codes[c]) for c in range(4)]
+    for part in range(1, parts):
+        own = [jnp.where(step >= part, own_refs[part][0, c], own[c]) for c in range(4)]
+        codes = [jnp.where(step >= part, code_refs[part][c], codes[c]) for c in range(4)]
     far = [(jnp.log2(code.astype(jnp.float32)) + CODE_SHIFT) * (1.0 / CODE_SCALE) for code in codes]
     pair = ordered_over(own, other, lax.axis_index("view") & 1 == 1)
     merged = ordered_over(pair, far, lax.axis_index("view") & 2 == 2)
@@ -427,16 +429,16 @@
 
 
 def merge_last(own, other, codes, finish):
-    _, _, rows, width = own.shape
-    steps = len(codes)
+    parts = len(codes)
+    _, _, rows, width = own[0].shape
     return pl.pallas_call(
-        functools.partial(last_kernel, finish=finish),
-        grid=(steps,),
-        in_specs=[VECTORS] * (2 + steps),
-        out_specs=pl.BlockSpec((4, rows // steps, width), lambda i: (0, i, 0)),
-        out_shape=jax.ShapeDtypeStruct(own.shape[1:], jnp.float32),
+        functools.partial(last_kernel, parts=parts, finish=finish),
+        grid=(parts,),
+        in_specs=[VECTORS] * (2 * parts + 1),
+        out_specs=pl.BlockSpec((4, rows, width), lambda i: (0, i, 0)),
+        out_shape=jax.ShapeDtypeStruct((4, parts * rows, width), jnp.float32),
         compiler_params=pltpu.CompilerParams(vmem_limit_bytes=24 * 2**20),
-    )(own, other, *codes)
+    )(*own, other, *codes)
 
 
 def over(nearer, farther):
@@ -503,7 +505,9 @@
     )
     ends = sum(ends[1:], ends[0])
 
-    def march_call(tiles, tile_count, out_groups=1, after=None, partial=None, with_lines=True):
+    def march_call(
+        tiles, tile_count, out_groups=1, after=None, partial=None, with_lines=True, short=False
+    ):
         here = ends
         if after is not None:
             here, _ = lax.optimization_barrier((ends, after))
@@ -518,6 +522,7 @@
             slices * view_count,
             tile,
             partial,
+            short,
         )
 
     if groups == 4:
@@ -531,8 +536,11 @@
             near = march_call(all_tiles(2, first), size, after=before)
             before = merge_pair(near, received, first * tile)
             codes.append(from_partner(before, "view", 1))
-        near = march_call(all_tiles(0), count, after=[before] + codes[:-1])
-        image = merge_last(near, received, codes, bits == 2)
+        nears = [march_call(all_tiles(0), size, after=before)]
+        for first in range(size, count, size):
+            after = [nears[-1]] + codes[:-1]
+            nears.append(march_call(all_tiles(0, first), size, after=after, short=True))
+        image = merge_last(nears, received, codes, bits == 2)
     elif groups == 2:
         far = march_call(all_tiles(1), count)
         received = from_partner(far, "view", 0)

time: 35.2 us -> 34.6 us (0.983)
  waiting for transfers between devices: 1.23 us -> 0.16 us
  Pallas kernels: 22.2 us -> 22.6 us
    ppermute x3, waiting for transfers between devices: 1.22 us -> 0.15 us  [from_partner(): return lax.ppermute(value, axis, pairs)]
    pallas_call x5 -> x6, Pallas kernels: 19.2 us -> 19.6 us  [march(): pl.pallas_call(functools.partial(march_kernel, tiles=tiles, count=count,...]
  transfers between devices with their start and end apart: 8 -> 8, of which waited for: 2 -> 1; matrix products, arithmetic and copies ran while one was open for 0% -> 0% of each run, Pallas kernels for 48% -> 49%
where the time goes in v11:
time: 34.6 us; the launch traced here: 34.4 us
  Pallas kernels  22.6 us (65%)
  starting transfers between devices  11.4 us (33%)
    pallas_call x6, Pallas kernels, march(): pl.pallas_call(functools.partial(march_kernel, tiles=tiles, count=count,...  19.6 us
    ppermute x5, starting transfers between devices, exchange(): lax.ppermute(face, axis, both)  9.18 us
    ppermute x3, starting transfers between devices, from_partner(): return lax.ppermute(value, axis, pairs)  2.24 us
    pallas_call x1, Pallas kernels, prepare(): pl.pallas_call(prepare_kernel, in_specs=[pl.BlockSpec(memory_space=pltpu....  1.89 us
    pallas_call x1, Pallas kernels, merge_last(): pl.pallas_call(functools.partial(last_kernel, parts=parts, finish=finish)...  0.99 us
  transfers between devices with their start and end apart: 8, of which 1 were waited for; matrix products, arithmetic and copies ran while one was open for 0% of the time, Pallas kernels for 49%

profile of v11, /device:TPU:12, one launch (start us, length us, event | category | flops | bytes accessed | tf_op | source)
XLA Modules:
  0.0 34.4 jit_solution(13164421217177036006)
XLA Ops:
  0.0 1.9 %shard_map.46 = (bf16[128,208]{1,0:T(8,128)(2,1)S(1)}, bf16[256,512]{1,0:T(8,128)(2,1)S(1)}, bf16[256,512]{1,0:T(8,128)(2,1)S(1)}, bf16[16,512]{1,0:T(8,128)(2,1...) custom-call(bf16[16,256,512]{2,1,0:T(8,128)(2,1)} %refs_3_.11, bf16[128,208]{1,0:T(8,128)(2,1)} %constant.2.clone.stencil_ref), custom_call_target="tpu_custom_call" | custom-call | tf_op jit(solution)/shard_map/pallas_call | solution.py:147
  1.9 0.1 collective-permute-start
  2.0 2.5 %collective-permute-start.1 = (bf16[256,512]{1,0:T(8,128)(2,1)S(1)}, bf16[256,512]{1,0:T(8,128)(2,1)S(1)}, u32[]{:S(2)}, u32[]{:S(2)}) collective-permute-start(bf16[256,512]{1,0:T(8,128)(2,1)S(1)} %get-tuple-element.17), channel_id=1, source_target_pairs={{8,16},{16,8},{9,17},{17,9},{10,18},{18,10},{11,19},{19,11},{12,20... | collective-permute-start | bytes 786440 | tf_op jit(solution)/shard_map/ppermute | solution.py:67
  4.5 1.6 %collective-permute-start.2 = (bf16[256,128]{1,0:T(8,128)(2,1)S(1)}, bf16[256,128]{1,0:T(8,128)(2,1)S(1)}, u32[]{:S(2)}, u32[]{:S(2)}) collective-permute-start(bf16[256,128]{1,0:T(8,128)(2,1)S(1)} %get-tuple-element.18), channel_id=1, source_target_pairs={{0,1},{1,0},{2,3},{3,2},{4,5},{5,4},{6,7},{7,6},{8,9},{9,8},{10,11... | collective-permute-start | bytes 196616 | tf_op jit(solution)/shard_map/ppermute | solution.py:67
  6.1 0.4 %collective-permute-start.3 = (bf16[16,512]{1,0:T(8,128)(2,1)S(1)}, bf16[16,512]{1,0:T(8,128)(2,1)S(1)}, u32[]{:S(2)}, u32[]{:S(2)}) collective-permute-start(bf16[16,512]{1,0:T(8,128)(2,1)S(1)} %get-tuple-element.19), channel_id=1, source_target_pairs={{0,2},{4,6},{2,0},{6,4},{1,3},{5,7},{3,1},{7,5},{8,10},{12,14},{10... | collective-permute-start | bytes 49160 | tf_op jit(solution)/shard_map/ppermute | solution.py:67
  6.5 4.6 %collective-permute-start.4 = (bf16[16,512]{1,0:T(8,128)(2,1)S(1)}, bf16[16,512]{1,0:T(8,128)(2,1)S(1)}, u32[]{:S(2)}, u32[]{:S(2)}) collective-permute-start(bf16[16,512]{1,0:T(8,128)(2,1)S(1)} %get-tuple-element.20), channel_id=1, source_target_pairs={{2,4},{4,2},{3,5},{5,3},{10,12},{12,10},{11,13},{13,11},{18,20},{2... | collective-permute-start | bytes 49160 | tf_op jit(solution)/shard_map/ppermute | solution.py:67
  11.1 0.0 collective-permute-done.2.refs_6_
  11.1 0.0 collective-permute-done.refs_4_
  11.2 6.8 %shard_map.47.refs_9_ = f32[2,4,64,512]{3,2,1,0:T(8,128)S(1)} custom-call(bf16[128,208]{1,0:T(8,128)(2,1)S(1)} %get-tuple-element.15.refs_0_, f32[3,16]{1,0:T(4,128)S(1)} %copy-done.1, f32[1,16]{1,0:T(1,128)S(1)} %bitcast.4, bf16[16,256,512]{2,1,0:T(8,128)(2,1)S(1)} %copy-done, bf16[256,512]{1,0:T(8,128)(2,1)S(1)} %collective-permute-done.refs_4_, ...), custom_call_target="tpu_custom_call" | custom-call | tf_op jit(solution)/shard_map/pallas_call | solution.py:366
  18.0 0.0 collective-permute-done.4.refs_8_
  18.0 2.7 %shard_map.48 = f32[2,4,64,512]{3,2,1,0:T(8,128)S(1)} custom-call(bf16[128,208]{1,0:T(8,128)(2,1)S(1)} %get-tuple-element.15.refs_0_, f32[3,16]{1,0:T(4,128)S(1)} %copy-done.1, f32[1,16]{1,0:T(1,128)S(1)} %bitcast.5, bf16[16,256,512]{2,1,0:T(8,128)(2,1)S(1)} %copy-done, ...), custom_call_target="tpu_custom_call", output_to_operand_aliasing={{}: (9, {})} | custom-call | tf_op jit(solution)/shard_map/pallas_call | solution.py:366
  20.8 0.1 collective-permute-start.5
  20.8 2.5 %shard_map.49.own_ref = f32[1,4,32,512]{3,2,1,0:T(8,128)S(1)} custom-call(bf16[128,208]{1,0:T(8,128)(2,1)S(1)} %get-tuple-element.15.refs_0_, f32[3,16]{1,0:T(4,128)S(1)} %copy-done.1, f32[1,16]{1,0:T(1,128)S(1)} %bitcast.6, bf16[16,256,512]{2,1,0:T(8,128)(2,1)S(1)} %copy-done, bf16[256,512]{1,0:T(8,128)(2,1)S(1)} %collective-permute-done.refs_4_, ...), custom_call_target="tpu_custom_call" | custom-call | tf_op jit(solution)/shard_map/pallas_call | solution.py:366
  23.4 0.1 collective-permute-done.5.other_ref.refs_2_
  23.5 0.1 shard_map.50
  23.6 0.6 %collective-permute-start.6 = (bf16[4,32,512]{2,1,0:T(8,128)(2,1)S(1)}, bf16[4,32,512]{2,1,0:T(8,128)(2,1)S(1)}, u32[]{:S(2)}, u32[]{:S(2)}) collective-permute-start(bf16[4,32,512]{2,1,0:T(8,128)(2,1)S(1)} %shard_map.50), channel_id=1, source_target_pairs={{0,16},{8,24},{16,0},{24,8},{1,17},{9,25},{17,1},{25,9},{2,18},{10... | collective-permute-start | bytes 393224 | tf_op jit(solution)/shard_map/ppermute | solution.py:457
  24.2 2.5 %shard_map.51.own_ref = f32[1,4,32,512]{3,2,1,0:T(8,128)S(1)} custom-call(bf16[128,208]{1,0:T(8,128)(2,1)S(1)} %get-tuple-element.15.refs_0_, f32[3,16]{1,0:T(4,128)S(1)} %copy-done.1, f32[1,16]{1,0:T(1,128)S(1)} %bitcast.7, bf16[16,256,512]{2,1,0:T(8,128)(2,1)S(1)} %copy-done, bf16[256,512]{1,0:T(8,128)(2,1)S(1)} %collective-permute-done.refs_4_, ...), custom_call_target="tpu_custom_call" | custom-call | tf_op jit(solution)/shard_map/pallas_call | solution.py:366
  26.7 0.1 shard_map.52
  26.8 1.5 %collective-permute-start.7 = (bf16[4,32,512]{2,1,0:T(8,128)(2,1)S(1)}, bf16[4,32,512]{2,1,0:T(8,128)(2,1)S(1)}, u32[]{:S(2)}, u32[]{:S(2)}) collective-permute-start(bf16[4,32,512]{2,1,0:T(8,128)(2,1)S(1)} %shard_map.52), channel_id=1, source_target_pairs={{0,16},{8,24},{16,0},{24,8},{1,17},{9,25},{17,1},{25,9},{2,18},{10... | collective-permute-start | bytes 393224 | tf_op jit(solution)/shard_map/ppermute | solution.py:457
  28.3 2.5 %shard_map.53.refs_0_ = f32[1,4,32,512]{3,2,1,0:T(8,128)S(1)} custom-call(bf16[128,208]{1,0:T(8,128)(2,1)S(1)} %get-tuple-element.15.refs_0_, f32[3,16]{1,0:T(4,128)S(1)} %copy-done.1, f32[1,16]{1,0:T(1,128)S(1)} %bitcast.8, bf16[16,256,512]{2,1,0:T(8,128)(2,1)S(1)} %copy-done, bf16[256,512]{1,0:T(8,128)(2,1)S(1)} %collective-permute-done.refs_4_, ...), custom_call_target="tpu_custom_call" | custom-call | tf_op jit(solution)/shard_map/pallas_call | solution.py:366
  30.8 0.0 collective-permute-done.6.refs_3_
  30.8 2.5 %shard_map.54.refs_1_ = f32[1,4,32,512]{3,2,1,0:T(8,128)S(1)} custom-call(bf16[128,208]{1,0:T(8,128)(2,1)S(1)} %get-tuple-element.15.refs_0_, f32[3,16]{1,0:T(4,128)S(1)} %copy-done.1, f32[1,16]{1,0:T(1,128)S(1)} %bitcast.9, bf16[16,256,512]{2,1,0:T(8,128)(2,1)S(1)} %copy-done, bf16[256,512]{1,0:T(8,128)(2,1)S(1)} %collective-permute-done.refs_4_, ...), custom_call_target="tpu_custom_call" | custom-call | flops 1 | bytes 1 | tf_op jit(solution)/shard_map/pallas_call | solution.py:366
  33.4 0.0 collective-permute-done.7.refs_4_
  33.4 1.0 %shard_map.55 = f32[4,64,512]{2,1,0:T(8,128)} custom-call(f32[1,4,32,512]{3,2,1,0:T(8,128)S(1)} %shard_map.53.refs_0_, f32[1,4,32,512]{3,2,1,0:T(8,128)S(1)} %shard_map.54.refs_1_, f32[2,4,64,512]{3,2,1,0:T(8,128)S(1)} %collective-permute-done.5.other_ref.refs_2_, bf16[4,32,512]{2,1,0:T(8,128)(2,1)S(1)} %collective-permute-done.6.refs_3_, ...), custom_call_target="tpu_custom_call" | custom-call | tf_op jit(solution)/shard_map/pallas_call | solution.py:434
  (8 shorter events, 0.0 us)
Async XLA Ops:
  0.0 11.2 %copy-start = (bf16[16,256,512]{2,1,0:T(8,128)(2,1)S(1)}, bf16[16,256,512]{2,1,0:T(8,128)(2,1)}, u32[]{:S(2)}) copy-start(bf16[16,256,512]{2,1,0:T(8,128)(2,1)} %refs_3_.11) | copy-start | bytes 12582916
  0.0 11.2 %copy-start.2 = (f32[16]{0:T(128)S(1)}, f32[16]{0:T(128)}, u32[]{:S(2)}) copy-start(f32[16]{0:T(128)} %param.6) | copy-start | bytes 196
  0.0 11.2 %copy-start.1 = (f32[3,16]{1,0:T(4,128)S(1)}, f32[3,16]{1,0:T(4,128)}, u32[]{:S(2)}) copy-start(f32[3,16]{1,0:T(4,128)} %refs_1_.11) | copy-start | bytes 580
  1.9 9.2 %collective-permute-start = (bf16[256,512]{1,0:T(8,128)(2,1)S(1)}, bf16[256,512]{1,0:T(8,128)(2,1)S(1)}, u32[]{:S(2)}, u32[]{:S(2)}) collective-permute-start(bf16[256,512]{1,0:T(8,128)(2,1)S(1)} %get-tuple-element.16), channel_id=1, source_target_pairs={{0,8},{16,24},{8,0},{24,16},{1,9},{17,25},{9,1},{25,17},{2,10},{18... | collective-permute-start | bytes 786440 | tf_op jit(solution)/shard_map/ppermute | solution.py:67
  2.0 9.2 %collective-permute-start.1 = (bf16[256,512]{1,0:T(8,128)(2,1)S(1)}, bf16[256,512]{1,0:T(8,128)(2,1)S(1)}, u32[]{:S(2)}, u32[]{:S(2)}) collective-permute-start(bf16[256,512]{1,0:T(8,128)(2,1)S(1)} %get-tuple-element.17), channel_id=1, source_target_pairs={{8,16},{16,8},{9,17},{17,9},{10,18},{18,10},{11,19},{19,11},{12,20... | collective-permute-start | bytes 786440 | tf_op jit(solution)/shard_map/ppermute | solution.py:67
  4.5 6.6 %collective-permute-start.2 = (bf16[256,128]{1,0:T(8,128)(2,1)S(1)}, bf16[256,128]{1,0:T(8,128)(2,1)S(1)}, u32[]{:S(2)}, u32[]{:S(2)}) collective-permute-start(bf16[256,128]{1,0:T(8,128)(2,1)S(1)} %get-tuple-element.18), channel_id=1, source_target_pairs={{0,1},{1,0},{2,3},{3,2},{4,5},{5,4},{6,7},{7,6},{8,9},{9,8},{10,11... | collective-permute-start | bytes 196616 | tf_op jit(solution)/shard_map/ppermute | solution.py:67
  6.1 11.9 %collective-permute-start.3 = (bf16[16,512]{1,0:T(8,128)(2,1)S(1)}, bf16[16,512]{1,0:T(8,128)(2,1)S(1)}, u32[]{:S(2)}, u32[]{:S(2)}) collective-permute-start(bf16[16,512]{1,0:T(8,128)(2,1)S(1)} %get-tuple-element.19), channel_id=1, source_target_pairs={{0,2},{4,6},{2,0},{6,4},{1,3},{5,7},{3,1},{7,5},{8,10},{12,14},{10... | collective-permute-start | bytes 49160 | tf_op jit(solution)/shard_map/ppermute | solution.py:67
  6.5 11.5 %collective-permute-start.4 = (bf16[16,512]{1,0:T(8,128)(2,1)S(1)}, bf16[16,512]{1,0:T(8,128)(2,1)S(1)}, u32[]{:S(2)}, u32[]{:S(2)}) collective-permute-start(bf16[16,512]{1,0:T(8,128)(2,1)S(1)} %get-tuple-element.20), channel_id=1, source_target_pairs={{2,4},{4,2},{3,5},{5,3},{10,12},{12,10},{11,13},{13,11},{18,20},{2... | collective-permute-start | bytes 49160 | tf_op jit(solution)/shard_map/ppermute | solution.py:67
  20.8 2.7 %collective-permute-start.5 = (f32[2,4,64,512]{3,2,1,0:T(8,128)S(1)}, f32[2,4,64,512]{3,2,1,0:T(8,128)S(1)}, u32[]{:S(2)}, u32[]{:S(2)}) collective-permute-start(f32[2,4,64,512]{3,2,1,0:T(8,128)S(1)} %shard_map.48), channel_id=1, source_target_pairs={{0,8},{8,0},{16,24},{24,16},{1,9},{9,1},{17,25},{25,17},{2,10},{10... | collective-permute-start | bytes 3145736 | tf_op jit(solution)/shard_map/ppermute | solution.py:457
  23.6 7.3 %collective-permute-start.6 = (bf16[4,32,512]{2,1,0:T(8,128)(2,1)S(1)}, bf16[4,32,512]{2,1,0:T(8,128)(2,1)S(1)}, u32[]{:S(2)}, u32[]{:S(2)}) collective-permute-start(bf16[4,32,512]{2,1,0:T(8,128)(2,1)S(1)} %shard_map.50), channel_id=1, source_target_pairs={{0,16},{8,24},{16,0},{24,8},{1,17},{9,25},{17,1},{25,9},{2,18},{10... | collective-permute-start | bytes 393224 | tf_op jit(solution)/shard_map/ppermute | solution.py:457
  26.8 6.6 %collective-permute-start.7 = (bf16[4,32,512]{2,1,0:T(8,128)(2,1)S(1)}, bf16[4,32,512]{2,1,0:T(8,128)(2,1)S(1)}, u32[]{:S(2)}, u32[]{:S(2)}) collective-permute-start(bf16[4,32,512]{2,1,0:T(8,128)(2,1)S(1)} %shard_map.52), channel_id=1, source_target_pairs={{0,16},{8,24},{16,0},{24,8},{1,17},{9,25},{17,1},{25,9},{2,18},{10... | collective-permute-start | bytes 393224 | tf_op jit(solution)/shard_map/ppermute | solution.py:457
